TPU v7x, 256 devices: a whole 4x4x8 slice. The times are simulated.
256 devices in a mesh: segment: 4 (over z_hi), mp: 16 (over y, x), dp: 4 (over z_lo, core).
Axes of the slice: x: 4, y: 4, z: 8 (z_hi: 4, z_lo: 2; z = z_hi * 2 + z_lo), core: 2. Of those that a mesh axis runs over, the one named last changes fastest.
Arguments:
- frames: bfloat16 [128, 128, 1536], P(('segment', 'dp'), 'mp'), may hold values from -6 to 6
- latent_init: bfloat16 [64, 1536], replicated, may hold values from -6 to 6
- norm_gains: bfloat16 [3, 1536], replicated, may hold values from 0.099609375 to 1.8984375
- res_query: bfloat16 [1536, 1536], P(None, 'mp'), may hold values from -0.15625 to 0.15625
- res_kv: bfloat16 [1536, 2, 1536], P(None, None, 'mp'), may hold values from -0.15625 to 0.15625
- res_out: bfloat16 [1536, 1536], replicated, may hold values from -0.15625 to 0.15625
- text: bfloat16 [4, 4, 768, 8192], P('segment', 'dp', None, 'mp'), may hold values from -6 to 6
- text_gain: bfloat16 [4, 8192], P('segment'), may hold values from 0.099609375 to 1.8984375
- w_query: bfloat16 [4, 8192, 8192], P('segment', 'dp', 'mp'), may hold values from -0.0625 to 0.0625
- w_kv: bfloat16 [4, 1536, 2, 8192], P('segment', 'dp', None, 'mp'), may hold values from -0.15625 to 0.15625
- xgate: float32 [4], P('segment'), may hold values from 0.3 to 1.2
- frame_counts: int32 [4, 4], P('segment', 'dp'), may hold values from 1 to 8
- frame_dest: int32 [128], replicated, may hold values from 0 to 127, each once
- cotangent: bfloat16 [4, 4, 768, 8192], P('segment', 'dp', None, 'mp'), may hold values from -6 to 6
Outputs:
- context: bfloat16 [4, 4, 768, 8192], P('segment', 'dp', None, 'mp')
- latent_grad: float32 [64, 128, 1536], P('mp', ('segment', 'dp'))
Inputs may be any that keep to these rules, and one draw needn't show every extreme that they name: frame_dest is a permutation of the slots; a slot is used by its destination sequence only if its frame number is below that sequence's frame count.
All inputs are finite; a program needn't handle non-finite values.
Results may differ from a plain program's by a relative error of at most 0.04.
Values may be sent and summed in bfloat16 or wider, within the bound.
No kernel may reach another device: no remote copies, remote signals or barrier semaphores. Data moves between devices by JAX's collectives and lax.ppermute only.
A program may use at most 128 MiB of HBM per device.

v0:
```python
import math

import jax
import jax.numpy as jnp
from jax import lax
from jax.sharding import PartitionSpec as P

HD = 128
E = 1536
RESAMPLE_HEAD_DIM = 96
LAT = 64
FMAX = 8


def layer_norm(inputs, gain_row):
    values = inputs.astype(jnp.float32)
    center = values - jnp.mean(values, axis=-1, keepdims=True)
    spread = jnp.mean(center * center, axis=-1, keepdims=True)
    return center * lax.rsqrt(spread + 1e-05) * gain_row.astype(jnp.float32)


def attend(query_matrix, key_value_block, live, gate):
    score_matrix = jnp.einsum(
        "rag,lag->arl", query_matrix, key_value_block[:, 0], preferred_element_type=jnp.float32
    ) / math.sqrt(query_matrix.shape[-1])
    score_matrix = jnp.where(live[None, None, :], score_matrix, -1e30)
    row_max = lax.stop_gradient(jnp.max(score_matrix, axis=-1, keepdims=True))
    unnormalized_weights = jnp.exp(score_matrix - row_max)
    row_sum = jnp.sum(unnormalized_weights, axis=-1)
    blended_values = jnp.einsum(
        "lfv,vla->fla",
        unnormalized_weights.astype(jnp.bfloat16),
        key_value_block[:, 1],
        preferred_element_type=jnp.float32,
    )
    blended_values = blended_values / jnp.transpose(row_sum)[:, :, None]
    return gate * blended_values.reshape(blended_values.shape[0], -1)


def per_device(
    frames,
    latent_init,
    norm_gains,
    res_query,
    res_kv,
    res_out,
    text,
    text_gain,
    w_query,
    w_kv,
    xgate,
    frame_counts,
    frame_dest,
    cotangent,
):
    mp_count = lax.axis_size("mp")
    share = LAT // mp_count
    slots = frame_dest.shape[0]
    owned = frames.shape[0]
    res_cols = res_query.shape[1]
    res_local = res_cols // RESAMPLE_HEAD_DIM
    res_scale = 1.0 / math.sqrt(RESAMPLE_HEAD_DIM)
    lat_norm = layer_norm(latent_init, norm_gains[1]).astype(jnp.bfloat16)
    resampler_heads = (
        jnp.dot(lat_norm, res_query, preferred_element_type=jnp.float32)
        .astype(jnp.bfloat16)
        .reshape(LAT, res_local, RESAMPLE_HEAD_DIM)
    )
    latent_pair_rows = (
        jnp.einsum("le,ekc->lkc", lat_norm, res_kv, preferred_element_type=jnp.float32)
        .astype(jnp.bfloat16)
        .reshape(LAT, 2, res_local, RESAMPLE_HEAD_DIM)
    )
    first_scores = (
        jnp.einsum(
            "epg,apg->pea",
            resampler_heads,
            latent_pair_rows[:, 0],
            preferred_element_type=jnp.float32,
        )
        * res_scale
    )
    first_max = jnp.max(first_scores, axis=-1)
    first_exp = jnp.exp(first_scores - first_max[:, :, None])
    first_sum = jnp.sum(first_exp, axis=-1)
    first_acc = jnp.einsum(
        "nvf,fnr->nvr",
        first_exp.astype(jnp.bfloat16),
        latent_pair_rows[:, 1],
        preferred_element_type=jnp.float32,
    )
    piece = lax.all_gather(frames, "mp", axis=1, tiled=True)
    run_max = jnp.broadcast_to(first_max, (owned,) + first_max.shape)
    run_sum = jnp.broadcast_to(first_sum, (owned,) + first_sum.shape)
    run_acc = jnp.broadcast_to(first_acc, (owned,) + first_acc.shape)
    width = piece.shape[1]
    media = layer_norm(piece, norm_gains[0]).astype(jnp.bfloat16)
    media_pairs = (
        jnp.einsum("fpe,ekc->fpkc", media, res_kv, preferred_element_type=jnp.float32)
        .astype(jnp.bfloat16)
        .reshape(owned, width, 2, res_local, RESAMPLE_HEAD_DIM)
    )
    score_matrix = (
        jnp.einsum(
            "lhd,fphd->fhlp",
            resampler_heads,
            media_pairs[:, :, 0],
            preferred_element_type=jnp.float32,
        )
        * res_scale
    )
    new_max = jnp.maximum(run_max, jnp.max(score_matrix, axis=-1))
    fade = jnp.exp(run_max - new_max)
    unnormalized_weights = jnp.exp(score_matrix - new_max[..., None])
    new_sum = run_sum * fade + jnp.sum(unnormalized_weights, axis=-1)
    new_acc = run_acc * fade[..., None] + jnp.einsum(
        "fhlp,fphd->fhld",
        unnormalized_weights.astype(jnp.bfloat16),
        media_pairs[:, :, 1],
        preferred_element_type=jnp.float32,
    )
    res_context = (new_acc / new_sum[..., None]).astype(jnp.bfloat16)
    out_rows = lax.dynamic_slice_in_dim(res_out, lax.axis_index("mp") * res_cols, res_cols, 0)
    out_heads = out_rows.reshape(res_local, RESAMPLE_HEAD_DIM, E)
    part = res_context
    update = lax.psum_scatter(
        jnp.einsum("fhlr,hre->lfe", part, out_heads, preferred_element_type=jnp.float32).astype(
            jnp.bfloat16
        ),
        "mp",
        scatter_dimension=0,
        tiled=True,
    ).astype(jnp.float32)
    base_rows = lax.dynamic_slice_in_dim(
        latent_init, lax.axis_index("mp") * share, share, 0
    ).astype(jnp.float32)
    latents = layer_norm(base_rows[:, None, :] + update, norm_gains[2]).astype(jnp.bfloat16)
    gathered = lax.all_gather(latents, ("segment", "dp"), axis=1, tiled=True)
    group = lax.axis_index(("segment", "dp"))
    wanted = group * owned + jnp.arange(owned, dtype=jnp.int32)
    picker = (frame_dest[None, :] == wanted[:, None]).astype(jnp.bfloat16)
    mine = jnp.einsum("js,rse->rje", picker, gathered, preferred_element_type=jnp.float32).astype(
        jnp.bfloat16
    )
    dest = lax.all_gather(mine, "mp", axis=0, tiled=True)
    whole_text = lax.all_gather(text[0], "mp", axis=2, tiled=True)
    seq_local = whole_text.shape[0]
    txt_len = whole_text.shape[1]
    tokens = seq_local * txt_len
    text_norm = (
        layer_norm(whole_text, text_gain[0])
        .astype(jnp.bfloat16)
        .reshape(tokens, whole_text.shape[2])
    )
    head_cols = w_query.shape[2]
    head_local = head_cols // HD
    query_sum = jnp.dot(
        text_norm,
        lax.all_gather(w_query[0], "dp", axis=0, tiled=True),
        preferred_element_type=jnp.float32,
    )
    query_matrix = query_sum.astype(jnp.bfloat16).reshape(seq_local, txt_len, head_local, HD)
    full_kv = lax.all_gather(w_kv[0], "dp", axis=0, tiled=True)
    pair_sum = jnp.einsum("lje,ekc->jlkc", dest, full_kv, preferred_element_type=jnp.float32)
    pair_list = pair_sum.astype(jnp.bfloat16).reshape(seq_local, FMAX * LAT, 2, head_local, HD)
    live = jnp.repeat(
        jnp.arange(FMAX, dtype=jnp.int32)[None, :] < frame_counts[0][:, None], LAT, axis=1
    )
    gate = jnp.tanh(xgate[0])

    def local_attend(pair_in):
        return jax.vmap(attend, in_axes=(0, 0, 0, None))(query_matrix, pair_in, live, gate)

    gated, pull = jax.vjp(local_attend, pair_list)
    context = gated.astype(jnp.bfloat16)[None]
    (pair_grad,) = pull(cotangent[0].astype(jnp.float32))
    pair_grad = pair_grad.reshape(owned, LAT, 2, head_cols)
    part = pair_grad
    dest_grad = lax.psum_scatter(
        jnp.einsum("jlkc,ekc->lje", part, full_kv, preferred_element_type=jnp.float32).astype(
            jnp.bfloat16
        ),
        "mp",
        scatter_dimension=0,
        tiled=True,
    ).astype(jnp.float32)
    every_grad = lax.all_gather(
        dest_grad.astype(jnp.bfloat16), ("segment", "dp"), axis=1, tiled=True
    ).astype(dest_grad.dtype)
    targets = lax.dynamic_slice_in_dim(frame_dest, group * owned, owned, 0)
    chooser = (jnp.arange(slots, dtype=jnp.int32)[None, :] == targets[:, None]).astype(jnp.float32)
    latent_grad = jnp.einsum("js,rse->rje", chooser, every_grad, precision=lax.Precision.HIGHEST)
    return (context, latent_grad)


def solution(mesh):
    in_specs = (
        P(("segment", "dp"), "mp", None),
        P(),
        P(),
        P(None, "mp"),
        P(None, None, "mp"),
        P(),
        P("segment", "dp", None, "mp"),
        P("segment", None),
        P("segment", "dp", "mp"),
        P("segment", "dp", None, "mp"),
        P("segment"),
        P("segment", "dp"),
        P(),
        P("segment", "dp", None, "mp"),
    )
    out_specs = (P("segment", "dp", None, "mp"), P("mp", ("segment", "dp"), None))
    return jax.shard_map(
        per_device, mesh=mesh, in_specs=in_specs, out_specs=out_specs, check_vma=False
    )
```

profile of v0, /device:TPU:1, one launch (start us, length us, event | category | flops | bytes accessed | tf_op | source)
XLA Modules:
  0.0 658.1 jit_solution(9813244482838572930)
XLA Ops:
  14.1 52.8 %all-gather.11.cloned.1.call-done = bf16[8,128,1536]{2,1,0:T(8,128)(2,1)} async-done(((bf16[8,8,1536]{2,1,0:T(8,128)(2,1)}), bf16[8,128,1536]{2,1,0:T(8,128)(2,1)}) %all-gather.11.cloned.1.call-update) | async-done | bytes 3145744 | tf_op jit(solution)/shard_map/all_gather | solution.py:92
  66.9 2.5 convert_reduce_fusion.1
  69.5 2.8 fusion.15
  79.0 75.6 %reduce-scatter.3.cloned.1.call-done = bf16[4,8,1536]{2,1,0:T(8,128)(2,1)} async-done(((bf16[64,8,1536]{2,1,0:T(8,128)(2,1)}), bf16[4,8,1536]{2,1,0:T(8,128)(2,1)}) %reduce-scatter.3.cloned.1.call-update) | async-done | bytes 98320 | tf_op jit(solution)/shard_map/reduce_scatter | solution.py:126
  158.4 2.1 copy.40
  160.6 38.4 %all-gather.13.cloned.1.call-done = bf16[4,128,1536]{2,0,1:T(4,128)(2,1)} async-done(((bf16[4,8,1536]{2,0,1:T(4,128)(2,1)}), bf16[4,128,1536]{2,0,1:T(4,128)(2,1)}) %all-gather.13.cloned.1.call-update) | async-done | bytes 1572880 | tf_op jit(solution)/shard_map/all_gather | solution.py:138
  199.0 2.4 fusion.49
  206.3 34.1 %all-gather.19.cloned.1.call-done = bf16[1,1536,2,512]{3,1,2,0:T(8,128)(2,1)} async-done(((bf16[1,384,2,512]{3,1,2,0:T(8,128)(2,1)}), bf16[1,1536,2,512]{3,1,2,0:T(8,128)(2,1)}) %all-gather.19.cloned.1.call-update) | async-done | bytes 3145744 | tf_op jit(solution)/shard_map/all_gather | solution.py:163
  240.4 50.8 %all-gather.15.cloned.1.call-done = bf16[64,8,1536]{2,1,0:T(8,128)(2,1)} async-done(((bf16[4,8,1536]{2,1,0:T(8,128)(2,1)}), bf16[64,8,1536]{2,1,0:T(8,128)(2,1)}) %all-gather.15.cloned.1.call-update) | async-done | bytes 1572880 | tf_op jit(solution)/shard_map/all_gather | solution.py:145
  291.2 4.1 fusion.69
  297.1 100.5 %all-gather.21.cloned.1.call-done = bf16[1,1,768,8192]{3,2,1,0:T(8,128)(2,1)} async-done(((bf16[1,1,768,512]{3,2,1,0:T(8,128)(2,1)}), bf16[1,1,768,8192]{3,2,1,0:T(8,128)(2,1)}) %all-gather.21.cloned.1.call-update) | async-done | bytes 12582928 | tf_op jit(solution)/shard_map/all_gather | solution.py:146
  397.7 6.4 convert_reduce_fusion
  404.0 8.0 %fusion.3 = f32[768]{0:T(1024)S(1)} fusion(bf16[1,1,768,8192]{3,2,1,0:T(8,128)(2,1)} %all-gather.21.cloned.1.call-done, f32[768]{0:T(1024)S(1)} %broadcast_multiply_fusion), kind=kLoop, calls=%fused_computation.5 | loop fusion | flops 25165056 | bytes 12589056 | tf_op jit(solution)/shard_map/reduce_sum | solution.py:18
  412.0 72.3 %all-gather.23.cloned.1.call-done = bf16[1,8192,512]{2,1,0:T(8,128)(2,1)} async-done(((bf16[1,2048,512]{2,1,0:T(8,128)(2,1)}), bf16[1,8192,512]{2,1,0:T(8,128)(2,1)}) %all-gather.23.cloned.1.call-update) | async-done | bytes 8388624 | tf_op jit(solution)/shard_map/all_gather | solution.py:159
  484.3 17.6 %fusion.64 = bf16[768,512]{0,1:T(8,128)(2,1)S(1)} fusion(bf16[1,8192,512]{2,1,0:T(8,128)(2,1)} %all-gather.23.cloned.1.call-done, bf16[1,1,768,8192]{3,2,1,0:T(8,128)(2,1)} %all-gather.21.cloned.1.call-done, f32[8192]{0:T(1024)S(1)} %bitcast.222, f32[768]{0:T(1024)S(1)} %add_rsqrt_fusion, f32[768]{0:T(1024)S(1)} %broadcast_multiply_fusion), kind=kOutput, calls=%fused_computation.65 | convolution fusion | flops 6474301440 | bytes 21796864 | tf_op jit(solution)/shard_map/dot_general | solution.py:157
  506.2 2.8 fusion.53
  508.9 7.0 %fusion.85 = bf16[1,512,1,4,128]{1,4,3,2,0:T(8,128)(2,1)} fusion(bf16[768,4,128]{0,2,1:T(8,128)(2,1)S(1)} %bitcast.217, f32[4,768,512]{1,2,0:T(8,128)} %copy-done.2, f32[4,768]{1,0:T(4,128)S(1)} %negate_bitcast_fusion, f32[4,768]{1,0:T(4,128)S(1)} %get-tuple-element.21, pred[512]{0:T(512)(128)(4,1)S(1)} %broadcast_in_dim.37, ...), kind=kOutput, calls=%fused_computation.70 | convolution fusion | flops 820117504 | bytes 9736704 | tf_op jit(solution)/shard_map/transpose(jvp(vmap(rag,lag->arl)))/dot_general | solution.py:23
  516.0 2.1 pad_add_fusion
  518.1 2.8 reshape.439
  520.9 3.4 copy.54
  524.2 5.3 fusion.44
  529.6 77.0 %reduce-scatter.5.cloned.1.call-done = bf16[4,8,1536]{2,1,0:T(8,128)(2,1)} async-done(((bf16[64,8,1536]{2,1,0:T(8,128)(2,1)}), bf16[4,8,1536]{2,1,0:T(8,128)(2,1)}) %reduce-scatter.5.cloned.1.call-update) | async-done | bytes 98320 | tf_op jit(solution)/shard_map/reduce_scatter | solution.py:179
  607.9 41.2 %all-gather.17.cloned.1.call-done = bf16[4,128,1536]{2,1,0:T(8,128)(2,1)} async-done(((bf16[4,8,1536]{2,1,0:T(8,128)(2,1)}), bf16[4,128,1536]{2,1,0:T(8,128)(2,1)}) %all-gather.17.cloned.1.call-update) | async-done | bytes 1572880 | tf_op jit(solution)/shard_map/all_gather | solution.py:187
  649.1 2.5 convolution_bitcast_fusion.1
  (82 shorter events, 28.2 us)
Async XLA Ops:
  7.2 3.9 copy-start
  7.2 59.8 %all-gather.11.cloned.1.call-start = ((), (), s32[]{:S(2)}) async-start(), calls=%async_computation.2 | async-start | bytes 3342336 | tf_op jit(solution)/shard_map/all_gather | solution.py:92
  7.9 146.7 %reduce-scatter.3.cloned.1.call-start = ((), (), s32[]{:S(2)}) async-start(), calls=%async_computation.3 | async-start | bytes 1671168 | tf_op jit(solution)/shard_map/reduce_scatter | solution.py:126
  66.9 5.4 copy-start.3
  73.8 125.2 %copy-start.8 = (s32[128]{0:T(128)S(1)}, s32[128]{0:T(128)}, u32[]{:S(2)}) copy-start(s32[128]{0:T(128)} %param.26) | copy-start | bytes 1540
  76.2 127.4 %copy-start.5 = (bf16[1,1,768,512]{3,2,1,0:T(8,128)(2,1)S(1)}, bf16[1,1,768,512]{3,2,1,0:T(8,128)(2,1)}, u32[]{:S(2)}) copy-start(bf16[1,1,768,512]{3,2,1,0:T(8,128)(2,1)} %param.27) | copy-start | bytes 2359300
  78.2 120.8 %all-gather.13.cloned.1.call-start = ((), (), s32[]{:S(2)}) async-start(), calls=%async_computation.4 | async-start | bytes 1671168 | tf_op jit(solution)/shard_map/all_gather | solution.py:138
  158.4 47.9 %copy-start.7 = (bf16[1,8192]{1,0:T(2,128)(2,1)S(1)}, bf16[1,8192]{1,0:T(2,128)(2,1)}, u32[]{:S(2)}) copy-start(bf16[1,8192]{1,0:T(2,128)(2,1)} %param.21) | copy-start | bytes 49156
  158.4 82.0 %all-gather.19.cloned.1.call-start = ((), (), s32[]{:S(2)}) async-start(), calls=%async_computation.8 | async-start | bytes 3932160 | tf_op jit(solution)/shard_map/all_gather | solution.py:163
  160.6 130.6 %all-gather.15.cloned.1.call-start = ((), (), s32[]{:S(2)}) async-start(), calls=%async_computation.5 | async-start | bytes 1671168 | tf_op jit(solution)/shard_map/all_gather | solution.py:145
  201.5 196.2 %all-gather.21.cloned.1.call-start = ((), (), s32[]{:S(2)}) async-start(), calls=%async_computation.9 | async-start | bytes 13369344 | tf_op jit(solution)/shard_map/all_gather | solution.py:146
  202.1 282.2 %all-gather.23.cloned.1.call-start = ((), (), s32[]{:S(2)}) async-start(), calls=%async_computation.10 | async-start | bytes 10485760 | tf_op jit(solution)/shard_map/all_gather | solution.py:159
  202.8 403.8 %reduce-scatter.5.cloned.1.call-start = ((), (), s32[]{:S(2)}) async-start(), calls=%async_computation.6 | async-start | bytes 1671168 | tf_op jit(solution)/shard_map/reduce_scatter | solution.py:179
  501.8 2.6 copy-start.4
  502.9 3.2 copy-start.2
  524.2 82.5 %copy-start.6 = (bf16[1,768,4,128]{1,3,2,0:T(8,128)(2,1)S(1)}, bf16[1,768,4,128]{1,3,2,0:T(8,128)(2,1)}, u32[]{:S(2)}) copy-start(bf16[1,768,4,128]{1,3,2,0:T(8,128)(2,1)} %get-tuple-element.14) | copy-start | bytes 2359300
  524.2 127.3 %copy-start.1 = (bf16[1536,2,96]{0,2,1:T(8,128)(2,1)S(1)}, bf16[1536,2,96]{0,2,1:T(8,128)(2,1)}, u32[]{:S(2)}) copy-start(bf16[1536,2,96]{0,2,1:T(8,128)(2,1)} %param.18) | copy-start | bytes 1769476
  529.6 119.5 %all-gather.17.cloned.1.call-start = ((), (), s32[]{:S(2)}) async-start(), calls=%async_computation.7 | async-start | bytes 1671168 | tf_op jit(solution)/shard_map/all_gather | solution.py:187
Sparse Core Ops, SparseCore 0:
  10.4 56.4 all-gather.10
  78.3 76.1 reduce-scatter.2
  158.5 40.4 all-gather.12
  201.3 39.1 all-gather.18
  243.3 47.8 all-gather.14
  293.5 104.1 all-gather.20
  399.5 84.7 all-gather.22
  529.7 76.8 reduce-scatter.4
  608.5 40.5 all-gather.16
where the time goes:
time: 659 us; the launch traced here: 658 us
  waiting for transfers between devices  545 us (83%)
  matrix products  50.9 us (8%)
  other arithmetic  30.7 us (5%)
  local copies, waits for them, and re-layouts  15.8 us (2%)
  between operations  15.5 us (2%)
    all_gather x1, waiting for transfers between devices, per_device(): whole_text = lax.all_gather(text[0], 'mp', axis=2, tiled=True)  101 us
    reduce_scatter x1, waiting for transfers between devices, per_device(): lax.psum_scatter(jnp.einsum('jlkc,ekc->lje', part, full_kv, preferred_ele...  77 us
    reduce_scatter x1, waiting for transfers between devices, per_device(): lax.psum_scatter(jnp.einsum('fhlr,hre->lfe', part, out_heads, preferred_e...  75.6 us
    all_gather x1, waiting for transfers between devices, per_device(): lax.all_gather(w_query[0], 'dp', axis=0, tiled=True)  72.3 us
    all_gather x1, waiting for transfers between devices, per_device(): piece = lax.all_gather(frames, 'mp', axis=1, tiled=True)  52.8 us
    all_gather x1, waiting for transfers between devices, per_device(): dest = lax.all_gather(mine, 'mp', axis=0, tiled=True)  50.8 us
    all_gather x1, waiting for transfers between devices, per_device(): lax.all_gather(dest_grad.astype(jnp.bfloat16), ('segment', 'dp'), axis=1,...  41.2 us
    all_gather x1, waiting for transfers between devices, per_device(): gathered = lax.all_gather(latents, ('segment', 'dp'), axis=1, tiled=True)  38.4 us
  transfers between devices with their start and end apart: 9, of which 9 were waited for; matrix products, arithmetic and copies ran while one was open for 5% of the time, Pallas kernels for 0%

commit v1 on v0

v1 whole, which is shorter than its diff:
```python
import functools
import math

import jax
import jax.numpy as jnp
from jax import lax
from jax.experimental import pallas as pl
from jax.experimental.pallas import tpu as pltpu
from jax.sharding import PartitionSpec as P

HD = 128
E = 1536
RESAMPLE_HEAD_DIM = 96
LAT = 64
FMAX = 8
SIDE = 4
GROUP = ("segment", "dp")
BF16 = jnp.bfloat16
F32 = jnp.float32
VMEM_LIMIT = 56 * 1024 * 1024


def layer_norm(inputs, gain_row):
    values = inputs.astype(F32)
    center = values - jnp.mean(values, axis=-1, keepdims=True)
    spread = jnp.mean(center * center, axis=-1, keepdims=True)
    return center * lax.rsqrt(spread + 1e-05) * gain_row.astype(F32)


def shift(value, axis, by):
    pairs = []
    for i in range(SIDE * SIDE):
        y, x = divmod(i, SIDE)
        if axis == "x":
            x = (x + by) % SIDE
        else:
            y = (y + by) % SIDE
        pairs.append((i, y * SIDE + x))
    return lax.ppermute(value, "mp", pairs)


def ring(value, axis):
    half = value.shape[0] // 2
    left = shift(value, axis, 1)
    right = shift(value, axis, -1)
    far = jnp.concatenate([shift(left[:half], axis, 1), shift(right[half:], axis, -1)], axis=0)
    return [value, left, right, far]


def dp_blocks(value):
    over_z = lax.ppermute(value, "dp", [(0, 2), (1, 3), (2, 0), (3, 1)])
    mate = [(0, 1), (1, 0), (2, 3), (3, 2)]
    return [value, lax.ppermute(value, "dp", mate), over_z, lax.ppermute(over_z, "dp", mate)]


def query_kernel(where, text_ref, gain_ref, w0, w1, w2, w3, out_ref, normed):
    rows, depth = text_ref.shape
    width = 512

    @pl.loop(0, rows // 16)
    def _(step):
        at = pl.ds(pl.multiple_of(step * 16, 16), 16)
        total = jnp.zeros((16, width), F32)
        for c in range(depth // width):
            total += text_ref[at, c * width : (c + 1) * width].astype(F32)
        mean = jnp.sum(total, axis=1, keepdims=True) * (1.0 / depth)
        total = jnp.zeros((16, width), F32)
        for c in range(depth // width):
            center = text_ref[at, c * width : (c + 1) * width].astype(F32) - mean
            total += center * center
        spread = jnp.sum(total, axis=1, keepdims=True) * (1.0 / depth)
        scale = lax.rsqrt(spread + 1e-05)
        for c in range(depth // width):
            cols = slice(c * width, (c + 1) * width)
            center = text_ref[at, cols].astype(F32) - mean
            normed[at, cols] = (center * scale * gain_ref[:, cols].astype(F32)).astype(BF16)

    total = None
    for j, weight in enumerate((w0, w1, w2, w3)):
        block = weight.shape[0]
        cols = pl.ds(pl.multiple_of(where[j] * block, block), block)
        term = jnp.dot(normed[:, cols], weight[...], preferred_element_type=F32)
        total = term if total is None else total + term
    out_ref[...] = total.astype(BF16)


def query_matmul(text, gain, weights, where):
    tokens, depth = text.shape
    cols = weights[0].shape[1]
    rows = 128
    return pl.pallas_call(
        query_kernel,
        grid_spec=pltpu.PrefetchScalarGridSpec(
            num_scalar_prefetch=1,
            grid=(tokens // rows,),
            in_specs=[
                pl.BlockSpec((rows, depth), lambda i, w: (i, 0)),
                pl.BlockSpec((1, depth), lambda i, w: (0, 0)),
            ]
            + [pl.BlockSpec(w.shape, lambda i, w: (0, 0)) for w in weights],
            out_specs=pl.BlockSpec((rows, cols), lambda i, w: (i, 0)),
            scratch_shapes=[pltpu.VMEM((rows, depth), BF16)],
        ),
        out_shape=jax.ShapeDtypeStruct((tokens, cols), BF16),
        compiler_params=pltpu.CompilerParams(vmem_limit_bytes=VMEM_LIMIT),
    )(where, text, gain, *weights)


def attend_kernel(count, gate_ref, q_ref, k_ref, v_ref, cot_ref, ctx_ref, dk_ref, dv_ref, acc_k, acc_v):
    tokens = q_ref.shape[0]
    keys = k_ref.shape[0]
    rows = 256
    gate = gate_ref[0]
    slot = lax.broadcasted_iota(jnp.int32, (rows, keys), 1) % FMAX
    live = slot < count[0]
    across = (((1,), (1,)), ((), ()))
    down = (((0,), (0,)), ((), ()))
    for step in range(tokens // rows):
        at = slice(step * rows, (step + 1) * rows)
        q = q_ref[at, :]
        score = lax.dot_general(q, k_ref[...], across, preferred_element_type=F32)
        score = jnp.where(live, score * (1.0 / math.sqrt(HD)), -1e30)
        weight = jnp.exp(score - jnp.max(score, axis=1, keepdims=True))
        inverse = 1.0 / jnp.sum(weight, axis=1, keepdims=True)
        rounded = weight.astype(BF16)
        blend = jnp.dot(rounded, v_ref[...], preferred_element_type=F32) * inverse
        ctx_ref[at, :] = (gate * blend).astype(BF16)
        cot = gate * cot_ref[at, :].astype(F32)
        d_blend = (cot * inverse).astype(BF16)
        d_sum = -jnp.sum(cot * blend, axis=1, keepdims=True) * inverse
        d_weight = lax.dot_general(d_blend, v_ref[...], across, preferred_element_type=F32)
        d_weight = d_weight.astype(BF16).astype(F32) + d_sum
        d_score = (d_weight * weight * (1.0 / math.sqrt(HD))).astype(BF16)
        grad_k = lax.dot_general(d_score, q, down, preferred_element_type=F32)
        grad_v = lax.dot_general(rounded, d_blend, down, preferred_element_type=F32)
        if step == 0:
            acc_k[...] = grad_k
            acc_v[...] = grad_v
        else:
            acc_k[...] += grad_k
            acc_v[...] += grad_v
    dk_ref[...] = acc_k[...].astype(BF16)
    dv_ref[...] = acc_v[...].astype(BF16)


def attention(query, pairs, cot, count, gate):
    tokens, cols = query.shape
    keys = pairs.shape[0]
    heads = cols // HD
    head = lambda n: pl.BlockSpec((n, HD), lambda h, c: (0, h))
    return pl.pallas_call(
        attend_kernel,
        grid_spec=pltpu.PrefetchScalarGridSpec(
            num_scalar_prefetch=1,
            grid=(heads,),
            in_specs=[
                pl.BlockSpec(memory_space=pltpu.SMEM),
                head(tokens),
                head(keys),
                pl.BlockSpec((keys, HD), lambda h, c: (0, h + heads)),
                head(tokens),
            ],
            out_specs=[head(tokens), head(keys), head(keys)],
            scratch_shapes=[pltpu.VMEM((keys, HD), F32), pltpu.VMEM((keys, HD), F32)],
        ),
        out_shape=[
            jax.ShapeDtypeStruct((tokens, cols), BF16),
            jax.ShapeDtypeStruct((keys, cols), BF16),
            jax.ShapeDtypeStruct((keys, cols), BF16),
        ],
        compiler_params=pltpu.CompilerParams(vmem_limit_bytes=VMEM_LIMIT),
    )(count, gate, query, pairs, pairs, cot)


def per_device(
    frames,
    latent_init,
    norm_gains,
    res_query,
    res_kv,
    res_out,
    text,
    text_gain,
    w_query,
    w_kv,
    xgate,
    frame_counts,
    frame_dest,
    cotangent,
):
    mp_count = lax.axis_size("mp")
    group = lax.axis_index(GROUP)
    dp = lax.axis_index("dp")
    share = LAT // mp_count
    slots = frame_dest.shape[0]
    owned = frames.shape[0]
    groups = slots // owned
    width = res_query.shape[1]
    res_scale = 1.0 / math.sqrt(RESAMPLE_HEAD_DIM)

    whole_text = lax.all_gather(text[0, 0], "mp", axis=1, tiled=True)
    media = layer_norm(frames, norm_gains[0]).astype(BF16)
    half = owned // 2
    ring_x = [ring(media[:half], "x"), ring(media[half:], "y")]
    query_blocks = dp_blocks(w_query[0])
    kv_local = jnp.concatenate([w_kv[0, :, 0], w_kv[0, :, 1]], axis=1)
    kv_blocks = dp_blocks(kv_local)

    lat_norm = layer_norm(latent_init, norm_gains[1]).astype(BF16)
    res_pair = jnp.concatenate([res_kv[:, 0], res_kv[:, 1]], axis=1)
    res_q = jnp.dot(lat_norm, res_query, preferred_element_type=F32).astype(BF16)
    lat_pairs = jnp.dot(lat_norm, res_pair, preferred_element_type=F32).astype(BF16)
    media_halves = []
    for blocks, axis in zip(ring_x, ("y", "x")):
        joined = jnp.concatenate(blocks, axis=1)
        parts = [
            jnp.einsum("fpe,ec->fpc", block, res_pair, preferred_element_type=F32).astype(BF16)
            for block in ring(joined, axis)
        ]
        media_halves.append(jnp.concatenate(parts, axis=1))
    media_pairs = jnp.concatenate(media_halves, axis=0)
    pair_list = jnp.concatenate(
        [jnp.broadcast_to(lat_pairs, (owned,) + lat_pairs.shape), media_pairs], axis=1
    )
    score = (
        jnp.einsum("ld,fpd->flp", res_q, pair_list[:, :, :width], preferred_element_type=F32)
        * res_scale
    )
    weights = jnp.exp(score - jnp.max(score, axis=-1, keepdims=True))
    blend = jnp.einsum(
        "flp,fpd->fld", weights.astype(BF16), pair_list[:, :, width:], preferred_element_type=F32
    )
    res_context = (blend / jnp.sum(weights, axis=-1)[:, :, None]).astype(BF16)

    piece = res_context.reshape(owned, groups, share * width).swapaxes(0, 1)
    piece = lax.all_to_all(piece, GROUP, 0, 0, tiled=True).reshape(slots, share * width)
    slot_ids = jnp.arange(slots, dtype=jnp.int32)
    to_dest = (frame_dest[None, :] == slot_ids[:, None]).astype(BF16)
    piece = jnp.dot(to_dest, piece, preferred_element_type=F32).astype(BF16)
    piece = lax.all_to_all(
        piece.reshape(mp_count, owned, share * width), "mp", 0, 0, tiled=True
    )
    rows = piece.reshape(mp_count, owned, share, width).transpose(2, 1, 0, 3)
    update = jnp.einsum(
        "lfc,ce->lfe", rows.reshape(share, owned, E), res_out, preferred_element_type=F32
    )
    base_rows = lax.dynamic_slice_in_dim(latent_init, group * share, share, 0).astype(F32)
    latents = layer_norm(base_rows[:, None, :] + update, norm_gains[2]).astype(BF16)
    dp_count = lax.axis_size("dp")

    def place(g, m):
        return (g // dp_count * mp_count + m) * dp_count + g % dp_count

    mine = lax.ppermute(
        latents.reshape(share * owned, E),
        ("segment", "mp", "dp"),
        [(place(g, m), place(m, g)) for g in range(groups) for m in range(mp_count)],
    )
    dest = lax.all_to_all(
        jnp.broadcast_to(mine, (mp_count,) + mine.shape), "mp", 0, 0, tiled=True
    ).reshape(LAT * owned, E)

    where = jnp.stack([dp, dp ^ 1, dp ^ 2, dp ^ 3]).astype(jnp.int32)
    query = query_matmul(whole_text, text_gain, query_blocks, where)
    full_kv = jnp.zeros((E, kv_local.shape[1]), BF16)
    for j, block in enumerate(kv_blocks):
        full_kv = lax.dynamic_update_slice_in_dim(
            full_kv, block, where[j] * kv_local.shape[0], 0
        )
    pairs = jnp.dot(dest, full_kv, preferred_element_type=F32).astype(BF16)
    context, grad_k, grad_v = attention(
        query, pairs, cotangent[0, 0], frame_counts[0], jnp.tanh(xgate)
    )

    grad = jnp.concatenate([grad_k, grad_v], axis=1)
    part = lax.dot_general(
        grad, full_kv, (((1,), (1,)), ((), ())), preferred_element_type=F32
    ).astype(BF16)
    part = lax.all_to_all(part.reshape(mp_count, share * owned, E), "mp", 0, 0, tiled=True)
    dest_grad = jnp.sum(part.astype(F32), axis=0).astype(BF16)
    cut = groups // share
    send = (
        dest_grad.reshape(share, owned, cut, E // cut)
        .transpose(0, 2, 1, 3)
        .reshape(groups, owned, E // cut)
    )
    send = lax.all_to_all(send, GROUP, 0, 0, tiled=True).reshape(slots, E // cut)
    to_owner = (frame_dest[:, None] == slot_ids[None, :]).astype(BF16)
    send = jnp.dot(to_owner, send, preferred_element_type=F32).astype(BF16)
    send = lax.all_to_all(send.reshape(groups, owned, E // cut), GROUP, 0, 0, tiled=True)
    latent_grad = (
        send.reshape(share, cut, owned, E // cut)
        .transpose(0, 2, 1, 3)
        .reshape(share, owned, E)
        .astype(F32)
    )
    return (context[None, None], latent_grad)


def solution(mesh):
    in_specs = (
        P(("segment", "dp"), "mp", None),
        P(),
        P(),
        P(None, "mp"),
        P(None, None, "mp"),
        P(),
        P("segment", "dp", None, "mp"),
        P("segment", None),
        P("segment", "dp", "mp"),
        P("segment", "dp", None, "mp"),
        P("segment"),
        P("segment", "dp"),
        P(),
        P("segment", "dp", None, "mp"),
    )
    out_specs = (P("segment", "dp", None, "mp"), P("mp", ("segment", "dp"), None))
    return jax.shard_map(
        per_device, mesh=mesh, in_specs=in_specs, out_specs=out_specs, check_vma=False
    )
```

time: 659 us -> 285 us (0.43)
  waiting for transfers between devices: 545 us -> 79.3 us
  starting transfers between devices: 0.36 us -> 63.8 us
  blocking collectives: 0 us -> 49.9 us
  Pallas kernels: 0 us -> 37.7 us
  matrix products: 50.9 us -> 15.6 us
  other arithmetic: 30.7 us -> 9.21 us
    all_gather x7 -> x1, waiting for transfers between devices: 390 us -> 0.01 us  [per_device(): whole_text = lax.all_gather(text[0, 0], 'mp', axis=1, tiled=True)]
    reduce_scatter x2 -> x0, waiting for transfers between devices: 153 us -> none  [the longest x1 77 us: per_device(): lax.psum_scatter(jnp.einsum('jlkc,ekc->lje', part, full_kv, preferred_ele...]
    all_to_all x0 -> x3, waiting for transfers between devices: none -> 58.1 us  [the longest x1 35.6 us: per_device(): lax.all_to_all(piece, GROUP, 0, 0, tiled=True).reshape(slots, share * width)]
    all_to_all x0 -> x3, blocking collectives: none -> 49.9 us  [the longest x1 26.1 us: per_device(): lax.all_to_all(part.reshape(mp_count, share * owned, E), 'mp', 0, 0, tile...]
    pallas_call x0 -> x2, Pallas kernels: none -> 37.7 us  [the longest x1 26.5 us: query_matmul(): pl.pallas_call(query_kernel, grid_spec=pltpu.PrefetchScalarGridSpec(num_s...]
    dot_general x16, matrix products: 50.9 us -> 15.6 us  [the longest x1 4.19 us: per_device(): pairs = jnp.dot(dest, full_kv, preferred_element_type=F32).astype(BF16)]
    ppermute x0 -> x23, starting transfers between devices: none -> 34.1 us  [the longest x16 24.4 us: shift(): return lax.ppermute(value, 'mp', pairs)]
    all_to_all x0 -> x3, starting transfers between devices: none -> 29.7 us  [the longest x1 13.4 us: per_device(): lax.all_to_all(jnp.broadcast_to(mine, (mp_count,) + mine.shape), 'mp', 0,...]
  transfers between devices with their start and end apart: 9 -> 27, of which waited for: 9 -> 12; matrix products, arithmetic and copies ran while one was open for 5% -> 11% of each run, Pallas kernels for 0% -> 0%
where the time goes in v1:
time: 285 us; the launch traced here: 284 us
  waiting for transfers between devices  79.3 us (28%)
  starting transfers between devices  63.8 us (22%)
  blocking collectives  49.9 us (18%)
  Pallas kernels  37.7 us (13%)
  between operations  15.8 us (6%)
  matrix products  15.6 us (5%)
  local copies, waits for them, and re-layouts  12.6 us (4%)
  other arithmetic  9.21 us (3%)
    all_to_all x1, waiting for transfers between devices, per_device(): lax.all_to_all(piece, GROUP, 0, 0, tiled=True).reshape(slots, share * width)  35.6 us
    pallas_call x1, Pallas kernels, query_matmul(): pl.pallas_call(query_kernel, grid_spec=pltpu.PrefetchScalarGridSpec(num_s...  26.5 us
    all_to_all x1, blocking collectives, per_device(): lax.all_to_all(part.reshape(mp_count, share * owned, E), 'mp', 0, 0, tile...  26.1 us
    ppermute x16, starting transfers between devices, shift(): return lax.ppermute(value, 'mp', pairs)  24.4 us
    all_to_all x1, waiting for transfers between devices, per_device(): lax.all_to_all(jnp.broadcast_to(mine, (mp_count,) + mine.shape), 'mp', 0,...  16 us
    ppermute x16, waiting for transfers between devices, shift(): return lax.ppermute(value, 'mp', pairs)  15.3 us
    all_to_all x1, starting transfers between devices, per_device(): lax.all_to_all(jnp.broadcast_to(mine, (mp_count,) + mine.shape), 'mp', 0,...  13.4 us
    all_to_all x1, blocking collectives, per_device(): lax.all_to_all(send, GROUP, 0, 0, tiled=True).reshape(slots, E // cut)  12.9 us
  transfers between devices with their start and end apart: 27, of which 12 were waited for; matrix products, arithmetic and copies ran while one was open for 11% of the time, Pallas kernels for 0%

profile of v1, /device:TPU:1, one launch (start us, length us, event | category | flops | bytes accessed | tf_op | source)
XLA Modules:
  0.0 284.0 jit_solution(4351709013102175000)
XLA Ops:
  12.1 3.7 %collective-permute-start.12 = (bf16[4,8,1536]{2,1,0:T(8,128)(2,1)S(1)}, bf16[4,8,1536]{2,1,0:T(8,128)(2,1)S(1)}, u32[]{:S(2)}, u32[]{:S(2)}) collective-permute-start(bf16[4,8,1536]{2,1,0:T(8,128)(2,1)S(1)} %get-tuple-element.18), channel_id=1, source_target_pairs={{0,48},{4,52},{8,56},{12,60},{16,0},{20,4},{24,8},{28,12},{32,16},... | collective-permute-start | bytes 294920 | tf_op jit(solution)/shard_map/ppermute | solution.py:39
  15.8 2.5 collective-permute-start.4
  21.0 3.0 %collective-permute-start.14 = (bf16[2,8,1536]{2,1,0:T(8,128)(2,1)S(1)}, bf16[2,8,1536]{2,1,0:T(8,128)(2,1)S(1)}, u32[]{:S(2)}, u32[]{:S(2)}) collective-permute-start(bf16[2,8,1536]{2,1,0:T(8,128)(2,1)S(1)} %slice.83), channel_id=1, source_target_pairs={{0,48},{4,52},{8,56},{12,60},{16,0},{20,4},{24,8},{28,12},{32,16},... | collective-permute-start | bytes 147464 | tf_op jit(solution)/shard_map/ppermute | solution.py:39
  24.2 3.0 %collective-permute-start.6 = (bf16[2,8,1536]{2,1,0:T(8,128)(2,1)S(1)}, bf16[2,8,1536]{2,1,0:T(8,128)(2,1)S(1)}, u32[]{:S(2)}, u32[]{:S(2)}) collective-permute-start(bf16[2,8,1536]{2,1,0:T(8,128)(2,1)S(1)} %slice.78), channel_id=1, source_target_pairs={{0,12},{4,0},{8,4},{12,8},{16,28},{20,16},{24,20},{28,24},{32,44},... | collective-permute-start | bytes 147464 | tf_op jit(solution)/shard_map/ppermute | solution.py:39
  28.3 3.0 %collective-permute-start.16 = (bf16[4,32,1536]{2,1,0:T(8,128)(2,1)S(1)}, bf16[4,32,1536]{2,1,0:T(8,128)(2,1)S(1)}, u32[]{:S(2)}, u32[]{:S(2)}) collective-permute-start(bf16[4,32,1536]{2,1,0:T(8,128)(2,1)S(1)} %maximum_maximum_fusion.2), channel_id=1, source_target_pairs={{0,12},{4,0},{8,4},{12,8},{16,28},{20,16},{24,20},{28,24},{32,44},... | collective-permute-start | bytes 1179656 | tf_op jit(solution)/shard_map/ppermute | solution.py:39
  33.1 2.3 collective-permute-start.8
  36.5 7.0 %collective-permute-done.16 = bf16[4,32,1536]{2,1,0:T(8,128)(2,1)S(1)} collective-permute-done((bf16[4,32,1536]{2,1,0:T(8,128)(2,1)S(1)}, bf16[4,32,1536]{2,1,0:T(8,128)(2,1)S(1)}, u32[]{:S(2)}, u32[]{:S(2)}) %collective-permute-start.16) | collective-permute-done | bytes 393248 | tf_op jit(solution)/shard_map/ppermute | solution.py:39
  43.5 3.6 %collective-permute-start.18 = (bf16[2,32,1536]{2,1,0:T(8,128)(2,1)S(1)}, bf16[2,32,1536]{2,1,0:T(8,128)(2,1)S(1)}, u32[]{:S(2)}, u32[]{:S(2)}) collective-permute-start(bf16[2,32,1536]{2,1,0:T(8,128)(2,1)S(1)} %slice.85), channel_id=1, source_target_pairs={{0,12},{4,0},{8,4},{12,8},{16,28},{20,16},{24,20},{28,24},{32,44},... | collective-permute-start | bytes 589832 | tf_op jit(solution)/shard_map/ppermute | solution.py:39
  48.2 2.8 %collective-permute-start.10 = (bf16[2,32,1536]{2,1,0:T(8,128)(2,1)S(1)}, bf16[2,32,1536]{2,1,0:T(8,128)(2,1)S(1)}, u32[]{:S(2)}, u32[]{:S(2)}) collective-permute-start(bf16[2,32,1536]{2,1,0:T(8,128)(2,1)S(1)} %slice.80), channel_id=1, source_target_pairs={{0,48},{4,52},{8,56},{12,60},{16,0},{20,4},{24,8},{28,12},{32,16},... | collective-permute-start | bytes 589832 | tf_op jit(solution)/shard_map/ppermute | solution.py:39
  62.2 9.6 %all-to-all-start = ((bf16[16,8,384]{2,1,0:T(8,128)(2,1)}), bf16[16,8,384]{2,1,0:T(8,128)(2,1)S(1)}, u32[]{:S(2)}, u32[]{:S(2)}) async-start(bf16[16,8,384]{2,1,0:T(8,128)(2,1)} %bitcast.89), calls=%async_computation | async-start | bytes 196608 | tf_op jit(solution)/shard_map/all_to_all | solution.py:236
  76.5 35.6 %all-to-all-done = bf16[16,8,384]{2,1,0:T(8,128)(2,1)S(1)} async-done(((bf16[16,8,384]{2,1,0:T(8,128)(2,1)}), bf16[16,8,384]{2,1,0:T(8,128)(2,1)S(1)}, u32[]{:S(2)}, u32[]{:S(2)}) %all-to-all-start) | async-done | bytes 98336 | tf_op jit(solution)/shard_map/all_to_all | solution.py:236
  112.9 6.7 %all-to-all-start.1 = ((bf16[16,8,384]{2,1,0:T(8,128)(2,1)}), bf16[16,8,384]{2,1,0:T(8,128)(2,1)S(1)}, u32[]{:S(2)}, u32[]{:S(2)}) async-start(bf16[16,8,384]{2,1,0:T(8,128)(2,1)} %fusion.7), calls=%async_computation.1 | async-start | bytes 196608 | tf_op jit(solution)/shard_map/all_to_all | solution.py:240
  120.9 6.6 %all-to-all-done.1 = bf16[16,8,384]{2,1,0:T(8,128)(2,1)S(1)} async-done(((bf16[16,8,384]{2,1,0:T(8,128)(2,1)}), bf16[16,8,384]{2,1,0:T(8,128)(2,1)S(1)}, u32[]{:S(2)}, u32[]{:S(2)}) %all-to-all-start.1) | async-done | bytes 98336 | tf_op jit(solution)/shard_map/all_to_all | solution.py:240
  130.9 3.3 %fusion.59 = (f32[4,8]{1,0:T(4,128)S(1)}, f32[4,8,1536]{2,1,0:T(8,128)S(1)}) fusion(bf16[4,8,1536]{2,1,0:T(8,128)(2,1)S(1)} %reshape.105, bf16[1536,1536]{1,0:T(8,128)(2,1)} %param.19, f32[4,1536]{1,0:T(4,128)} %dynamic-slice_convert_fusion), kind=kOutput, calls=%fused_computation.102 | convolution fusion | flops 151093216 | bytes 5038208 | tf_op jit(solution)/shard_map/lfc,ce->lfe/dot_general | solution.py:244
  138.3 5.2 %collective-permute-done.19 = bf16[32,1536]{1,0:T(8,128)(2,1)S(1)} collective-permute-done((bf16[32,1536]{1,0:T(8,128)(2,1)S(1)}, bf16[32,1536]{1,0:T(8,128)(2,1)S(1)}, u32[]{:S(2)}, u32[]{:S(2)}) %collective-permute-start.19) | collective-permute-done | bytes 98336 | tf_op jit(solution)/shard_map/ppermute | solution.py:254
  144.8 13.4 %all-to-all-start.2 = ((bf16[16,32,1536]{2,1,0:T(8,128)(2,1)}), bf16[16,32,1536]{2,1,0:T(8,128)(2,1)}, u32[]{:S(2)}, u32[]{:S(2)}) async-start(bf16[16,32,1536]{2,1,0:T(8,128)(2,1)} %broadcast_in_dim.9), calls=%async_computation.2 | async-start | bytes 3145728 | tf_op jit(solution)/shard_map/all_to_all | solution.py:259
  165.2 16.0 %all-to-all-done.2 = bf16[16,32,1536]{2,1,0:T(8,128)(2,1)} async-done(((bf16[16,32,1536]{2,1,0:T(8,128)(2,1)}), bf16[16,32,1536]{2,1,0:T(8,128)(2,1)}, u32[]{:S(2)}, u32[]{:S(2)}) %all-to-all-start.2) | async-done | bytes 1572896 | tf_op jit(solution)/shard_map/all_to_all | solution.py:259
  181.1 4.2 %convolution_convert_fusion.1.k_ref.v_ref = bf16[512,1024]{1,0:T(8,128)(2,1)} fusion(bf16[512,1536]{1,0:T(8,128)(2,1)} %bitcast.18, bf16[1536,1024]{1,0:T(8,128)(2,1)S(1)} %constant_dynamic-update-slice_fusion), kind=kOutput, calls=%fused_computation.4 | convolution fusion | flops 1611137024 | bytes 5767168 | tf_op jit(solution)/shard_map/dot_general | solution.py:270
  185.4 26.5 %shard_map.149.q_ref = bf16[768,512]{1,0:T(8,128)(2,1)} custom-call(s32[4]{0:T(128)} %pad_add_fusion.where, bf16[768,8192]{1,0:T(8,128)(2,1)} %bitcast.91, bf16[1,8192]{1,0:T(2,128)(2,1)} %gain_ref.1, bf16[2048,512]{1,0:T(8,128)(2,1)} %bitcast.6.w0, bf16[2048,512]{1,0:T(8,128)(2,1)} %collective-permute-done.w1, bf16[2048,512]{1,0:T(8,128)(2,1)} %collective-permute-done.1.w2, ...), custom_call_target="tpu_custom_call" | custom-call | tf_op jit(solution)/shard_map/pallas_call | solution.py:91
  211.9 11.1 %shard_map.150 = (bf16[768,512]{1,0:T(8,128)(2,1)}, bf16[512,512]{1,0:T(8,128)(2,1)}, bf16[512,512]{1,0:T(8,128)(2,1)}) custom-call(s32[1]{0:T(128)} %bitcast.90.count, f32[1]{0:T(128)S(6)} %tanh.3.gate_ref, bf16[768,512]{1,0:T(8,128)(2,1)} %shard_map.149.q_ref, bf16[512,1024]{1,0:T(8,128)(2,1)} %convolution_convert_fusion.1.k_ref.v_ref, ...), custom_call_target="tpu_custom_call" | custom-call | tf_op jit(solution)/shard_map/pallas_call | solution.py:151
  223.0 3.0 %convolution_convert_fusion = bf16[512,1536]{1,0:T(8,128)(2,1)S(1)} fusion(bf16[1536,1024]{1,0:T(8,128)(2,1)S(1)} %constant_dynamic-update-slice_fusion, bf16[512,512]{1,0:T(8,128)(2,1)} %get-tuple-element.7, bf16[512,512]{1,0:T(8,128)(2,1)} %get-tuple-element.6), kind=kOutput, calls=%fused_computation.2 | convolution fusion | flops 1613496320 | bytes 5767168 | tf_op jit(solution)/shard_map/dot_general | solution.py:276
  226.1 26.1 %all_to_all.30 = bf16[16,32,1536]{2,1,0:T(8,128)(2,1)S(1)} all-to-all(bf16[16,32,1536]{2,1,0:T(8,128)(2,1)S(1)} %bitcast.92), channel_id=1, replica_groups=mesh['segment'=4,'mp'=16,'dp'=4] {'mp'}, dimensions={0} | all-to-all | bytes 3145728 | tf_op jit(solution)/shard_map/all_to_all | solution.py:279
  252.4 12.9 %all_to_all.31 = bf16[16,8,384]{2,1,0:T(8,128)(2,1)S(1)} all-to-all(bf16[16,8,384]{2,1,0:T(8,128)(2,1)S(1)} %bitcast.95), channel_id=1, replica_groups=mesh['segment'=4,'mp'=16,'dp'=4] {'segment','dp'}, dimensions={0} | all-to-all | bytes 196608 | tf_op jit(solution)/shard_map/all_to_all | solution.py:287
  265.5 10.9 %all_to_all.32 = bf16[16,8,384]{2,1,0:T(8,128)(2,1)S(1)} all-to-all(bf16[16,8,384]{2,1,0:T(8,128)(2,1)S(1)} %fusion.8), channel_id=1, replica_groups=mesh['segment'=4,'mp'=16,'dp'=4] {'segment','dp'}, dimensions={0} | all-to-all | bytes 196608 | tf_op jit(solution)/shard_map/all_to_all | solution.py:290
  (112 shorter events, 46.2 us)
Async XLA Ops:
  7.2 178.1 %all-gather.3.cloned.1.call-start = ((), (), s32[]{:S(2)}) async-start(), calls=%async_computation.6 | async-start | bytes 13369344 | tf_op jit(solution)/shard_map/all_gather | solution.py:201
  12.1 8.9 %collective-permute-start.12 = (bf16[4,8,1536]{2,1,0:T(8,128)(2,1)S(1)}, bf16[4,8,1536]{2,1,0:T(8,128)(2,1)S(1)}, u32[]{:S(2)}, u32[]{:S(2)}) collective-permute-start(bf16[4,8,1536]{2,1,0:T(8,128)(2,1)S(1)} %get-tuple-element.18), channel_id=1, source_target_pairs={{0,48},{4,52},{8,56},{12,60},{16,0},{20,4},{24,8},{28,12},{32,16},... | collective-permute-start | bytes 294920 | tf_op jit(solution)/shard_map/ppermute | solution.py:39
  15.8 8.3 %collective-permute-start.11 = (bf16[4,8,1536]{2,1,0:T(8,128)(2,1)S(1)}, bf16[4,8,1536]{2,1,0:T(8,128)(2,1)S(1)}, u32[]{:S(2)}, u32[]{:S(2)}) collective-permute-start(bf16[4,8,1536]{2,1,0:T(8,128)(2,1)S(1)} %get-tuple-element.18), channel_id=1, source_target_pairs={{0,16},{4,20},{8,24},{12,28},{16,32},{20,36},{24,40},{28,44},{32,4... | collective-permute-start | bytes 294920 | tf_op jit(solution)/shard_map/ppermute | solution.py:39
  15.8 8.4 %collective-permute-start.4 = (bf16[4,8,1536]{2,1,0:T(8,128)(2,1)S(1)}, bf16[4,8,1536]{2,1,0:T(8,128)(2,1)S(1)}, u32[]{:S(2)}, u32[]{:S(2)}) collective-permute-start(bf16[4,8,1536]{2,1,0:T(8,128)(2,1)S(1)} %get-tuple-element.17), channel_id=1, source_target_pairs={{0,12},{4,0},{8,4},{12,8},{16,28},{20,16},{24,20},{28,24},{32,44},... | collective-permute-start | bytes 294920 | tf_op jit(solution)/shard_map/ppermute | solution.py:39
  18.2 9.0 %collective-permute-start.3 = (bf16[4,8,1536]{2,1,0:T(8,128)(2,1)S(1)}, bf16[4,8,1536]{2,1,0:T(8,128)(2,1)S(1)}, u32[]{:S(2)}, u32[]{:S(2)}) collective-permute-start(bf16[4,8,1536]{2,1,0:T(8,128)(2,1)S(1)} %get-tuple-element.17), channel_id=1, source_target_pairs={{0,4},{4,8},{8,12},{12,0},{16,20},{20,24},{24,28},{28,16},{32,36},... | collective-permute-start | bytes 294920 | tf_op jit(solution)/shard_map/ppermute | solution.py:39
  18.2 167.1 %collective-permute-start = (bf16[2048,512]{1,0:T(8,128)(2,1)}, bf16[2048,512]{1,0:T(8,128)(2,1)}, u32[]{:S(2)}, u32[]{:S(2)}) collective-permute-start(bf16[2048,512]{1,0:T(8,128)(2,1)} %bitcast.6.w0), channel_id=1, source_target_pairs={{0,1},{1,0},{2,3},{3,2},{4,5},{5,4},{6,7},{7,6},{8,9},{9,8},{10,11... | collective-permute-start | bytes 6291464 | tf_op jit(solution)/shard_map/ppermute | solution.py:53
  21.0 6.3 %collective-permute-start.14 = (bf16[2,8,1536]{2,1,0:T(8,128)(2,1)S(1)}, bf16[2,8,1536]{2,1,0:T(8,128)(2,1)S(1)}, u32[]{:S(2)}, u32[]{:S(2)}) collective-permute-start(bf16[2,8,1536]{2,1,0:T(8,128)(2,1)S(1)} %slice.83), channel_id=1, source_target_pairs={{0,48},{4,52},{8,56},{12,60},{16,0},{20,4},{24,8},{28,12},{32,16},... | collective-permute-start | bytes 147464 | tf_op jit(solution)/shard_map/ppermute | solution.py:39
  24.2 7.2 %collective-permute-start.6 = (bf16[2,8,1536]{2,1,0:T(8,128)(2,1)S(1)}, bf16[2,8,1536]{2,1,0:T(8,128)(2,1)S(1)}, u32[]{:S(2)}, u32[]{:S(2)}) collective-permute-start(bf16[2,8,1536]{2,1,0:T(8,128)(2,1)S(1)} %slice.78), channel_id=1, source_target_pairs={{0,12},{4,0},{8,4},{12,8},{16,28},{20,16},{24,20},{28,24},{32,44},... | collective-permute-start | bytes 147464 | tf_op jit(solution)/shard_map/ppermute | solution.py:39
  27.2 5.9 %collective-permute-start.5 = (bf16[2,8,1536]{2,1,0:T(8,128)(2,1)S(1)}, bf16[2,8,1536]{2,1,0:T(8,128)(2,1)S(1)}, u32[]{:S(2)}, u32[]{:S(2)}) collective-permute-start(bf16[2,8,1536]{2,1,0:T(8,128)(2,1)S(1)} %slice.77), channel_id=1, source_target_pairs={{0,4},{4,8},{8,12},{12,0},{16,20},{20,24},{24,28},{28,16},{32,36},... | collective-permute-start | bytes 147464 | tf_op jit(solution)/shard_map/ppermute | solution.py:39
  28.3 15.2 %collective-permute-start.16 = (bf16[4,32,1536]{2,1,0:T(8,128)(2,1)S(1)}, bf16[4,32,1536]{2,1,0:T(8,128)(2,1)S(1)}, u32[]{:S(2)}, u32[]{:S(2)}) collective-permute-start(bf16[4,32,1536]{2,1,0:T(8,128)(2,1)S(1)} %maximum_maximum_fusion.2), channel_id=1, source_target_pairs={{0,12},{4,0},{8,4},{12,8},{16,28},{20,16},{24,20},{28,24},{32,44},... | collective-permute-start | bytes 1179656 | tf_op jit(solution)/shard_map/ppermute | solution.py:39
  31.3 16.8 %collective-permute-start.15 = (bf16[4,32,1536]{2,1,0:T(8,128)(2,1)S(1)}, bf16[4,32,1536]{2,1,0:T(8,128)(2,1)S(1)}, u32[]{:S(2)}, u32[]{:S(2)}) collective-permute-start(bf16[4,32,1536]{2,1,0:T(8,128)(2,1)S(1)} %maximum_maximum_fusion.2), channel_id=1, source_target_pairs={{0,4},{4,8},{8,12},{12,0},{16,20},{20,24},{24,28},{28,16},{32,36},... | collective-permute-start | bytes 1179656 | tf_op jit(solution)/shard_map/ppermute | solution.py:39
  33.1 15.0 %collective-permute-start.8 = (bf16[4,32,1536]{2,1,0:T(8,128)(2,1)S(1)}, bf16[4,32,1536]{2,1,0:T(8,128)(2,1)S(1)}, u32[]{:S(2)}, u32[]{:S(2)}) collective-permute-start(bf16[4,32,1536]{2,1,0:T(8,128)(2,1)S(1)} %maximum_maximum_fusion.1), channel_id=1, source_target_pairs={{0,48},{4,52},{8,56},{12,60},{16,0},{20,4},{24,8},{28,12},{32,16},... | collective-permute-start | bytes 1179656 | tf_op jit(solution)/shard_map/ppermute | solution.py:39
  35.5 15.6 %collective-permute-start.7 = (bf16[4,32,1536]{2,1,0:T(8,128)(2,1)S(1)}, bf16[4,32,1536]{2,1,0:T(8,128)(2,1)S(1)}, u32[]{:S(2)}, u32[]{:S(2)}) collective-permute-start(bf16[4,32,1536]{2,1,0:T(8,128)(2,1)S(1)} %maximum_maximum_fusion.1), channel_id=1, source_target_pairs={{0,16},{4,20},{8,24},{12,28},{16,32},{20,36},{24,40},{28,44},{32,4... | collective-permute-start | bytes 1179656 | tf_op jit(solution)/shard_map/ppermute | solution.py:39
  43.5 10.8 %collective-permute-start.18 = (bf16[2,32,1536]{2,1,0:T(8,128)(2,1)S(1)}, bf16[2,32,1536]{2,1,0:T(8,128)(2,1)S(1)}, u32[]{:S(2)}, u32[]{:S(2)}) collective-permute-start(bf16[2,32,1536]{2,1,0:T(8,128)(2,1)S(1)} %slice.85), channel_id=1, source_target_pairs={{0,12},{4,0},{8,4},{12,8},{16,28},{20,16},{24,20},{28,24},{32,44},... | collective-permute-start | bytes 589832 | tf_op jit(solution)/shard_map/ppermute | solution.py:39
  48.1 8.5 %collective-permute-start.17 = (bf16[2,32,1536]{2,1,0:T(8,128)(2,1)S(1)}, bf16[2,32,1536]{2,1,0:T(8,128)(2,1)S(1)}, u32[]{:S(2)}, u32[]{:S(2)}) collective-permute-start(bf16[2,32,1536]{2,1,0:T(8,128)(2,1)S(1)} %slice.84), channel_id=1, source_target_pairs={{0,4},{4,8},{8,12},{12,0},{16,20},{20,24},{24,28},{28,16},{32,36},... | collective-permute-start | bytes 589832 | tf_op jit(solution)/shard_map/ppermute | solution.py:39
  48.2 10.5 %collective-permute-start.10 = (bf16[2,32,1536]{2,1,0:T(8,128)(2,1)S(1)}, bf16[2,32,1536]{2,1,0:T(8,128)(2,1)S(1)}, u32[]{:S(2)}, u32[]{:S(2)}) collective-permute-start(bf16[2,32,1536]{2,1,0:T(8,128)(2,1)S(1)} %slice.80), channel_id=1, source_target_pairs={{0,48},{4,52},{8,56},{12,60},{16,0},{20,4},{24,8},{28,12},{32,16},... | collective-permute-start | bytes 589832 | tf_op jit(solution)/shard_map/ppermute | solution.py:39
  51.1 8.3 %collective-permute-start.9 = (bf16[2,32,1536]{2,1,0:T(8,128)(2,1)S(1)}, bf16[2,32,1536]{2,1,0:T(8,128)(2,1)S(1)}, u32[]{:S(2)}, u32[]{:S(2)}) collective-permute-start(bf16[2,32,1536]{2,1,0:T(8,128)(2,1)S(1)} %slice.79), channel_id=1, source_target_pairs={{0,16},{4,20},{8,24},{12,28},{16,32},{20,36},{24,40},{28,44},{32,4... | collective-permute-start | bytes 589832 | tf_op jit(solution)/shard_map/ppermute | solution.py:39
  54.3 80.1 %collective-permute-start.1 = (bf16[2048,512]{1,0:T(8,128)(2,1)}, bf16[2048,512]{1,0:T(8,128)(2,1)}, u32[]{:S(2)}, u32[]{:S(2)}) collective-permute-start(bf16[2048,512]{1,0:T(8,128)(2,1)} %bitcast.6.w0), channel_id=1, source_target_pairs={{0,2},{1,3},{2,0},{3,1},{4,6},{5,7},{6,4},{7,5},{8,10},{9,11},{10,... | collective-permute-start | bytes 6291464 | tf_op jit(solution)/shard_map/ppermute | solution.py:51
  62.2 49.8 %all-to-all-start = ((bf16[16,8,384]{2,1,0:T(8,128)(2,1)}), bf16[16,8,384]{2,1,0:T(8,128)(2,1)S(1)}, u32[]{:S(2)}, u32[]{:S(2)}) async-start(bf16[16,8,384]{2,1,0:T(8,128)(2,1)} %bitcast.89), calls=%async_computation | async-start | bytes 196608 | tf_op jit(solution)/shard_map/all_to_all | solution.py:236
  75.1 84.2 %collective-permute-start.21 = (bf16[384,1024]{1,0:T(8,128)(2,1)}, bf16[384,1024]{1,0:T(8,128)(2,1)}, u32[]{:S(2)}, u32[]{:S(2)}) collective-permute-start(bf16[384,1024]{1,0:T(8,128)(2,1)} %get-tuple-element.11), channel_id=1, source_target_pairs={{0,2},{1,3},{2,0},{3,1},{4,6},{5,7},{6,4},{7,5},{8,10},{9,11},{10,... | collective-permute-start | bytes 2359304 | tf_op jit(solution)/shard_map/ppermute | solution.py:51
  112.9 14.6 %all-to-all-start.1 = ((bf16[16,8,384]{2,1,0:T(8,128)(2,1)}), bf16[16,8,384]{2,1,0:T(8,128)(2,1)S(1)}, u32[]{:S(2)}, u32[]{:S(2)}) async-start(bf16[16,8,384]{2,1,0:T(8,128)(2,1)} %fusion.7), calls=%async_computation.1 | async-start | bytes 196608 | tf_op jit(solution)/shard_map/all_to_all | solution.py:240
  134.4 51.0 %collective-permute-start.2 = (bf16[2048,512]{1,0:T(8,128)(2,1)}, bf16[2048,512]{1,0:T(8,128)(2,1)}, u32[]{:S(2)}, u32[]{:S(2)}) collective-permute-start(bf16[2048,512]{1,0:T(8,128)(2,1)} %collective-permute-done.1.w2), channel_id=1, source_target_pairs={{0,1},{1,0},{2,3},{3,2},{4,5},{5,4},{6,7},{7,6},{8,9},{9,8},{10,11... | collective-permute-start | bytes 6291464 | tf_op jit(solution)/shard_map/ppermute | solution.py:53
  136.1 7.3 %collective-permute-start.19 = (bf16[32,1536]{1,0:T(8,128)(2,1)S(1)}, bf16[32,1536]{1,0:T(8,128)(2,1)S(1)}, u32[]{:S(2)}, u32[]{:S(2)}) collective-permute-start(bf16[32,1536]{1,0:T(8,128)(2,1)S(1)} %fusion.43), channel_id=1, source_target_pairs={{0,0},{4,1},{8,2},{12,3},{16,64},{20,65},{24,66},{28,67},{32,128},... | collective-permute-start | bytes 294920 | tf_op jit(solution)/shard_map/ppermute | solution.py:254
  144.8 36.3 %all-to-all-start.2 = ((bf16[16,32,1536]{2,1,0:T(8,128)(2,1)}), bf16[16,32,1536]{2,1,0:T(8,128)(2,1)}, u32[]{:S(2)}, u32[]{:S(2)}) async-start(bf16[16,32,1536]{2,1,0:T(8,128)(2,1)} %broadcast_in_dim.9), calls=%async_computation.2 | async-start | bytes 3145728 | tf_op jit(solution)/shard_map/all_to_all | solution.py:259
  (10 other events, 131.0 us)
Sparse Core Ops, SparseCore 0:
  10.4 118.5 all-gather.2

commit v2 on v1

--- a/solution.py
+++ b/solution.py
@@ -47,39 +47,91 @@
     return [value, left, right, far]
 
 
+def twice(k):
+    return ((k << 1) ^ ((k >> 3) * 19)) & 15
+
+
+def halved(k):
+    return (k >> 1) ^ ((k & 1) * 9)
+
+
 def dp_blocks(value):
     over_z = lax.ppermute(value, "dp", [(0, 2), (1, 3), (2, 0), (3, 1)])
     mate = [(0, 1), (1, 0), (2, 3), (3, 2)]
     return [value, lax.ppermute(value, "dp", mate), over_z, lax.ppermute(over_z, "dp", mate)]
 
 
-def query_kernel(where, text_ref, gain_ref, w0, w1, w2, w3, out_ref, normed):
+def norm_kernel(value_ref, gain_ref, out_ref):
+    out_ref[...] = layer_norm(value_ref[...], gain_ref[...]).astype(BF16)
+
+
+def norm_rows(value, gain):
+    return pl.pallas_call(
+        norm_kernel, out_shape=jax.ShapeDtypeStruct(value.shape, BF16)
+    )(value, gain)
+
+
+def latent_kernel(piece_ref, weight_ref, base_ref, gain_ref, out_ref):
+    width = RESAMPLE_HEAD_DIM
+    share = piece_ref.shape[1] // width
+    heads = weight_ref.shape[0] // width
+    owned = piece_ref.shape[0] // heads
+    piece = piece_ref[...].astype(F32)
+    total = base_ref[...]
+    for h in range(heads):
+        rows = piece[h * owned : (h + 1) * owned]
+        left = jnp.concatenate(
+            [rows[:, j * width : (j + 1) * width] for j in range(share)], axis=0
+        )
+        total = total + jnp.dot(
+            left.astype(BF16),
+            weight_ref[h * width : (h + 1) * width, :],
+            preferred_element_type=F32,
+        )
+    out_ref[...] = layer_norm(total, gain_ref[...]).astype(BF16)
+
+
+def latent_rows(piece, weight, base, gain):
+    return pl.pallas_call(
+        latent_kernel,
+        out_shape=jax.ShapeDtypeStruct(base.shape, BF16),
+        compiler_params=pltpu.CompilerParams(vmem_limit_bytes=VMEM_LIMIT),
+    )(piece, weight, base, gain)
+
+
+def query_kernel(where, text_ref, gain_ref, *rest):
+    weights, out_ref, mean_ref, scale_ref = rest[:-3], rest[-3], rest[-2], rest[-1]
     rows, depth = text_ref.shape
     width = 512
 
     @pl.loop(0, rows // 16)
     def _(step):
         at = pl.ds(pl.multiple_of(step * 16, 16), 16)
-        total = jnp.zeros((16, width), F32)
-        for c in range(depth // width):
-            total += text_ref[at, c * width : (c + 1) * width].astype(F32)
-        mean = jnp.sum(total, axis=1, keepdims=True) * (1.0 / depth)
-        total = jnp.zeros((16, width), F32)
-        for c in range(depth // width):
-            center = text_ref[at, c * width : (c + 1) * width].astype(F32) - mean
-            total += center * center
-        spread = jnp.sum(total, axis=1, keepdims=True) * (1.0 / depth)
-        scale = lax.rsqrt(spread + 1e-05)
-        for c in range(depth // width):
-            cols = slice(c * width, (c + 1) * width)
-            center = text_ref[at, cols].astype(F32) - mean
-            normed[at, cols] = (center * scale * gain_ref[:, cols].astype(F32)).astype(BF16)
-
+        first = text_ref[at, :width].astype(F32)
+        origin = jnp.sum(first, axis=1, keepdims=True) * (1.0 / width)
+        total = first - origin
+        square = total * total
+        for c in range(1, depth // width):
+            off = text_ref[at, c * width : (c + 1) * width].astype(F32) - origin
+            total += off
+            square += off * off
+        total = jnp.sum(total, axis=1, keepdims=True) * (1.0 / depth)
+        square = jnp.sum(square, axis=1, keepdims=True) * (1.0 / depth)
+        spread = jnp.maximum(square - total * total, 0.0)
+        mean_ref[at, :] = jnp.broadcast_to(origin + total, (16, 128))
+        scale_ref[at, :] = jnp.broadcast_to(lax.rsqrt(spread + 1e-05), (16, 128))
+
+    mean = mean_ref[:, :1]
+    scale = scale_ref[:, :1]
     total = None
-    for j, weight in enumerate((w0, w1, w2, w3)):
-        block = weight.shape[0]
-        cols = pl.ds(pl.multiple_of(where[j] * block, block), block)
-        term = jnp.dot(normed[:, cols], weight[...], preferred_element_type=F32)
+    parts = len(weights) // 4
+    block = weights[0].shape[0]
+    for j, weight in enumerate(weights):
+        at = (where[j // parts] * parts + j % parts) * block
+        cols = pl.ds(pl.multiple_of(at, block), block)
+        center = text_ref[:, cols].astype(F32) - mean
+        normed = (center * scale * gain_ref[:, cols].astype(F32)).astype(BF16)
+        term = jnp.dot(normed, weight[...], preferred_element_type=F32)
         total = term if total is None else total + term
     out_ref[...] = total.astype(BF16)
 
@@ -87,7 +139,7 @@
 def query_matmul(text, gain, weights, where):
     tokens, depth = text.shape
     cols = weights[0].shape[1]
-    rows = 128
+    rows = 256
     return pl.pallas_call(
         query_kernel,
         grid_spec=pltpu.PrefetchScalarGridSpec(
@@ -99,14 +151,14 @@
             ]
             + [pl.BlockSpec(w.shape, lambda i, w: (0, 0)) for w in weights],
             out_specs=pl.BlockSpec((rows, cols), lambda i, w: (i, 0)),
-            scratch_shapes=[pltpu.VMEM((rows, depth), BF16)],
+            scratch_shapes=[pltpu.VMEM((rows, 128), F32), pltpu.VMEM((rows, 128), F32)],
         ),
         out_shape=jax.ShapeDtypeStruct((tokens, cols), BF16),
         compiler_params=pltpu.CompilerParams(vmem_limit_bytes=VMEM_LIMIT),
     )(where, text, gain, *weights)
 
 
-def attend_kernel(count, gate_ref, q_ref, k_ref, v_ref, cot_ref, ctx_ref, dk_ref, dv_ref, acc_k, acc_v):
+def attend_kernel(count, order, gate_ref, q_ref, k_ref, v_ref, cot_ref, ctx_ref, dk_ref, dv_ref, acc_k, acc_v):
     tokens = q_ref.shape[0]
     keys = k_ref.shape[0]
     rows = 256
@@ -139,25 +191,29 @@
         else:
             acc_k[...] += grad_k
             acc_v[...] += grad_v
-    dk_ref[...] = acc_k[...].astype(BF16)
-    dv_ref[...] = acc_v[...].astype(BF16)
-
-
-def attention(query, pairs, cot, count, gate):
+    chunks = order.shape[0]
+    size = keys // chunks
+    for j in range(chunks):
+        to = pl.ds(pl.multiple_of(order[j] * size, size), size)
+        dk_ref[to, :] = acc_k[j * size : (j + 1) * size, :].astype(BF16)
+        dv_ref[to, :] = acc_v[j * size : (j + 1) * size, :].astype(BF16)
+
+
+def attention(query, pairs, cot, count, order, gate):
     tokens, cols = query.shape
     keys = pairs.shape[0]
     heads = cols // HD
-    head = lambda n: pl.BlockSpec((n, HD), lambda h, c: (0, h))
+    head = lambda n: pl.BlockSpec((n, HD), lambda h, c, o: (0, h))
     return pl.pallas_call(
         attend_kernel,
         grid_spec=pltpu.PrefetchScalarGridSpec(
-            num_scalar_prefetch=1,
+            num_scalar_prefetch=2,
             grid=(heads,),
             in_specs=[
                 pl.BlockSpec(memory_space=pltpu.SMEM),
                 head(tokens),
                 head(keys),
-                pl.BlockSpec((keys, HD), lambda h, c: (0, h + heads)),
+                pl.BlockSpec((keys, HD), lambda h, c, o: (0, h + heads)),
                 head(tokens),
             ],
             out_specs=[head(tokens), head(keys), head(keys)],
@@ -169,7 +225,7 @@
             jax.ShapeDtypeStruct((keys, cols), BF16),
         ],
         compiler_params=pltpu.CompilerParams(vmem_limit_bytes=VMEM_LIMIT),
-    )(count, gate, query, pairs, pairs, cot)
+    )(count, order, gate, query, pairs, pairs, cot)
 
 
 def per_device(
@@ -198,13 +254,16 @@
     width = res_query.shape[1]
     res_scale = 1.0 / math.sqrt(RESAMPLE_HEAD_DIM)
 
-    whole_text = lax.all_gather(text[0, 0], "mp", axis=1, tiled=True)
-    media = layer_norm(frames, norm_gains[0]).astype(BF16)
+    split = (text.shape[2] // 3) * 2
+    text_first = lax.all_gather(text[0, 0, :split], "mp", axis=1, tiled=True)
+    text_last = lax.all_gather(text[0, 0, split:], "mp", axis=1, tiled=True)
+    media = norm_rows(frames.reshape(-1, E), norm_gains[:1]).reshape(frames.shape)
     half = owned // 2
     ring_x = [ring(media[:half], "x"), ring(media[half:], "y")]
-    query_blocks = dp_blocks(w_query[0])
     kv_local = jnp.concatenate([w_kv[0, :, 0], w_kv[0, :, 1]], axis=1)
     kv_blocks = dp_blocks(kv_local)
+    depth = w_query.shape[1] // 2
+    query_low = dp_blocks(w_query[0, :depth])
 
     lat_norm = layer_norm(latent_init, norm_gains[1]).astype(BF16)
     res_pair = jnp.concatenate([res_kv[:, 0], res_kv[:, 1]], axis=1)
@@ -234,34 +293,42 @@
 
     piece = res_context.reshape(owned, groups, share * width).swapaxes(0, 1)
     piece = lax.all_to_all(piece, GROUP, 0, 0, tiled=True).reshape(slots, share * width)
+    piece, query_rest = lax.optimization_barrier((piece, w_query[0, depth:]))
+    query_high = dp_blocks(query_rest)
     slot_ids = jnp.arange(slots, dtype=jnp.int32)
-    to_dest = (frame_dest[None, :] == slot_ids[:, None]).astype(BF16)
+    target = (twice(group) ^ (slot_ids // owned)) * owned + slot_ids % owned
+    to_dest = (frame_dest[None, :] == target[:, None]).astype(BF16)
     piece = jnp.dot(to_dest, piece, preferred_element_type=F32).astype(BF16)
     piece = lax.all_to_all(
         piece.reshape(mp_count, owned, share * width), "mp", 0, 0, tiled=True
     )
-    rows = piece.reshape(mp_count, owned, share, width).transpose(2, 1, 0, 3)
-    update = jnp.einsum(
-        "lfc,ce->lfe", rows.reshape(share, owned, E), res_out, preferred_element_type=F32
-    )
     base_rows = lax.dynamic_slice_in_dim(latent_init, group * share, share, 0).astype(F32)
-    latents = layer_norm(base_rows[:, None, :] + update, norm_gains[2]).astype(BF16)
+    latents = latent_rows(
+        piece.reshape(slots, share * width),
+        res_out,
+        jnp.repeat(base_rows, owned, axis=0),
+        norm_gains[2:],
+    )
     dp_count = lax.axis_size("dp")
 
     def place(g, m):
         return (g // dp_count * mp_count + m) * dp_count + g % dp_count
 
     mine = lax.ppermute(
-        latents.reshape(share * owned, E),
+        latents,
         ("segment", "mp", "dp"),
-        [(place(g, m), place(m, g)) for g in range(groups) for m in range(mp_count)],
+        [(place(g, m), place(twice(g) ^ m, m)) for g in range(groups) for m in range(mp_count)],
     )
     dest = lax.all_to_all(
         jnp.broadcast_to(mine, (mp_count,) + mine.shape), "mp", 0, 0, tiled=True
     ).reshape(LAT * owned, E)
+    order = halved(group ^ jnp.arange(mp_count, dtype=jnp.int32))
 
     where = jnp.stack([dp, dp ^ 1, dp ^ 2, dp ^ 3]).astype(jnp.int32)
-    query = query_matmul(whole_text, text_gain, query_blocks, where)
+    query_blocks = [w for both in zip(query_low, query_high) for w in both]
+    query_first = query_matmul(text_first, text_gain, query_blocks, where)
+    dest, query_first = lax.optimization_barrier((dest, query_first))
+    query_last = query_matmul(text_last, text_gain, query_blocks, where)
     full_kv = jnp.zeros((E, kv_local.shape[1]), BF16)
     for j, block in enumerate(kv_blocks):
         full_kv = lax.dynamic_update_slice_in_dim(
@@ -269,7 +336,12 @@
         )
     pairs = jnp.dot(dest, full_kv, preferred_element_type=F32).astype(BF16)
     context, grad_k, grad_v = attention(
-        query, pairs, cotangent[0, 0], frame_counts[0], jnp.tanh(xgate)
+        jnp.concatenate([query_first, query_last], axis=0),
+        pairs,
+        cotangent[0, 0],
+        frame_counts[0],
+        order,
+        jnp.tanh(xgate),
     )
 
     grad = jnp.concatenate([grad_k, grad_v], axis=1)

time: 285 us -> 288 us (1.011)
  waiting for transfers between devices: 79.3 us -> 57 us
  Pallas kernels: 37.7 us -> 50.3 us
  local copies, waits for them, and re-layouts: 12.6 us -> 23.2 us
  starting transfers between devices: 63.8 us -> 53.5 us
  matrix products: 15.6 us -> 23 us
  blocking collectives: 49.9 us -> 54.6 us
    all_gather x1 -> x2, waiting for transfers between devices: 0.01 us -> 16.4 us  [the longest x1 16.3 us: per_device(): text_first = lax.all_gather(text[0, 0, :split], 'mp', axis=1, tiled=True)]
    all_to_all x1, waiting for transfers between devices: 16 us -> 0.01 us  [per_device(): lax.all_to_all(jnp.broadcast_to(mine, (mp_count,) + mine.shape), 'mp', 0,...]
    ppermute x16, waiting for transfers between devices: 15.3 us -> 3.04 us  [shift(): return lax.ppermute(value, 'mp', pairs)]
    all_to_all x1, waiting for transfers between devices: 35.6 us -> 24.4 us  [per_device(): lax.all_to_all(piece, GROUP, 0, 0, tiled=True).reshape(slots, share * width)]
    all_to_all x1, starting transfers between devices: 13.4 us -> 4.41 us  [per_device(): lax.all_to_all(jnp.broadcast_to(mine, (mp_count,) + mine.shape), 'mp', 0,...]
    pallas_call x0 -> x2, Pallas kernels: none -> 5.88 us  [the longest x1 4.04 us: latent_rows(): pl.pallas_call(latent_kernel, out_shape=jax.ShapeDtypeStruct(base.shape,...]
    pallas_call x1 -> x2, Pallas kernels: 26.5 us -> 32.3 us  [query_matmul(): pl.pallas_call(query_kernel, grid_spec=pltpu.PrefetchScalarGridSpec(num_s...]
    dot_general x8, matrix products: 2.63 us -> 7.79 us  [per_device(): jnp.einsum('fpe,ec->fpc', block, res_pair, preferred_element_type=F32)]
  transfers between devices with their start and end apart: 27 -> 31, of which waited for: 12 -> 6; matrix products, arithmetic and copies ran while one was open for 11% -> 15% of each run, Pallas kernels for 0% -> 13%
where the time goes in v2:
time: 288 us; the launch traced here: 287 us
  waiting for transfers between devices  57 us (20%)
  blocking collectives  54.6 us (19%)
  starting transfers between devices  53.5 us (19%)
  Pallas kernels  50.3 us (17%)
  local copies, waits for them, and re-layouts  23.2 us (8%)
  matrix products  23 us (8%)
  between operations  16.1 us (6%)
  other arithmetic  9.22 us (3%)
    pallas_call x2, Pallas kernels, query_matmul(): pl.pallas_call(query_kernel, grid_spec=pltpu.PrefetchScalarGridSpec(num_s...  32.3 us
    all_to_all x1, blocking collectives, per_device(): lax.all_to_all(part.reshape(mp_count, share * owned, E), 'mp', 0, 0, tile...  27 us
    all_to_all x1, waiting for transfers between devices, per_device(): lax.all_to_all(piece, GROUP, 0, 0, tiled=True).reshape(slots, share * width)  24.4 us
    ppermute x16, starting transfers between devices, shift(): return lax.ppermute(value, 'mp', pairs)  23.1 us
    all_to_all x1, blocking collectives, per_device(): lax.all_to_all(send, GROUP, 0, 0, tiled=True).reshape(slots, E // cut)  16.7 us
    all_gather x1, waiting for transfers between devices, per_device(): text_first = lax.all_gather(text[0, 0, :split], 'mp', axis=1, tiled=True)  16.3 us
    pallas_call x1, Pallas kernels, attention(): pl.pallas_call(attend_kernel, grid_spec=pltpu.PrefetchScalarGridSpec(num_...  12.1 us
    all_to_all x1, starting transfers between devices, per_device(): lax.all_to_all(piece, GROUP, 0, 0, tiled=True).reshape(slots, share * width)  10.9 us
  transfers between devices with their start and end apart: 31, of which 6 were waited for; matrix products, arithmetic and copies ran while one was open for 15% of the time, Pallas kernels for 13%

profile of v2, /device:TPU:1, one launch (start us, length us, event | category | flops | bytes accessed | tf_op | source)
XLA Modules:
  0.0 286.9 jit_solution(16107106122518421792)
XLA Ops:
  23.5 3.5 %collective-permute-start.23 = (bf16[384,1024]{1,0:T(8,128)(2,1)}, bf16[384,1024]{1,0:T(8,128)(2,1)}, u32[]{:S(2)}, u32[]{:S(2)}) collective-permute-start(bf16[384,1024]{1,0:T(8,128)(2,1)} %get-tuple-element.18), channel_id=1, source_target_pairs={{0,1},{1,0},{2,3},{3,2},{4,5},{5,4},{6,7},{7,6},{8,9},{9,8},{10,11... | collective-permute-start | bytes 2359304 | tf_op jit(solution)/shard_map/ppermute | solution.py:61
  28.7 2.7 collective-permute-start.3
  31.6 2.7 collective-permute-start.11
  38.2 2.7 collective-permute-start.13
  43.8 3.0 %collective-permute-done.4 = bf16[4,32,1536]{2,1,0:T(8,128)(2,1)} collective-permute-done((bf16[4,32,1536]{2,1,0:T(8,128)(2,1)S(1)}, bf16[4,32,1536]{2,1,0:T(8,128)(2,1)}, u32[]{:S(2)}, u32[]{:S(2)}) %collective-permute-start.4) | collective-permute-done | bytes 393248 | tf_op jit(solution)/shard_map/ppermute | solution.py:39
  48.8 2.7 collective-permute-start.7
  53.6 2.7 collective-permute-start.15
  72.9 10.9 %all-to-all-start = ((bf16[16,8,384]{2,1,0:T(8,128)(2,1)}), bf16[16,8,384]{2,1,0:T(8,128)(2,1)S(1)}, u32[]{:S(2)}, u32[]{:S(2)}) async-start(bf16[16,8,384]{2,1,0:T(8,128)(2,1)} %bitcast.92), calls=%async_computation | async-start | bytes 196608 | tf_op jit(solution)/shard_map/all_to_all | solution.py:295
  85.2 24.4 %all-to-all-done = bf16[16,8,384]{2,1,0:T(8,128)(2,1)S(1)} async-done(((bf16[16,8,384]{2,1,0:T(8,128)(2,1)}), bf16[16,8,384]{2,1,0:T(8,128)(2,1)S(1)}, u32[]{:S(2)}, u32[]{:S(2)}) %all-to-all-start) | async-done | bytes 98336 | tf_op jit(solution)/shard_map/all_to_all | solution.py:295
  111.7 3.5 %all-to-all-start.1 = ((bf16[16,8,384]{2,1,0:T(8,128)(2,1)}), bf16[16,8,384]{2,1,0:T(8,128)(2,1)S(1)}, u32[]{:S(2)}, u32[]{:S(2)}) async-start(bf16[16,8,384]{2,1,0:T(8,128)(2,1)} %fusion.2), calls=%async_computation.1 | async-start | bytes 196608 | tf_op jit(solution)/shard_map/all_to_all | solution.py:302
  116.6 5.2 %all-to-all-done.1 = bf16[16,8,384]{2,1,0:T(8,128)(2,1)S(1)} async-done(((bf16[16,8,384]{2,1,0:T(8,128)(2,1)}), bf16[16,8,384]{2,1,0:T(8,128)(2,1)S(1)}, u32[]{:S(2)}, u32[]{:S(2)}) %all-to-all-start.1) | async-done | bytes 98336 | tf_op jit(solution)/shard_map/all_to_all | solution.py:302
  122.4 4.0 %shard_map.150 = bf16[32,1536]{1,0:T(8,128)(2,1)} custom-call(bf16[128,384]{1,0:T(8,128)(2,1)} %bitcast.95, bf16[1536,1536]{1,0:T(8,128)(2,1)} %weight_ref.1, f32[32,1536]{1,0:T(8,128)} %broadcast_bitcast_fusion.base_ref, bf16[1,1536]{1,0:T(2,128)(2,1)} %get-tuple-element.26.gain_ref), custom_call_target="tpu_custom_call" | custom-call | tf_op jit(solution)/shard_map/pallas_call | solution.py:95
  126.5 3.9 %collective-permute-start.16 = (bf16[32,1536]{1,0:T(8,128)(2,1)}, bf16[32,1536]{1,0:T(8,128)(2,1)S(1)}, u32[]{:S(2)}, u32[]{:S(2)}) collective-permute-start(bf16[32,1536]{1,0:T(8,128)(2,1)} %shard_map.150), channel_id=1, source_target_pairs={{0,0},{4,5},{8,10},{12,15},{16,80},{20,85},{24,90},{28,95},{32,160... | collective-permute-start | bytes 294920 | tf_op jit(solution)/shard_map/ppermute | solution.py:317
  130.4 7.8 %collective-permute-done.16 = bf16[32,1536]{1,0:T(8,128)(2,1)S(1)} collective-permute-done((bf16[32,1536]{1,0:T(8,128)(2,1)}, bf16[32,1536]{1,0:T(8,128)(2,1)S(1)}, u32[]{:S(2)}, u32[]{:S(2)}) %collective-permute-start.16) | collective-permute-done | bytes 98336 | tf_op jit(solution)/shard_map/ppermute | solution.py:317
  139.4 4.4 %all-to-all-start.2 = ((bf16[16,32,1536]{2,1,0:T(8,128)(2,1)}), bf16[16,32,1536]{2,1,0:T(8,128)(2,1)}, u32[]{:S(2)}, u32[]{:S(2)}) async-start(bf16[16,32,1536]{2,1,0:T(8,128)(2,1)} %broadcast_in_dim.12), calls=%async_computation.2 | async-start | bytes 3145728 | tf_op jit(solution)/shard_map/all_to_all | solution.py:322
  154.3 12.7 %shard_map.152 = bf16[256,512]{1,0:T(8,128)(2,1)} custom-call(s32[4]{0:T(128)} %pad_add_fusion.where, bf16[256,8192]{1,0:T(8,128)(2,1)} %bitcast.88, bf16[1,8192]{1,0:T(2,128)(2,1)} %gain_ref.3, bf16[1024,512]{1,0:T(8,128)(2,1)} %copy-done.2, bf16[1024,512]{1,0:T(8,128)(2,1)} %copy-done.1, bf16[1024,512]{1,0:T(8,128)(2,1)} %collective-permute-done.17.rest_2_, ...), custom_call_target="tpu_custom_call" | custom-call | tf_op jit(solution)/shard_map/pallas_call | solution.py:143
  167.0 16.3 %all-gather.5.cloned.1.call-done = bf16[1,1,512,8192]{3,2,1,0:T(8,128)(2,1)} async-done(((bf16[1,1,512,512]{3,2,1,0:T(8,128)(2,1)}), bf16[1,1,512,8192]{3,2,1,0:T(8,128)(2,1)}) %all-gather.5.cloned.1.call-update) | async-done | bytes 8388624 | tf_op jit(solution)/shard_map/all_gather | solution.py:258
  183.3 19.6 %shard_map.151 = bf16[512,512]{1,0:T(8,128)(2,1)} custom-call(s32[4]{0:T(128)} %pad_add_fusion.where, bf16[512,8192]{1,0:T(8,128)(2,1)} %bitcast.87, bf16[1,8192]{1,0:T(2,128)(2,1)} %gain_ref.3, bf16[1024,512]{1,0:T(8,128)(2,1)} %copy-done.2, bf16[1024,512]{1,0:T(8,128)(2,1)} %copy-done.1, bf16[1024,512]{1,0:T(8,128)(2,1)} %collective-permute-done.17.rest_2_, ...), custom_call_target="tpu_custom_call" | custom-call | tf_op jit(solution)/shard_map/pallas_call | solution.py:143
  203.0 5.2 %convolution_convert_fusion.1.k_ref.v_ref = bf16[512,1024]{1,0:T(8,128)(2,1)} fusion(bf16[512,1536]{1,0:T(8,128)(2,1)} %bitcast.15, bf16[1536,1024]{1,0:T(8,128)(2,1)} %constant_dynamic-update-slice_fusion), kind=kOutput, calls=%fused_computation.1 | convolution fusion | flops 1611137024 | bytes 5767168 | tf_op jit(solution)/shard_map/dot_general | solution.py:337
  209.2 12.1 %shard_map.153 = (bf16[768,512]{1,0:T(8,128)(2,1)}, bf16[512,512]{1,0:T(8,128)(2,1)}, bf16[512,512]{1,0:T(8,128)(2,1)}) custom-call(s32[1]{0:T(128)} %bitcast.86.count, s32[16]{0:T(128)} %multiply_xor_fusion.order, f32[1]{0:T(128)S(6)} %tanh.3.gate_ref, bf16[768,512]{1,0:T(8,128)(2,1)} %pad_maximum_fusion.q_ref, ...), custom_call_target="tpu_custom_call" | custom-call | tf_op jit(solution)/shard_map/pallas_call | solution.py:207
  221.3 3.0 %convolution_convert_fusion = bf16[512,1536]{1,0:T(8,128)(2,1)S(1)} fusion(bf16[1536,1024]{1,0:T(8,128)(2,1)S(1)} %copy-done.6, bf16[512,512]{1,0:T(8,128)(2,1)} %get-tuple-element.15, bf16[512,512]{1,0:T(8,128)(2,1)} %get-tuple-element.14), kind=kOutput, calls=%fused_computation | convolution fusion | flops 1613496320 | bytes 5767168 | tf_op jit(solution)/shard_map/dot_general | solution.py:348
  224.3 27.0 %all_to_all.30 = bf16[16,32,1536]{2,1,0:T(8,128)(2,1)S(1)} all-to-all(bf16[16,32,1536]{2,1,0:T(8,128)(2,1)S(1)} %bitcast.89), channel_id=1, replica_groups=mesh['segment'=4,'mp'=16,'dp'=4] {'mp'}, dimensions={0} | all-to-all | bytes 3145728 | tf_op jit(solution)/shard_map/all_to_all | solution.py:351
  251.6 16.7 %all_to_all.31 = bf16[16,8,384]{2,1,0:T(8,128)(2,1)S(1)} all-to-all(bf16[16,8,384]{2,1,0:T(8,128)(2,1)S(1)} %bitcast.93), channel_id=1, replica_groups=mesh['segment'=4,'mp'=16,'dp'=4] {'segment','dp'}, dimensions={0} | all-to-all | bytes 196608 | tf_op jit(solution)/shard_map/all_to_all | solution.py:359
  268.4 10.9 %all_to_all.32 = bf16[16,8,384]{2,1,0:T(8,128)(2,1)S(1)} all-to-all(bf16[16,8,384]{2,1,0:T(8,128)(2,1)S(1)} %fusion.3), channel_id=1, replica_groups=mesh['segment'=4,'mp'=16,'dp'=4] {'segment','dp'}, dimensions={0} | all-to-all | bytes 196608 | tf_op jit(solution)/shard_map/all_to_all | solution.py:362
  (165 shorter events, 63.1 us)
Async XLA Ops:
  7.2 147.1 %all-gather.7.cloned.1.call-start = ((), (), s32[]{:S(2)}) async-start(), calls=%async_computation.7 | async-start | bytes 4456448 | tf_op jit(solution)/shard_map/all_gather | solution.py:259
  9.0 174.3 %all-gather.5.cloned.1.call-start = ((), (), s32[]{:S(2)}) async-start(), calls=%async_computation.6 | async-start | bytes 8912896 | tf_op jit(solution)/shard_map/all_gather | solution.py:258
  14.4 14.1 %collective-permute-start = (bf16[4,8,1536]{2,1,0:T(8,128)(2,1)S(1)}, bf16[4,8,1536]{2,1,0:T(8,128)(2,1)S(1)}, u32[]{:S(2)}, u32[]{:S(2)}) collective-permute-start(bf16[4,8,1536]{2,1,0:T(8,128)(2,1)S(1)} %get-tuple-element.24), channel_id=1, source_target_pairs={{0,4},{4,8},{8,12},{12,0},{16,20},{20,24},{24,28},{28,16},{32,36},... | collective-permute-start | bytes 294920 | tf_op jit(solution)/shard_map/ppermute | solution.py:39
  16.5 12.1 %collective-permute-start.1 = (bf16[4,8,1536]{2,1,0:T(8,128)(2,1)S(1)}, bf16[4,8,1536]{2,1,0:T(8,128)(2,1)S(1)}, u32[]{:S(2)}, u32[]{:S(2)}) collective-permute-start(bf16[4,8,1536]{2,1,0:T(8,128)(2,1)S(1)} %get-tuple-element.24), channel_id=1, source_target_pairs={{0,12},{4,0},{8,4},{12,8},{16,28},{20,16},{24,20},{28,24},{32,44},... | collective-permute-start | bytes 294920 | tf_op jit(solution)/shard_map/ppermute | solution.py:39
  17.9 13.5 %collective-permute-start.8 = (bf16[4,8,1536]{2,1,0:T(8,128)(2,1)S(1)}, bf16[4,8,1536]{2,1,0:T(8,128)(2,1)S(1)}, u32[]{:S(2)}, u32[]{:S(2)}) collective-permute-start(bf16[4,8,1536]{2,1,0:T(8,128)(2,1)S(1)} %get-tuple-element.25), channel_id=1, source_target_pairs={{0,16},{4,20},{8,24},{12,28},{16,32},{20,36},{24,40},{28,44},{32,4... | collective-permute-start | bytes 294920 | tf_op jit(solution)/shard_map/ppermute | solution.py:39
  19.3 12.3 %collective-permute-start.9 = (bf16[4,8,1536]{2,1,0:T(8,128)(2,1)S(1)}, bf16[4,8,1536]{2,1,0:T(8,128)(2,1)S(1)}, u32[]{:S(2)}, u32[]{:S(2)}) collective-permute-start(bf16[4,8,1536]{2,1,0:T(8,128)(2,1)S(1)} %get-tuple-element.25), channel_id=1, source_target_pairs={{0,48},{4,52},{8,56},{12,60},{16,0},{20,4},{24,8},{28,12},{32,16},... | collective-permute-start | bytes 294920 | tf_op jit(solution)/shard_map/ppermute | solution.py:39
  23.5 120.5 %collective-permute-start.23 = (bf16[384,1024]{1,0:T(8,128)(2,1)}, bf16[384,1024]{1,0:T(8,128)(2,1)}, u32[]{:S(2)}, u32[]{:S(2)}) collective-permute-start(bf16[384,1024]{1,0:T(8,128)(2,1)} %get-tuple-element.18), channel_id=1, source_target_pairs={{0,1},{1,0},{2,3},{3,2},{4,5},{5,4},{6,7},{7,6},{8,9},{9,8},{10,11... | collective-permute-start | bytes 2359304 | tf_op jit(solution)/shard_map/ppermute | solution.py:61
  34.3 12.5 %collective-permute-start.4 = (bf16[4,32,1536]{2,1,0:T(8,128)(2,1)S(1)}, bf16[4,32,1536]{2,1,0:T(8,128)(2,1)}, u32[]{:S(2)}, u32[]{:S(2)}) collective-permute-start(bf16[4,32,1536]{2,1,0:T(8,128)(2,1)S(1)} %maximum_maximum_fusion.1), channel_id=1, source_target_pairs={{0,16},{4,20},{8,24},{12,28},{16,32},{20,36},{24,40},{28,44},{32,4... | collective-permute-start | bytes 1179656 | tf_op jit(solution)/shard_map/ppermute | solution.py:39
  34.4 13.4 %collective-permute-start.5 = (bf16[4,32,1536]{2,1,0:T(8,128)(2,1)S(1)}, bf16[4,32,1536]{2,1,0:T(8,128)(2,1)}, u32[]{:S(2)}, u32[]{:S(2)}) collective-permute-start(bf16[4,32,1536]{2,1,0:T(8,128)(2,1)S(1)} %maximum_maximum_fusion.1), channel_id=1, source_target_pairs={{0,48},{4,52},{8,56},{12,60},{16,0},{20,4},{24,8},{28,12},{32,16},... | collective-permute-start | bytes 1179656 | tf_op jit(solution)/shard_map/ppermute | solution.py:39
  38.1 13.4 %collective-permute-start.12 = (bf16[4,32,1536]{2,1,0:T(8,128)(2,1)S(1)}, bf16[4,32,1536]{2,1,0:T(8,128)(2,1)}, u32[]{:S(2)}, u32[]{:S(2)}) collective-permute-start(bf16[4,32,1536]{2,1,0:T(8,128)(2,1)S(1)} %maximum_maximum_fusion.2), channel_id=1, source_target_pairs={{0,4},{4,8},{8,12},{12,0},{16,20},{20,24},{24,28},{28,16},{32,36},... | collective-permute-start | bytes 1179656 | tf_op jit(solution)/shard_map/ppermute | solution.py:39
  38.2 14.4 %collective-permute-start.13 = (bf16[4,32,1536]{2,1,0:T(8,128)(2,1)S(1)}, bf16[4,32,1536]{2,1,0:T(8,128)(2,1)}, u32[]{:S(2)}, u32[]{:S(2)}) collective-permute-start(bf16[4,32,1536]{2,1,0:T(8,128)(2,1)S(1)} %maximum_maximum_fusion.2), channel_id=1, source_target_pairs={{0,12},{4,0},{8,4},{12,8},{16,28},{20,16},{24,20},{28,24},{32,44},... | collective-permute-start | bytes 1179656 | tf_op jit(solution)/shard_map/ppermute | solution.py:39
  47.8 13.8 %collective-permute-start.6 = (bf16[2,32,1536]{2,1,0:T(8,128)(2,1)S(1)}, bf16[2,32,1536]{2,1,0:T(8,128)(2,1)S(1)}, u32[]{:S(2)}, u32[]{:S(2)}) collective-permute-start(bf16[2,32,1536]{2,1,0:T(8,128)(2,1)S(1)} %slice.103), channel_id=1, source_target_pairs={{0,16},{4,20},{8,24},{12,28},{16,32},{20,36},{24,40},{28,44},{32,4... | collective-permute-start | bytes 589832 | tf_op jit(solution)/shard_map/ppermute | solution.py:39
  48.8 14.0 %collective-permute-start.7 = (bf16[2,32,1536]{2,1,0:T(8,128)(2,1)S(1)}, bf16[2,32,1536]{2,1,0:T(8,128)(2,1)S(1)}, u32[]{:S(2)}, u32[]{:S(2)}) collective-permute-start(bf16[2,32,1536]{2,1,0:T(8,128)(2,1)S(1)} %slice.104), channel_id=1, source_target_pairs={{0,48},{4,52},{8,56},{12,60},{16,0},{20,4},{24,8},{28,12},{32,16},... | collective-permute-start | bytes 589832 | tf_op jit(solution)/shard_map/ppermute | solution.py:39
  52.5 11.0 %collective-permute-start.14 = (bf16[2,32,1536]{2,1,0:T(8,128)(2,1)S(1)}, bf16[2,32,1536]{2,1,0:T(8,128)(2,1)S(1)}, u32[]{:S(2)}, u32[]{:S(2)}) collective-permute-start(bf16[2,32,1536]{2,1,0:T(8,128)(2,1)S(1)} %slice.108), channel_id=1, source_target_pairs={{0,4},{4,8},{8,12},{12,0},{16,20},{20,24},{24,28},{28,16},{32,36},... | collective-permute-start | bytes 589832 | tf_op jit(solution)/shard_map/ppermute | solution.py:39
  53.6 10.0 %collective-permute-start.15 = (bf16[2,32,1536]{2,1,0:T(8,128)(2,1)S(1)}, bf16[2,32,1536]{2,1,0:T(8,128)(2,1)S(1)}, u32[]{:S(2)}, u32[]{:S(2)}) collective-permute-start(bf16[2,32,1536]{2,1,0:T(8,128)(2,1)S(1)} %slice.109), channel_id=1, source_target_pairs={{0,12},{4,0},{8,4},{12,8},{16,28},{20,16},{24,20},{28,24},{32,44},... | collective-permute-start | bytes 589832 | tf_op jit(solution)/shard_map/ppermute | solution.py:39
  61.6 83.4 %collective-permute-start.24 = (bf16[384,1024]{1,0:T(8,128)(2,1)}, bf16[384,1024]{1,0:T(8,128)(2,1)}, u32[]{:S(2)}, u32[]{:S(2)}) collective-permute-start(bf16[384,1024]{1,0:T(8,128)(2,1)} %get-tuple-element.18), channel_id=1, source_target_pairs={{0,2},{1,3},{2,0},{3,1},{4,6},{5,7},{6,4},{7,5},{8,10},{9,11},{10,... | collective-permute-start | bytes 2359304 | tf_op jit(solution)/shard_map/ppermute | solution.py:59
  62.8 81.7 %collective-permute-start.19 = (bf16[1024,512]{1,0:T(8,128)(2,1)S(1)}, bf16[1024,512]{1,0:T(8,128)(2,1)S(1)}, u32[]{:S(2)}, u32[]{:S(2)}) collective-permute-start(bf16[1024,512]{1,0:T(8,128)(2,1)S(1)} %get-tuple-element.17.rest_0_), channel_id=1, source_target_pairs={{0,2},{1,3},{2,0},{3,1},{4,6},{5,7},{6,4},{7,5},{8,10},{9,11},{10,... | collective-permute-start | bytes 3145736 | tf_op jit(solution)/shard_map/ppermute | solution.py:59
  72.9 36.6 %all-to-all-start = ((bf16[16,8,384]{2,1,0:T(8,128)(2,1)}), bf16[16,8,384]{2,1,0:T(8,128)(2,1)S(1)}, u32[]{:S(2)}, u32[]{:S(2)}) async-start(bf16[16,8,384]{2,1,0:T(8,128)(2,1)} %bitcast.92), calls=%async_computation | async-start | bytes 196608 | tf_op jit(solution)/shard_map/all_to_all | solution.py:295
  109.6 35.0 %collective-permute-start.20 = (bf16[1024,512]{1,0:T(8,128)(2,1)S(1)}, bf16[1024,512]{1,0:T(8,128)(2,1)}, u32[]{:S(2)}, u32[]{:S(2)}) collective-permute-start(bf16[1024,512]{1,0:T(8,128)(2,1)S(1)} %get-tuple-element.10.rest_1_), channel_id=1, source_target_pairs={{0,2},{1,3},{2,0},{3,1},{4,6},{5,7},{6,4},{7,5},{8,10},{9,11},{10,... | collective-permute-start | bytes 3145736 | tf_op jit(solution)/shard_map/ppermute | solution.py:59
  111.7 10.1 %all-to-all-start.1 = ((bf16[16,8,384]{2,1,0:T(8,128)(2,1)}), bf16[16,8,384]{2,1,0:T(8,128)(2,1)S(1)}, u32[]{:S(2)}, u32[]{:S(2)}) async-start(bf16[16,8,384]{2,1,0:T(8,128)(2,1)} %fusion.2), calls=%async_computation.1 | async-start | bytes 196608 | tf_op jit(solution)/shard_map/all_to_all | solution.py:302
  126.5 11.6 %collective-permute-start.16 = (bf16[32,1536]{1,0:T(8,128)(2,1)}, bf16[32,1536]{1,0:T(8,128)(2,1)S(1)}, u32[]{:S(2)}, u32[]{:S(2)}) collective-permute-start(bf16[32,1536]{1,0:T(8,128)(2,1)} %shard_map.150), channel_id=1, source_target_pairs={{0,0},{4,5},{8,10},{12,15},{16,80},{20,85},{24,90},{28,95},{32,160... | collective-permute-start | bytes 294920 | tf_op jit(solution)/shard_map/ppermute | solution.py:317
  139.4 63.5 %all-to-all-start.2 = ((bf16[16,32,1536]{2,1,0:T(8,128)(2,1)}), bf16[16,32,1536]{2,1,0:T(8,128)(2,1)}, u32[]{:S(2)}, u32[]{:S(2)}) async-start(bf16[16,32,1536]{2,1,0:T(8,128)(2,1)} %broadcast_in_dim.12), calls=%async_computation.2 | async-start | bytes 3145728 | tf_op jit(solution)/shard_map/all_to_all | solution.py:322
  143.8 10.4 %collective-permute-start.17 = (bf16[1024,512]{1,0:T(8,128)(2,1)S(1)}, bf16[1024,512]{1,0:T(8,128)(2,1)}, u32[]{:S(2)}, u32[]{:S(2)}) collective-permute-start(bf16[1024,512]{1,0:T(8,128)(2,1)S(1)} %get-tuple-element.17.rest_0_), channel_id=1, source_target_pairs={{0,1},{1,0},{2,3},{3,2},{4,5},{5,4},{6,7},{7,6},{8,9},{9,8},{10,11... | collective-permute-start | bytes 3145736 | tf_op jit(solution)/shard_map/ppermute | solution.py:61
  144.0 10.3 %collective-permute-start.18 = (bf16[1024,512]{1,0:T(8,128)(2,1)S(1)}, bf16[1024,512]{1,0:T(8,128)(2,1)}, u32[]{:S(2)}, u32[]{:S(2)}) collective-permute-start(bf16[1024,512]{1,0:T(8,128)(2,1)S(1)} %get-tuple-element.10.rest_1_), channel_id=1, source_target_pairs={{0,1},{1,0},{2,3},{3,2},{4,5},{5,4},{6,7},{7,6},{8,9},{9,8},{10,11... | collective-permute-start | bytes 3145736 | tf_op jit(solution)/shard_map/ppermute | solution.py:61
  (37 other events, 509.5 us)
Sparse Core Ops, SparseCore 0:
  10.4 69.9 all-gather.6
  82.9 100.3 all-gather.4

commit v3 on v2

--- a/solution.py
+++ b/solution.py
@@ -17,7 +17,7 @@
 GROUP = ("segment", "dp")
 BF16 = jnp.bfloat16
 F32 = jnp.float32
-VMEM_LIMIT = 56 * 1024 * 1024
+VMEM_LIMIT = 36 * 1024 * 1024
 
 
 def layer_norm(inputs, gain_row):
@@ -55,10 +55,13 @@
     return (k >> 1) ^ ((k & 1) * 9)
 
 
-def dp_blocks(value):
-    over_z = lax.ppermute(value, "dp", [(0, 2), (1, 3), (2, 0), (3, 1)])
+def over_z(value):
+    return lax.ppermute(value, "dp", [(0, 2), (1, 3), (2, 0), (3, 1)])
+
+
+def dp_blocks(value, across):
     mate = [(0, 1), (1, 0), (2, 3), (3, 2)]
-    return [value, lax.ppermute(value, "dp", mate), over_z, lax.ppermute(over_z, "dp", mate)]
+    return [value, lax.ppermute(value, "dp", mate), across, lax.ppermute(across, "dp", mate)]
 
 
 def norm_kernel(value_ref, gain_ref, out_ref):
@@ -149,7 +152,10 @@
                 pl.BlockSpec((rows, depth), lambda i, w: (i, 0)),
                 pl.BlockSpec((1, depth), lambda i, w: (0, 0)),
             ]
-            + [pl.BlockSpec(w.shape, lambda i, w: (0, 0)) for w in weights],
+            + [
+                pl.BlockSpec(w.shape, lambda i, w: (0, 0), pipeline_mode=pl.Buffered(1))
+                for w in weights
+            ],
             out_specs=pl.BlockSpec((rows, cols), lambda i, w: (i, 0)),
             scratch_shapes=[pltpu.VMEM((rows, 128), F32), pltpu.VMEM((rows, 128), F32)],
         ),
@@ -158,74 +164,96 @@
     )(where, text, gain, *weights)
 
 
-def attend_kernel(count, order, gate_ref, q_ref, k_ref, v_ref, cot_ref, ctx_ref, dk_ref, dv_ref, acc_k, acc_v):
+def attend_kernel(
+    count, order, where, gate_ref, q_ref, cot_ref, dest_ref, kv0, kv1, kv2, kv3,
+    ctx_ref, part_ref, grads, acc, pair,
+):
     tokens = q_ref.shape[0]
-    keys = k_ref.shape[0]
+    keys = dest_ref.shape[0]
+    block = kv0.shape[0]
     rows = 256
     gate = gate_ref[0]
-    slot = lax.broadcasted_iota(jnp.int32, (rows, keys), 1) % FMAX
-    live = slot < count[0]
+    head = pl.program_id(0)
+    cols_k = pl.ds(pl.multiple_of(head * HD, HD), HD)
+    cols_v = pl.ds(pl.multiple_of((head + pl.num_programs(0)) * HD, HD), HD)
+    places = [pl.ds(pl.multiple_of(where[j] * block, block), block) for j in range(4)]
+    kv = (kv0, kv1, kv2, kv3)
     across = (((1,), (1,)), ((), ()))
     down = (((0,), (0,)), ((), ()))
+    total = None
+    for place, weight in zip(places, kv):
+        both = jnp.concatenate([weight[:, cols_k], weight[:, cols_v]], axis=1)
+        term = jnp.dot(dest_ref[:, place], both, preferred_element_type=F32)
+        total = term if total is None else total + term
+    pair[...] = total.astype(BF16)
+    slot = lax.broadcasted_iota(jnp.int32, (1, keys), 1) % FMAX
+    bias = jnp.where(slot < count[0], 0.0, -1e30)
+    scale = 1.0 / math.sqrt(HD)
     for step in range(tokens // rows):
         at = slice(step * rows, (step + 1) * rows)
         q = q_ref[at, :]
-        score = lax.dot_general(q, k_ref[...], across, preferred_element_type=F32)
-        score = jnp.where(live, score * (1.0 / math.sqrt(HD)), -1e30)
-        weight = jnp.exp(score - jnp.max(score, axis=1, keepdims=True))
+        score = lax.dot_general(q, pair[:, :HD], across, preferred_element_type=F32) + bias
+        top = jnp.max(score, axis=1, keepdims=True)
+        weight = jnp.exp((score - top) * scale)
         inverse = 1.0 / jnp.sum(weight, axis=1, keepdims=True)
         rounded = weight.astype(BF16)
-        blend = jnp.dot(rounded, v_ref[...], preferred_element_type=F32) * inverse
+        blend = jnp.dot(rounded, pair[:, HD:], preferred_element_type=F32) * inverse
         ctx_ref[at, :] = (gate * blend).astype(BF16)
         cot = gate * cot_ref[at, :].astype(F32)
         d_blend = (cot * inverse).astype(BF16)
         d_sum = -jnp.sum(cot * blend, axis=1, keepdims=True) * inverse
-        d_weight = lax.dot_general(d_blend, v_ref[...], across, preferred_element_type=F32)
-        d_weight = d_weight.astype(BF16).astype(F32) + d_sum
-        d_score = (d_weight * weight * (1.0 / math.sqrt(HD))).astype(BF16)
+        d_weight = lax.dot_general(d_blend, pair[:, HD:], across, preferred_element_type=F32)
+        d_score = ((d_weight + d_sum) * weight).astype(BF16)
         grad_k = lax.dot_general(d_score, q, down, preferred_element_type=F32)
         grad_v = lax.dot_general(rounded, d_blend, down, preferred_element_type=F32)
         if step == 0:
-            acc_k[...] = grad_k
-            acc_v[...] = grad_v
+            acc[:, :HD] = grad_k
+            acc[:, HD:] = grad_v
         else:
-            acc_k[...] += grad_k
-            acc_v[...] += grad_v
+            acc[:, :HD] += grad_k
+            acc[:, HD:] += grad_v
     chunks = order.shape[0]
     size = keys // chunks
     for j in range(chunks):
         to = pl.ds(pl.multiple_of(order[j] * size, size), size)
-        dk_ref[to, :] = acc_k[j * size : (j + 1) * size, :].astype(BF16)
-        dv_ref[to, :] = acc_v[j * size : (j + 1) * size, :].astype(BF16)
-
-
-def attention(query, pairs, cot, count, order, gate):
+        at = slice(j * size, (j + 1) * size)
+        grads[to, cols_k] = (acc[at, :HD] * scale).astype(BF16)
+        grads[to, cols_v] = acc[at, HD:].astype(BF16)
+
+    @pl.when(head == pl.num_programs(0) - 1)
+    def _():
+        for place, weight in zip(places, kv):
+            part_ref[:, place] = lax.dot_general(
+                grads[...], weight[...], across, preferred_element_type=F32
+            ).astype(BF16)
+
+
+def attention(query, dest, kv_blocks, cot, count, order, where, gate):
     tokens, cols = query.shape
-    keys = pairs.shape[0]
+    keys, width = dest.shape
     heads = cols // HD
-    head = lambda n: pl.BlockSpec((n, HD), lambda h, c, o: (0, h))
+    head = pl.BlockSpec((tokens, HD), lambda h, *_: (0, h))
+    whole = lambda a: pl.BlockSpec(a.shape, lambda h, *_: (0, 0), pipeline_mode=pl.Buffered(1))
     return pl.pallas_call(
         attend_kernel,
         grid_spec=pltpu.PrefetchScalarGridSpec(
-            num_scalar_prefetch=2,
+            num_scalar_prefetch=3,
             grid=(heads,),
-            in_specs=[
-                pl.BlockSpec(memory_space=pltpu.SMEM),
-                head(tokens),
-                head(keys),
-                pl.BlockSpec((keys, HD), lambda h, c, o: (0, h + heads)),
-                head(tokens),
+            in_specs=[pl.BlockSpec(memory_space=pltpu.SMEM), head, head, whole(dest)]
+            + [whole(w) for w in kv_blocks],
+            out_specs=[head, pl.BlockSpec((keys, width), lambda h, *_: (0, 0))],
+            scratch_shapes=[
+                pltpu.VMEM((keys, 2 * cols), BF16),
+                pltpu.VMEM((keys, 2 * HD), F32),
+                pltpu.VMEM((keys, 2 * HD), BF16),
             ],
-            out_specs=[head(tokens), head(keys), head(keys)],
-            scratch_shapes=[pltpu.VMEM((keys, HD), F32), pltpu.VMEM((keys, HD), F32)],
         ),
         out_shape=[
             jax.ShapeDtypeStruct((tokens, cols), BF16),
-            jax.ShapeDtypeStruct((keys, cols), BF16),
-            jax.ShapeDtypeStruct((keys, cols), BF16),
+            jax.ShapeDtypeStruct((keys, width), BF16),
         ],
         compiler_params=pltpu.CompilerParams(vmem_limit_bytes=VMEM_LIMIT),
-    )(count, order, gate, query, pairs, pairs, cot)
+    )(count, order, where, gate, query, cot, dest, *kv_blocks)
 
 
 def per_device(
@@ -254,29 +282,29 @@
     width = res_query.shape[1]
     res_scale = 1.0 / math.sqrt(RESAMPLE_HEAD_DIM)
 
-    split = (text.shape[2] // 3) * 2
-    text_first = lax.all_gather(text[0, 0, :split], "mp", axis=1, tiled=True)
-    text_last = lax.all_gather(text[0, 0, split:], "mp", axis=1, tiled=True)
+    whole_text = lax.all_gather(text[0, 0], "mp", axis=1, tiled=True)
     media = norm_rows(frames.reshape(-1, E), norm_gains[:1]).reshape(frames.shape)
     half = owned // 2
     ring_x = [ring(media[:half], "x"), ring(media[half:], "y")]
     kv_local = jnp.concatenate([w_kv[0, :, 0], w_kv[0, :, 1]], axis=1)
-    kv_blocks = dp_blocks(kv_local)
+    kv_across = over_z(kv_local)
     depth = w_query.shape[1] // 2
-    query_low = dp_blocks(w_query[0, :depth])
+    low_across = over_z(w_query[0, :depth])
 
     lat_norm = layer_norm(latent_init, norm_gains[1]).astype(BF16)
     res_pair = jnp.concatenate([res_kv[:, 0], res_kv[:, 1]], axis=1)
     res_q = jnp.dot(lat_norm, res_query, preferred_element_type=F32).astype(BF16)
     lat_pairs = jnp.dot(lat_norm, res_pair, preferred_element_type=F32).astype(BF16)
     media_halves = []
-    for blocks, axis in zip(ring_x, ("y", "x")):
-        joined = jnp.concatenate(blocks, axis=1)
+    joined_halves = [jnp.concatenate(blocks, axis=1) for blocks in ring_x]
+    joined_halves, kv_across = lax.optimization_barrier((joined_halves, kv_across))
+    for joined, axis in zip(joined_halves, ("y", "x")):
         parts = [
             jnp.einsum("fpe,ec->fpc", block, res_pair, preferred_element_type=F32).astype(BF16)
             for block in ring(joined, axis)
         ]
         media_halves.append(jnp.concatenate(parts, axis=1))
+    media_halves, low_across = lax.optimization_barrier((media_halves, low_across))
     media_pairs = jnp.concatenate(media_halves, axis=0)
     pair_list = jnp.concatenate(
         [jnp.broadcast_to(lat_pairs, (owned,) + lat_pairs.shape), media_pairs], axis=1
@@ -294,7 +322,9 @@
     piece = res_context.reshape(owned, groups, share * width).swapaxes(0, 1)
     piece = lax.all_to_all(piece, GROUP, 0, 0, tiled=True).reshape(slots, share * width)
     piece, query_rest = lax.optimization_barrier((piece, w_query[0, depth:]))
-    query_high = dp_blocks(query_rest)
+    query_high = dp_blocks(query_rest, over_z(query_rest))
+    query_low = dp_blocks(w_query[0, :depth], low_across)
+    kv_blocks = dp_blocks(kv_local, kv_across)
     slot_ids = jnp.arange(slots, dtype=jnp.int32)
     target = (twice(group) ^ (slot_ids // owned)) * owned + slot_ids % owned
     to_dest = (frame_dest[None, :] == target[:, None]).astype(BF16)
@@ -326,28 +356,12 @@
 
     where = jnp.stack([dp, dp ^ 1, dp ^ 2, dp ^ 3]).astype(jnp.int32)
     query_blocks = [w for both in zip(query_low, query_high) for w in both]
-    query_first = query_matmul(text_first, text_gain, query_blocks, where)
-    dest, query_first = lax.optimization_barrier((dest, query_first))
-    query_last = query_matmul(text_last, text_gain, query_blocks, where)
-    full_kv = jnp.zeros((E, kv_local.shape[1]), BF16)
-    for j, block in enumerate(kv_blocks):
-        full_kv = lax.dynamic_update_slice_in_dim(
-            full_kv, block, where[j] * kv_local.shape[0], 0
-        )
-    pairs = jnp.dot(dest, full_kv, preferred_element_type=F32).astype(BF16)
-    context, grad_k, grad_v = attention(
-        jnp.concatenate([query_first, query_last], axis=0),
-        pairs,
-        cotangent[0, 0],
-        frame_counts[0],
-        order,
-        jnp.tanh(xgate),
-    )
-
-    grad = jnp.concatenate([grad_k, grad_v], axis=1)
-    part = lax.dot_general(
-        grad, full_kv, (((1,), (1,)), ((), ())), preferred_element_type=F32
-    ).astype(BF16)
+    query = query_matmul(whole_text, text_gain, query_blocks, where)
+    dest, query = lax.optimization_barrier((dest, query))
+    context, part = attention(
+        query, dest, kv_blocks, cotangent[0, 0], frame_counts[0], order, where, jnp.tanh(xgate)
+    )
+
     part = lax.all_to_all(part.reshape(mp_count, share * owned, E), "mp", 0, 0, tiled=True)
     dest_grad = jnp.sum(part.astype(F32), axis=0).astype(BF16)
     cut = groups // share

time: 288 us -> 244 us (0.85)
  waiting for transfers between devices: 57 us -> 34.4 us
  matrix products: 23 us -> 5.21 us
  starting transfers between devices: 53.5 us -> 61.4 us
  other arithmetic: 9.22 us -> 3.63 us
  local copies, waits for them, and re-layouts: 23.2 us -> 18.8 us
    all_gather x2 -> x1, waiting for transfers between devices: 16.4 us -> 0.01 us  [per_device(): whole_text = lax.all_gather(text[0, 0], 'mp', axis=1, tiled=True)]
    all_to_all x1, waiting for transfers between devices: 24.4 us -> 8.47 us  [per_device(): lax.all_to_all(piece, GROUP, 0, 0, tiled=True).reshape(slots, share * width)]
    dot_general x2 -> x0, matrix products: 8.27 us -> none  [the longest x1 5.25 us: per_device(): pairs = jnp.dot(dest, full_kv, preferred_element_type=F32).astype(BF16)]
    pallas_call x1, Pallas kernels: 12.1 us -> 19.8 us  [attention(): pl.pallas_call(attend_kernel, grid_spec=pltpu.PrefetchScalarGridSpec(num_...]
    unnamed x60 -> x50, local copies, waits for them, and re-layouts: 1.69 us -> 8.94 us
    pallas_call x2 -> x1, Pallas kernels: 32.3 us -> 25.1 us  [query_matmul(): pl.pallas_call(query_kernel, grid_spec=pltpu.PrefetchScalarGridSpec(num_s...]
    dynamic_update_slice x3 -> x0, local copies, waits for them, and re-layouts: 6.24 us -> none  [per_device(): lax.dynamic_update_slice_in_dim(full_kv, block, where[j] * kv_local.shape...]
    ppermute x16, waiting for transfers between devices: 3.04 us -> 9.11 us  [shift(): return lax.ppermute(value, 'mp', pairs)]
  transfers between devices with their start and end apart: 31 -> 30, of which waited for: 6 -> 9; matrix products, arithmetic and copies ran while one was open for 15% -> 7% of each run, Pallas kernels for 13% -> 11%
where the time goes in v3:
time: 244 us; the launch traced here: 243 us
  starting transfers between devices  61.4 us (25%)
  blocking collectives  56.2 us (23%)
  Pallas kernels  47.8 us (20%)
  waiting for transfers between devices  34.4 us (14%)
  local copies, waits for them, and re-layouts  18.8 us (8%)
  between operations  15.9 us (7%)
  matrix products  5.21 us (2%)
  other arithmetic  3.63 us (1%)
    all_to_all x1, blocking collectives, per_device(): lax.all_to_all(part.reshape(mp_count, share * owned, E), 'mp', 0, 0, tile...  28.6 us
    pallas_call x1, Pallas kernels, query_matmul(): pl.pallas_call(query_kernel, grid_spec=pltpu.PrefetchScalarGridSpec(num_s...  25.1 us
    ppermute x16, starting transfers between devices, shift(): return lax.ppermute(value, 'mp', pairs)  22.9 us
    pallas_call x1, Pallas kernels, attention(): pl.pallas_call(attend_kernel, grid_spec=pltpu.PrefetchScalarGridSpec(num_...  19.8 us
    all_to_all x1, blocking collectives, per_device(): lax.all_to_all(send, GROUP, 0, 0, tiled=True).reshape(slots, E // cut)  16.7 us
    all_to_all x1, starting transfers between devices, per_device(): lax.all_to_all(piece, GROUP, 0, 0, tiled=True).reshape(slots, share * width)  13.3 us
    all_to_all x1, blocking collectives, per_device(): lax.all_to_all(send.reshape(groups, owned, E // cut), GROUP, 0, 0, tiled=...  10.9 us
    ppermute x16, waiting for transfers between devices, shift(): return lax.ppermute(value, 'mp', pairs)  9.11 us
  transfers between devices with their start and end apart: 30, of which 9 were waited for; matrix products, arithmetic and copies ran while one was open for 7% of the time, Pallas kernels for 11%

profile of v3, /device:TPU:1, one launch (start us, length us, event | category | flops | bytes accessed | tf_op | source)
XLA Modules:
  0.0 243.3 jit_solution(10570393879547253269)
XLA Ops:
  9.3 1.8 shard_map.149
  12.1 2.2 collective-permute-start.4
  27.3 2.7 %collective-permute-start.7 = (bf16[2,8,1536]{2,1,0:T(8,128)(2,1)}, bf16[2,8,1536]{2,1,0:T(8,128)(2,1)}, u32[]{:S(2)}, u32[]{:S(2)}) collective-permute-start(bf16[2,8,1536]{2,1,0:T(8,128)(2,1)} %slice.98), channel_id=1, source_target_pairs={{0,48},{4,52},{8,56},{12,60},{16,0},{20,4},{24,8},{28,12},{32,16},... | collective-permute-start | bytes 147464 | tf_op jit(solution)/shard_map/ppermute | solution.py:39
  31.7 2.7 %collective-permute-start.3 = (bf16[2,8,1536]{2,1,0:T(8,128)(2,1)S(1)}, bf16[2,8,1536]{2,1,0:T(8,128)(2,1)S(1)}, u32[]{:S(2)}, u32[]{:S(2)}) collective-permute-start(bf16[2,8,1536]{2,1,0:T(8,128)(2,1)S(1)} %slice.95), channel_id=1, source_target_pairs={{0,12},{4,0},{8,4},{12,8},{16,28},{20,16},{24,20},{28,24},{32,44},... | collective-permute-start | bytes 147464 | tf_op jit(solution)/shard_map/ppermute | solution.py:39
  37.6 2.0 collective-permute-start.14
  40.0 2.2 collective-permute-start.10
  42.9 8.3 %collective-permute-done.13 = bf16[4,32,1536]{2,1,0:T(8,128)(2,1)S(1)} collective-permute-done((bf16[4,32,1536]{2,1,0:T(8,128)(2,1)S(1)}, bf16[4,32,1536]{2,1,0:T(8,128)(2,1)S(1)}, u32[]{:S(2)}, u32[]{:S(2)}) %collective-permute-start.13) | collective-permute-done | bytes 393248 | tf_op jit(solution)/shard_map/ppermute | solution.py:39
  51.7 2.5 %collective-permute-start.16 = (bf16[2,32,1536]{2,1,0:T(8,128)(2,1)S(1)}, bf16[2,32,1536]{2,1,0:T(8,128)(2,1)S(1)}, u32[]{:S(2)}, u32[]{:S(2)}) collective-permute-start(bf16[2,32,1536]{2,1,0:T(8,128)(2,1)S(1)} %slice.102), channel_id=1, source_target_pairs={{0,12},{4,0},{8,4},{12,8},{16,28},{20,16},{24,20},{28,24},{32,44},... | collective-permute-start | bytes 589832 | tf_op jit(solution)/shard_map/ppermute | solution.py:39
  58.4 5.0 %collective-permute-start.19 = (bf16[1024,512]{1,0:T(8,128)(2,1)}, bf16[1024,512]{1,0:T(8,128)(2,1)}, u32[]{:S(2)}, u32[]{:S(2)}) collective-permute-start(bf16[1024,512]{1,0:T(8,128)(2,1)} %get-tuple-element.27.rest_0_), channel_id=1, source_target_pairs={{0,1},{1,0},{2,3},{3,2},{4,5},{5,4},{6,7},{7,6},{8,9},{9,8},{10,11... | collective-permute-start | bytes 3145736 | tf_op jit(solution)/shard_map/ppermute | solution.py:64
  67.0 13.3 %all-to-all-start = ((bf16[16,8,384]{2,1,0:T(8,128)(2,1)}), bf16[16,8,384]{2,1,0:T(8,128)(2,1)S(1)}, u32[]{:S(2)}, u32[]{:S(2)}) async-start(bf16[16,8,384]{2,1,0:T(8,128)(2,1)} %bitcast.83), calls=%async_computation | async-start | bytes 196608 | tf_op jit(solution)/shard_map/all_to_all | solution.py:323
  80.4 8.5 %all-to-all-done = bf16[16,8,384]{2,1,0:T(8,128)(2,1)S(1)} async-done(((bf16[16,8,384]{2,1,0:T(8,128)(2,1)}), bf16[16,8,384]{2,1,0:T(8,128)(2,1)S(1)}, u32[]{:S(2)}, u32[]{:S(2)}) %all-to-all-start) | async-done | bytes 98336 | tf_op jit(solution)/shard_map/all_to_all | solution.py:323
  89.8 4.8 %all-to-all-start.1 = ((bf16[16,8,384]{2,1,0:T(8,128)(2,1)}), bf16[16,8,384]{2,1,0:T(8,128)(2,1)S(1)}, u32[]{:S(2)}, u32[]{:S(2)}) async-start(bf16[16,8,384]{2,1,0:T(8,128)(2,1)} %fusion.2), calls=%async_computation.1 | async-start | bytes 196608 | tf_op jit(solution)/shard_map/all_to_all | solution.py:332
  94.6 7.9 %all-to-all-done.1 = bf16[16,8,384]{2,1,0:T(8,128)(2,1)S(1)} async-done(((bf16[16,8,384]{2,1,0:T(8,128)(2,1)}), bf16[16,8,384]{2,1,0:T(8,128)(2,1)S(1)}, u32[]{:S(2)}, u32[]{:S(2)}) %all-to-all-start.1) | async-done | bytes 98336 | tf_op jit(solution)/shard_map/all_to_all | solution.py:332
  102.5 2.4 copy-done.1
  105.9 4.8 %collective-permute-start.18 = (bf16[32,1536]{1,0:T(8,128)(2,1)S(1)}, bf16[32,1536]{1,0:T(8,128)(2,1)S(1)}, u32[]{:S(2)}, u32[]{:S(2)}) collective-permute-start(bf16[32,1536]{1,0:T(8,128)(2,1)S(1)} %shard_map.150), channel_id=1, source_target_pairs={{0,0},{4,5},{8,10},{12,15},{16,80},{20,85},{24,90},{28,95},{32,160... | collective-permute-start | bytes 294920 | tf_op jit(solution)/shard_map/ppermute | solution.py:347
  110.7 4.4 %collective-permute-done.18 = bf16[32,1536]{1,0:T(8,128)(2,1)S(1)} collective-permute-done((bf16[32,1536]{1,0:T(8,128)(2,1)S(1)}, bf16[32,1536]{1,0:T(8,128)(2,1)S(1)}, u32[]{:S(2)}, u32[]{:S(2)}) %collective-permute-start.18) | collective-permute-done | bytes 98336 | tf_op jit(solution)/shard_map/ppermute | solution.py:347
  116.5 3.8 %all-to-all-start.2 = ((bf16[16,32,1536]{2,1,0:T(8,128)(2,1)}), bf16[16,32,1536]{2,1,0:T(8,128)(2,1)S(1)}, u32[]{:S(2)}, u32[]{:S(2)}) async-start(bf16[16,32,1536]{2,1,0:T(8,128)(2,1)} %broadcast_in_dim.10), calls=%async_computation.2 | async-start | bytes 3145728 | tf_op jit(solution)/shard_map/all_to_all | solution.py:352
  120.3 2.8 %collective-permute-start.22 = (bf16[1024,512]{1,0:T(8,128)(2,1)}, bf16[1024,512]{1,0:T(8,128)(2,1)}, u32[]{:S(2)}, u32[]{:S(2)}) collective-permute-start(bf16[1024,512]{1,0:T(8,128)(2,1)} %collective-permute-done.17.rest_4_), channel_id=1, source_target_pairs={{0,1},{1,0},{2,3},{3,2},{4,5},{5,4},{6,7},{7,6},{8,9},{9,8},{10,11... | collective-permute-start | bytes 3145736 | tf_op jit(solution)/shard_map/ppermute | solution.py:64
  126.2 2.2 collective-permute-done.20.rest_3_
  128.7 25.1 %shard_map.151.q_ref = bf16[768,512]{1,0:T(8,128)(2,1)S(1)} custom-call(s32[4]{0:T(128)S(1)} %pad_add_fusion.where, bf16[768,8192]{1,0:T(8,128)(2,1)} %bitcast.89, bf16[1,8192]{1,0:T(2,128)(2,1)S(1)} %copy-done.9, bf16[1024,512]{1,0:T(8,128)(2,1)} %get-tuple-element.27.rest_0_, bf16[1024,512]{1,0:T(8,128)(2,1)S(1)} %get-tuple-element.19.rest_1_, ...), custom_call_target="tpu_custom_call" | custom-call | tf_op jit(solution)/shard_map/pallas_call | solution.py:146
  159.3 19.8 %shard_map.152 = (bf16[768,512]{1,0:T(8,128)(2,1)}, bf16[512,1536]{1,0:T(8,128)(2,1)S(1)}) custom-call(s32[1]{0:T(128)} %bitcast.84.count, s32[16]{0:T(128)S(1)} %multiply_xor_fusion.order, s32[4]{0:T(128)S(1)} %pad_add_fusion.where, f32[1]{0:T(128)S(6)} %tanh.3.gate_ref, bf16[768,512]{1,0:T(8,128)(2,1)S(1)} %copy-done.3, bf16[768,512]{1,0:T(8,128)(2,1)S(1)} %bitcast.87, ...), custom_call_target="tpu_custom_call" | custom-call | tf_op jit(solution)/shard_map/pallas_call | solution.py:237
  179.1 28.6 %all_to_all.30 = bf16[16,32,1536]{2,1,0:T(8,128)(2,1)S(1)} all-to-all(bf16[16,32,1536]{2,1,0:T(8,128)(2,1)S(1)} %bitcast.86), channel_id=1, replica_groups=mesh['segment'=4,'mp'=16,'dp'=4] {'mp'}, dimensions={0} | all-to-all | bytes 3145728 | tf_op jit(solution)/shard_map/all_to_all | solution.py:365
  207.9 16.7 %all_to_all.31 = bf16[16,8,384]{2,1,0:T(8,128)(2,1)S(1)} all-to-all(bf16[16,8,384]{2,1,0:T(8,128)(2,1)S(1)} %bitcast.91), channel_id=1, replica_groups=mesh['segment'=4,'mp'=16,'dp'=4] {'segment','dp'}, dimensions={0} | all-to-all | bytes 196608 | tf_op jit(solution)/shard_map/all_to_all | solution.py:373
  224.9 10.9 %all_to_all.32 = bf16[16,8,384]{2,1,0:T(8,128)(2,1)S(1)} all-to-all(bf16[16,8,384]{2,1,0:T(8,128)(2,1)S(1)} %fusion.3), channel_id=1, replica_groups=mesh['segment'=4,'mp'=16,'dp'=4] {'segment','dp'}, dimensions={0} | all-to-all | bytes 196608 | tf_op jit(solution)/shard_map/all_to_all | solution.py:376
  (144 shorter events, 41.9 us)
Async XLA Ops:
  7.2 121.6 %all-gather.3.cloned.1.call-start = ((), (), s32[]{:S(2)}) async-start(), calls=%async_computation.6 | async-start | bytes 13369344 | tf_op jit(solution)/shard_map/all_gather | solution.py:285
  12.1 12.3 %collective-permute-start.4 = (bf16[4,8,1536]{2,1,0:T(8,128)(2,1)S(1)}, bf16[4,8,1536]{2,1,0:T(8,128)(2,1)}, u32[]{:S(2)}, u32[]{:S(2)}) collective-permute-start(bf16[4,8,1536]{2,1,0:T(8,128)(2,1)S(1)} %get-tuple-element.32), channel_id=1, source_target_pairs={{0,16},{4,20},{8,24},{12,28},{16,32},{20,36},{24,40},{28,44},{32,4... | collective-permute-start | bytes 294920 | tf_op jit(solution)/shard_map/ppermute | solution.py:39
  14.3 11.5 %collective-permute-start.5 = (bf16[4,8,1536]{2,1,0:T(8,128)(2,1)S(1)}, bf16[4,8,1536]{2,1,0:T(8,128)(2,1)}, u32[]{:S(2)}, u32[]{:S(2)}) collective-permute-start(bf16[4,8,1536]{2,1,0:T(8,128)(2,1)S(1)} %get-tuple-element.32), channel_id=1, source_target_pairs={{0,48},{4,52},{8,56},{12,60},{16,0},{20,4},{24,8},{28,12},{32,16},... | collective-permute-start | bytes 294920 | tf_op jit(solution)/shard_map/ppermute | solution.py:39
  15.8 14.7 %collective-permute-start = (bf16[4,8,1536]{2,1,0:T(8,128)(2,1)S(1)}, bf16[4,8,1536]{2,1,0:T(8,128)(2,1)S(1)}, u32[]{:S(2)}, u32[]{:S(2)}) collective-permute-start(bf16[4,8,1536]{2,1,0:T(8,128)(2,1)S(1)} %get-tuple-element.33), channel_id=1, source_target_pairs={{0,4},{4,8},{8,12},{12,0},{16,20},{20,24},{24,28},{28,16},{32,36},... | collective-permute-start | bytes 294920 | tf_op jit(solution)/shard_map/ppermute | solution.py:39
  17.1 14.6 %collective-permute-start.1 = (bf16[4,8,1536]{2,1,0:T(8,128)(2,1)S(1)}, bf16[4,8,1536]{2,1,0:T(8,128)(2,1)S(1)}, u32[]{:S(2)}, u32[]{:S(2)}) collective-permute-start(bf16[4,8,1536]{2,1,0:T(8,128)(2,1)S(1)} %get-tuple-element.33), channel_id=1, source_target_pairs={{0,12},{4,0},{8,4},{12,8},{16,28},{20,16},{24,20},{28,24},{32,44},... | collective-permute-start | bytes 294920 | tf_op jit(solution)/shard_map/ppermute | solution.py:39
  20.0 16.9 %collective-permute-start.8 = (bf16[384,1024]{1,0:T(8,128)(2,1)S(1)}, bf16[384,1024]{1,0:T(8,128)(2,1)S(1)}, u32[]{:S(2)}, u32[]{:S(2)}) collective-permute-start(bf16[384,1024]{1,0:T(8,128)(2,1)S(1)} %pad_maximum_fusion.kv0), channel_id=1, source_target_pairs={{0,2},{1,3},{2,0},{3,1},{4,6},{5,7},{6,4},{7,5},{8,10},{9,11},{10,... | collective-permute-start | bytes 2359304 | tf_op jit(solution)/shard_map/ppermute | solution.py:59
  27.3 7.2 %collective-permute-start.7 = (bf16[2,8,1536]{2,1,0:T(8,128)(2,1)}, bf16[2,8,1536]{2,1,0:T(8,128)(2,1)}, u32[]{:S(2)}, u32[]{:S(2)}) collective-permute-start(bf16[2,8,1536]{2,1,0:T(8,128)(2,1)} %slice.98), channel_id=1, source_target_pairs={{0,48},{4,52},{8,56},{12,60},{16,0},{20,4},{24,8},{28,12},{32,16},... | collective-permute-start | bytes 147464 | tf_op jit(solution)/shard_map/ppermute | solution.py:39
  30.5 33.6 %collective-permute-start.17 = (bf16[1024,512]{1,0:T(8,128)(2,1)}, bf16[1024,512]{1,0:T(8,128)(2,1)}, u32[]{:S(2)}, u32[]{:S(2)}) collective-permute-start(bf16[1024,512]{1,0:T(8,128)(2,1)} %get-tuple-element.27.rest_0_), channel_id=1, source_target_pairs={{0,2},{1,3},{2,0},{3,1},{4,6},{5,7},{6,4},{7,5},{8,10},{9,11},{10,... | collective-permute-start | bytes 3145736 | tf_op jit(solution)/shard_map/ppermute | solution.py:59
  36.9 14.4 %collective-permute-start.13 = (bf16[4,32,1536]{2,1,0:T(8,128)(2,1)S(1)}, bf16[4,32,1536]{2,1,0:T(8,128)(2,1)S(1)}, u32[]{:S(2)}, u32[]{:S(2)}) collective-permute-start(bf16[4,32,1536]{2,1,0:T(8,128)(2,1)S(1)} %maximum_maximum_fusion.2), channel_id=1, source_target_pairs={{0,4},{4,8},{8,12},{12,0},{16,20},{20,24},{24,28},{28,16},{32,36},... | collective-permute-start | bytes 1179656 | tf_op jit(solution)/shard_map/ppermute | solution.py:39
  37.6 14.1 %collective-permute-start.14 = (bf16[4,32,1536]{2,1,0:T(8,128)(2,1)S(1)}, bf16[4,32,1536]{2,1,0:T(8,128)(2,1)S(1)}, u32[]{:S(2)}, u32[]{:S(2)}) collective-permute-start(bf16[4,32,1536]{2,1,0:T(8,128)(2,1)S(1)} %maximum_maximum_fusion.2), channel_id=1, source_target_pairs={{0,12},{4,0},{8,4},{12,8},{16,28},{20,16},{24,20},{28,24},{32,44},... | collective-permute-start | bytes 1179656 | tf_op jit(solution)/shard_map/ppermute | solution.py:39
  39.6 14.6 %collective-permute-start.9 = (bf16[4,32,1536]{2,1,0:T(8,128)(2,1)S(1)}, bf16[4,32,1536]{2,1,0:T(8,128)(2,1)S(1)}, u32[]{:S(2)}, u32[]{:S(2)}) collective-permute-start(bf16[4,32,1536]{2,1,0:T(8,128)(2,1)S(1)} %maximum_maximum_fusion.1), channel_id=1, source_target_pairs={{0,16},{4,20},{8,24},{12,28},{16,32},{20,36},{24,40},{28,44},{32,4... | collective-permute-start | bytes 1179656 | tf_op jit(solution)/shard_map/ppermute | solution.py:39
  40.0 15.5 %collective-permute-start.10 = (bf16[4,32,1536]{2,1,0:T(8,128)(2,1)S(1)}, bf16[4,32,1536]{2,1,0:T(8,128)(2,1)S(1)}, u32[]{:S(2)}, u32[]{:S(2)}) collective-permute-start(bf16[4,32,1536]{2,1,0:T(8,128)(2,1)S(1)} %maximum_maximum_fusion.1), channel_id=1, source_target_pairs={{0,48},{4,52},{8,56},{12,60},{16,0},{20,4},{24,8},{28,12},{32,16},... | collective-permute-start | bytes 1179656 | tf_op jit(solution)/shard_map/ppermute | solution.py:39
  51.3 7.1 %collective-permute-start.15 = (bf16[2,32,1536]{2,1,0:T(8,128)(2,1)S(1)}, bf16[2,32,1536]{2,1,0:T(8,128)(2,1)S(1)}, u32[]{:S(2)}, u32[]{:S(2)}) collective-permute-start(bf16[2,32,1536]{2,1,0:T(8,128)(2,1)S(1)} %slice.101), channel_id=1, source_target_pairs={{0,4},{4,8},{8,12},{12,0},{16,20},{20,24},{24,28},{28,16},{32,36},... | collective-permute-start | bytes 589832 | tf_op jit(solution)/shard_map/ppermute | solution.py:39
  51.7 11.7 %collective-permute-start.16 = (bf16[2,32,1536]{2,1,0:T(8,128)(2,1)S(1)}, bf16[2,32,1536]{2,1,0:T(8,128)(2,1)S(1)}, u32[]{:S(2)}, u32[]{:S(2)}) collective-permute-start(bf16[2,32,1536]{2,1,0:T(8,128)(2,1)S(1)} %slice.102), channel_id=1, source_target_pairs={{0,12},{4,0},{8,4},{12,8},{16,28},{20,16},{24,20},{28,24},{32,44},... | collective-permute-start | bytes 589832 | tf_op jit(solution)/shard_map/ppermute | solution.py:39
  54.1 9.6 %collective-permute-start.11 = (bf16[2,32,1536]{2,1,0:T(8,128)(2,1)S(1)}, bf16[2,32,1536]{2,1,0:T(8,128)(2,1)S(1)}, u32[]{:S(2)}, u32[]{:S(2)}) collective-permute-start(bf16[2,32,1536]{2,1,0:T(8,128)(2,1)S(1)} %slice.99), channel_id=1, source_target_pairs={{0,16},{4,20},{8,24},{12,28},{16,32},{20,36},{24,40},{28,44},{32,4... | collective-permute-start | bytes 589832 | tf_op jit(solution)/shard_map/ppermute | solution.py:39
  55.6 8.1 %collective-permute-start.12 = (bf16[2,32,1536]{2,1,0:T(8,128)(2,1)S(1)}, bf16[2,32,1536]{2,1,0:T(8,128)(2,1)S(1)}, u32[]{:S(2)}, u32[]{:S(2)}) collective-permute-start(bf16[2,32,1536]{2,1,0:T(8,128)(2,1)S(1)} %slice.100), channel_id=1, source_target_pairs={{0,48},{4,52},{8,56},{12,60},{16,0},{20,4},{24,8},{28,12},{32,16},... | collective-permute-start | bytes 589832 | tf_op jit(solution)/shard_map/ppermute | solution.py:39
  58.4 65.4 %collective-permute-start.19 = (bf16[1024,512]{1,0:T(8,128)(2,1)}, bf16[1024,512]{1,0:T(8,128)(2,1)}, u32[]{:S(2)}, u32[]{:S(2)}) collective-permute-start(bf16[1024,512]{1,0:T(8,128)(2,1)} %get-tuple-element.27.rest_0_), channel_id=1, source_target_pairs={{0,1},{1,0},{2,3},{3,2},{4,5},{5,4},{6,7},{7,6},{8,9},{9,8},{10,11... | collective-permute-start | bytes 3145736 | tf_op jit(solution)/shard_map/ppermute | solution.py:64
  67.0 21.8 %all-to-all-start = ((bf16[16,8,384]{2,1,0:T(8,128)(2,1)}), bf16[16,8,384]{2,1,0:T(8,128)(2,1)S(1)}, u32[]{:S(2)}, u32[]{:S(2)}) async-start(bf16[16,8,384]{2,1,0:T(8,128)(2,1)} %bitcast.83), calls=%async_computation | async-start | bytes 196608 | tf_op jit(solution)/shard_map/all_to_all | solution.py:323
  88.8 34.4 %collective-permute-start.21 = (bf16[1024,512]{1,0:T(8,128)(2,1)S(1)}, bf16[1024,512]{1,0:T(8,128)(2,1)}, u32[]{:S(2)}, u32[]{:S(2)}) collective-permute-start(bf16[1024,512]{1,0:T(8,128)(2,1)S(1)} %get-tuple-element.19.rest_1_), channel_id=1, source_target_pairs={{0,2},{1,3},{2,0},{3,1},{4,6},{5,7},{6,4},{7,5},{8,10},{9,11},{10,... | collective-permute-start | bytes 3145736 | tf_op jit(solution)/shard_map/ppermute | solution.py:59
  89.8 12.7 %all-to-all-start.1 = ((bf16[16,8,384]{2,1,0:T(8,128)(2,1)}), bf16[16,8,384]{2,1,0:T(8,128)(2,1)S(1)}, u32[]{:S(2)}, u32[]{:S(2)}) async-start(bf16[16,8,384]{2,1,0:T(8,128)(2,1)} %fusion.2), calls=%async_computation.1 | async-start | bytes 196608 | tf_op jit(solution)/shard_map/all_to_all | solution.py:332
  105.9 9.3 %collective-permute-start.18 = (bf16[32,1536]{1,0:T(8,128)(2,1)S(1)}, bf16[32,1536]{1,0:T(8,128)(2,1)S(1)}, u32[]{:S(2)}, u32[]{:S(2)}) collective-permute-start(bf16[32,1536]{1,0:T(8,128)(2,1)S(1)} %shard_map.150), channel_id=1, source_target_pairs={{0,0},{4,5},{8,10},{12,15},{16,80},{20,85},{24,90},{28,95},{32,160... | collective-permute-start | bytes 294920 | tf_op jit(solution)/shard_map/ppermute | solution.py:347
  116.5 38.3 %all-to-all-start.2 = ((bf16[16,32,1536]{2,1,0:T(8,128)(2,1)}), bf16[16,32,1536]{2,1,0:T(8,128)(2,1)S(1)}, u32[]{:S(2)}, u32[]{:S(2)}) async-start(bf16[16,32,1536]{2,1,0:T(8,128)(2,1)} %broadcast_in_dim.10), calls=%async_computation.2 | async-start | bytes 3145728 | tf_op jit(solution)/shard_map/all_to_all | solution.py:352
  123.6 31.1 %collective-permute-start.24 = (bf16[384,1024]{1,0:T(8,128)(2,1)}, bf16[384,1024]{1,0:T(8,128)(2,1)}, u32[]{:S(2)}, u32[]{:S(2)}) collective-permute-start(bf16[384,1024]{1,0:T(8,128)(2,1)} %copy-done.4), channel_id=1, source_target_pairs={{0,1},{1,0},{2,3},{3,2},{4,5},{5,4},{6,7},{7,6},{8,9},{9,8},{10,11... | collective-permute-start | bytes 2359304 | tf_op jit(solution)/shard_map/ppermute | solution.py:64
  123.7 31.0 %collective-permute-start.25 = (bf16[384,1024]{1,0:T(8,128)(2,1)}, bf16[384,1024]{1,0:T(8,128)(2,1)}, u32[]{:S(2)}, u32[]{:S(2)}) collective-permute-start(bf16[384,1024]{1,0:T(8,128)(2,1)} %copy-done.7), channel_id=1, source_target_pairs={{0,1},{1,0},{2,3},{3,2},{4,5},{5,4},{6,7},{7,6},{8,9},{9,8},{10,11... | collective-permute-start | bytes 2359304 | tf_op jit(solution)/shard_map/ppermute | solution.py:64
  (31 other events, 212.5 us)
Sparse Core Ops, SparseCore 0:
  10.4 112.3 all-gather.2

commit v4 on v3

--- a/solution.py
+++ b/solution.py
@@ -102,44 +102,52 @@
     )(piece, weight, base, gain)
 
 
-def query_kernel(where, text_ref, gain_ref, *rest):
-    weights, out_ref, mean_ref, scale_ref = rest[:-3], rest[-3], rest[-2], rest[-1]
+def query_kernel(where, text_ref, *rest):
+    weights = rest[:8]
+    out_ref, held, centered, scale_ref, sems = rest[8:]
     rows, depth = text_ref.shape
-    width = 512
-
-    @pl.loop(0, rows // 16)
+    group, width = 64, 256
+    parts = len(weights)
+    block = weights[0].shape[0]
+    copies = [pltpu.make_async_copy(w, held.at[j], sems.at[j]) for j, w in enumerate(weights)]
+    first = pl.program_id(0) == 0
+
+    @pl.when(first)
+    def _():
+        for copy in copies:
+            copy.start()
+
+    @pl.loop(0, rows // group)
     def _(step):
-        at = pl.ds(pl.multiple_of(step * 16, 16), 16)
-        first = text_ref[at, :width].astype(F32)
-        origin = jnp.sum(first, axis=1, keepdims=True) * (1.0 / width)
-        total = first - origin
-        square = total * total
-        for c in range(1, depth // width):
-            off = text_ref[at, c * width : (c + 1) * width].astype(F32) - origin
-            total += off
+        at = pl.ds(pl.multiple_of(step * group, group), group)
+        total = jnp.zeros((group, width), F32)
+        for c in range(depth // width):
+            total += text_ref[at, c * width : (c + 1) * width].astype(F32)
+        mean = jnp.sum(total, axis=1, keepdims=True) * (1.0 / depth)
+        square = jnp.zeros((group, width), F32)
+        for c in range(depth // width):
+            cols = slice(c * width, (c + 1) * width)
+            off = text_ref[at, cols].astype(F32) - mean
+            centered[at, cols] = off.astype(BF16)
             square += off * off
-        total = jnp.sum(total, axis=1, keepdims=True) * (1.0 / depth)
-        square = jnp.sum(square, axis=1, keepdims=True) * (1.0 / depth)
-        spread = jnp.maximum(square - total * total, 0.0)
-        mean_ref[at, :] = jnp.broadcast_to(origin + total, (16, 128))
-        scale_ref[at, :] = jnp.broadcast_to(lax.rsqrt(spread + 1e-05), (16, 128))
-
-    mean = mean_ref[:, :1]
-    scale = scale_ref[:, :1]
+        spread = jnp.sum(square, axis=1, keepdims=True) * (1.0 / depth)
+        scale_ref[at, :] = jnp.broadcast_to(lax.rsqrt(spread + 1e-05), (group, 128))
+
+    @pl.when(first)
+    def _():
+        for copy in copies:
+            copy.wait()
+
     total = None
-    parts = len(weights) // 4
-    block = weights[0].shape[0]
-    for j, weight in enumerate(weights):
-        at = (where[j // parts] * parts + j % parts) * block
+    for j in range(parts):
+        at = (where[j // 2] * 2 + j % 2) * block
         cols = pl.ds(pl.multiple_of(at, block), block)
-        center = text_ref[:, cols].astype(F32) - mean
-        normed = (center * scale * gain_ref[:, cols].astype(F32)).astype(BF16)
-        term = jnp.dot(normed, weight[...], preferred_element_type=F32)
+        term = jnp.dot(centered[:, cols], held[j], preferred_element_type=F32)
         total = term if total is None else total + term
-    out_ref[...] = total.astype(BF16)
-
-
-def query_matmul(text, gain, weights, where):
+    out_ref[...] = (total * scale_ref[:, :1]).astype(BF16)
+
+
+def query_matmul(text, weights, where):
     tokens, depth = text.shape
     cols = weights[0].shape[1]
     rows = 256
@@ -148,64 +156,70 @@
         grid_spec=pltpu.PrefetchScalarGridSpec(
             num_scalar_prefetch=1,
             grid=(tokens // rows,),
-            in_specs=[
-                pl.BlockSpec((rows, depth), lambda i, w: (i, 0)),
-                pl.BlockSpec((1, depth), lambda i, w: (0, 0)),
-            ]
-            + [
-                pl.BlockSpec(w.shape, lambda i, w: (0, 0), pipeline_mode=pl.Buffered(1))
-                for w in weights
+            in_specs=[pl.BlockSpec((rows, depth), lambda i, w: (i, 0))]
+            + [pl.BlockSpec(memory_space=pl.ANY) for w in weights],
+            out_specs=pl.BlockSpec((rows, cols), lambda i, w: (i, 0)),
+            scratch_shapes=[
+                pltpu.VMEM((len(weights),) + weights[0].shape, BF16),
+                pltpu.VMEM((rows, depth), BF16),
+                pltpu.VMEM((rows, 128), F32),
+                pltpu.SemaphoreType.DMA((len(weights),)),
             ],
-            out_specs=pl.BlockSpec((rows, cols), lambda i, w: (i, 0)),
-            scratch_shapes=[pltpu.VMEM((rows, 128), F32), pltpu.VMEM((rows, 128), F32)],
         ),
         out_shape=jax.ShapeDtypeStruct((tokens, cols), BF16),
         compiler_params=pltpu.CompilerParams(vmem_limit_bytes=VMEM_LIMIT),
-    )(where, text, gain, *weights)
+    )(where, text, *weights)
 
 
 def attend_kernel(
     count, order, where, gate_ref, q_ref, cot_ref, dest_ref, kv0, kv1, kv2, kv3,
-    ctx_ref, part_ref, grads, acc, pair,
+    ctx_ref, part_ref, full, pairs, grads, acc, sems,
 ):
     tokens = q_ref.shape[0]
     keys = dest_ref.shape[0]
     block = kv0.shape[0]
-    rows = 256
+    rows = 768
     gate = gate_ref[0]
     head = pl.program_id(0)
+    heads = pl.num_programs(0)
     cols_k = pl.ds(pl.multiple_of(head * HD, HD), HD)
-    cols_v = pl.ds(pl.multiple_of((head + pl.num_programs(0)) * HD, HD), HD)
-    places = [pl.ds(pl.multiple_of(where[j] * block, block), block) for j in range(4)]
-    kv = (kv0, kv1, kv2, kv3)
+    cols_v = pl.ds(pl.multiple_of((head + heads) * HD, HD), HD)
     across = (((1,), (1,)), ((), ()))
     down = (((0,), (0,)), ((), ()))
-    total = None
-    for place, weight in zip(places, kv):
-        both = jnp.concatenate([weight[:, cols_k], weight[:, cols_v]], axis=1)
-        term = jnp.dot(dest_ref[:, place], both, preferred_element_type=F32)
-        total = term if total is None else total + term
-    pair[...] = total.astype(BF16)
-    slot = lax.broadcasted_iota(jnp.int32, (1, keys), 1) % FMAX
+
+    @pl.when(head == 0)
+    def _():
+        copies = []
+        for j, weight in enumerate((kv0, kv1, kv2, kv3)):
+            place = pl.ds(pl.multiple_of(where[j] * block, block), block)
+            copies.append(pltpu.make_async_copy(weight, full.at[place, :], sems.at[j]))
+        for copy in copies:
+            copy.start()
+        for copy in copies:
+            copy.wait()
+        pairs[...] = jnp.dot(dest_ref[...], full[...], preferred_element_type=F32).astype(BF16)
+
+    key = pairs[:, cols_k]
+    value = pairs[:, cols_v]
+    slot = lax.broadcasted_iota(jnp.int32, (keys, 1), 0) % FMAX
     bias = jnp.where(slot < count[0], 0.0, -1e30)
     scale = 1.0 / math.sqrt(HD)
     for step in range(tokens // rows):
         at = slice(step * rows, (step + 1) * rows)
         q = q_ref[at, :]
-        score = lax.dot_general(q, pair[:, :HD], across, preferred_element_type=F32) + bias
-        top = jnp.max(score, axis=1, keepdims=True)
+        score = lax.dot_general(key, q, across, preferred_element_type=F32) + bias
+        top = jnp.max(score, axis=0, keepdims=True)
         weight = jnp.exp((score - top) * scale)
-        inverse = 1.0 / jnp.sum(weight, axis=1, keepdims=True)
-        rounded = weight.astype(BF16)
-        blend = jnp.dot(rounded, pair[:, HD:], preferred_element_type=F32) * inverse
-        ctx_ref[at, :] = (gate * blend).astype(BF16)
-        cot = gate * cot_ref[at, :].astype(F32)
-        d_blend = (cot * inverse).astype(BF16)
-        d_sum = -jnp.sum(cot * blend, axis=1, keepdims=True) * inverse
-        d_weight = lax.dot_general(d_blend, pair[:, HD:], across, preferred_element_type=F32)
-        d_score = ((d_weight + d_sum) * weight).astype(BF16)
-        grad_k = lax.dot_general(d_score, q, down, preferred_element_type=F32)
-        grad_v = lax.dot_general(rounded, d_blend, down, preferred_element_type=F32)
+        prob = weight * (1.0 / jnp.sum(weight, axis=0, keepdims=True))
+        rounded = prob.astype(BF16)
+        blend = lax.dot_general(value, rounded, down, preferred_element_type=F32)
+        ctx_ref[at, :] = (gate * blend.T).astype(BF16)
+        cot = (gate * cot_ref[at, :].astype(F32)).astype(BF16)
+        d_prob = lax.dot_general(value, cot, across, preferred_element_type=F32)
+        d_sum = jnp.sum(prob * d_prob, axis=0, keepdims=True)
+        d_score = ((d_prob - d_sum) * prob).astype(BF16)
+        grad_k = jnp.dot(d_score, q, preferred_element_type=F32)
+        grad_v = jnp.dot(rounded, cot, preferred_element_type=F32)
         if step == 0:
             acc[:, :HD] = grad_k
             acc[:, HD:] = grad_v
@@ -220,12 +234,11 @@
         grads[to, cols_k] = (acc[at, :HD] * scale).astype(BF16)
         grads[to, cols_v] = acc[at, HD:].astype(BF16)
 
-    @pl.when(head == pl.num_programs(0) - 1)
+    @pl.when(head == heads - 1)
     def _():
-        for place, weight in zip(places, kv):
-            part_ref[:, place] = lax.dot_general(
-                grads[...], weight[...], across, preferred_element_type=F32
-            ).astype(BF16)
+        part_ref[...] = lax.dot_general(
+            grads[...], full[...], across, preferred_element_type=F32
+        ).astype(BF16)
 
 
 def attention(query, dest, kv_blocks, cot, count, order, where, gate):
@@ -240,19 +253,21 @@
             num_scalar_prefetch=3,
             grid=(heads,),
             in_specs=[pl.BlockSpec(memory_space=pltpu.SMEM), head, head, whole(dest)]
-            + [whole(w) for w in kv_blocks],
+            + [pl.BlockSpec(memory_space=pl.ANY) for w in kv_blocks],
             out_specs=[head, pl.BlockSpec((keys, width), lambda h, *_: (0, 0))],
             scratch_shapes=[
+                pltpu.VMEM((width, 2 * cols), BF16),
+                pltpu.VMEM((keys, 2 * cols), BF16),
                 pltpu.VMEM((keys, 2 * cols), BF16),
                 pltpu.VMEM((keys, 2 * HD), F32),
-                pltpu.VMEM((keys, 2 * HD), BF16),
+                pltpu.SemaphoreType.DMA((len(kv_blocks),)),
             ],
         ),
         out_shape=[
             jax.ShapeDtypeStruct((tokens, cols), BF16),
             jax.ShapeDtypeStruct((keys, width), BF16),
         ],
-        compiler_params=pltpu.CompilerParams(vmem_limit_bytes=VMEM_LIMIT),
+        compiler_params=pltpu.CompilerParams(vmem_limit_bytes=56 * 1024 * 1024),
     )(count, order, where, gate, query, cot, dest, *kv_blocks)
 
 
@@ -289,7 +304,9 @@
     kv_local = jnp.concatenate([w_kv[0, :, 0], w_kv[0, :, 1]], axis=1)
     kv_across = over_z(kv_local)
     depth = w_query.shape[1] // 2
-    low_across = over_z(w_query[0, :depth])
+    gain = lax.dynamic_slice_in_dim(text_gain[0], dp * 2 * depth, 2 * depth, 0)
+    scaled = (w_query[0].astype(F32) * gain.astype(F32)[:, None]).astype(BF16)
+    low_across = over_z(scaled[:depth])
 
     lat_norm = layer_norm(latent_init, norm_gains[1]).astype(BF16)
     res_pair = jnp.concatenate([res_kv[:, 0], res_kv[:, 1]], axis=1)
@@ -321,9 +338,9 @@
 
     piece = res_context.reshape(owned, groups, share * width).swapaxes(0, 1)
     piece = lax.all_to_all(piece, GROUP, 0, 0, tiled=True).reshape(slots, share * width)
-    piece, query_rest = lax.optimization_barrier((piece, w_query[0, depth:]))
+    piece, query_rest = lax.optimization_barrier((piece, scaled[depth:]))
     query_high = dp_blocks(query_rest, over_z(query_rest))
-    query_low = dp_blocks(w_query[0, :depth], low_across)
+    query_low = dp_blocks(scaled[:depth], low_across)
     kv_blocks = dp_blocks(kv_local, kv_across)
     slot_ids = jnp.arange(slots, dtype=jnp.int32)
     target = (twice(group) ^ (slot_ids // owned)) * owned + slot_ids % owned
@@ -356,7 +373,7 @@
 
     where = jnp.stack([dp, dp ^ 1, dp ^ 2, dp ^ 3]).astype(jnp.int32)
     query_blocks = [w for both in zip(query_low, query_high) for w in both]
-    query = query_matmul(whole_text, text_gain, query_blocks, where)
+    query = query_matmul(whole_text, query_blocks, where)
     dest, query = lax.optimization_barrier((dest, query))
     context, part = attention(
         query, dest, kv_blocks, cotangent[0, 0], frame_counts[0], order, where, jnp.tanh(xgate)

time: 244 us -> 235 us (0.963)
  Pallas kernels: 47.8 us -> 36 us
  other arithmetic: 3.63 us -> 12.1 us
  blocking collectives: 56.2 us -> 51.2 us
  matrix products: 5.21 us -> 9.57 us
  waiting for transfers between devices: 34.4 us -> 31.2 us
  starting transfers between devices: 61.4 us -> 58.5 us
    pallas_call x1, Pallas kernels: 25.1 us -> 16.9 us  [query_matmul(): pl.pallas_call(query_kernel, grid_spec=pltpu.PrefetchScalarGridSpec(num_s...]
    ppermute x16, waiting for transfers between devices: 9.11 us -> 5.3 us  [shift(): return lax.ppermute(value, 'mp', pairs)]
    pallas_call x1, Pallas kernels: 19.8 us -> 16.3 us  [attention(): pl.pallas_call(attend_kernel, grid_spec=pltpu.PrefetchScalarGridSpec(num_...]
    ppermute x3, starting transfers between devices: 3.6 us -> 0.3 us  [dp_blocks(): lax.ppermute(across, 'dp', mate)]
    all_to_all x1, waiting for transfers between devices: 0.01 us -> 3.23 us  [per_device(): lax.all_to_all(jnp.broadcast_to(mine, (mp_count,) + mine.shape), 'mp', 0,...]
    all_to_all x1, blocking collectives: 28.6 us -> 25.8 us  [per_device(): lax.all_to_all(part.reshape(mp_count, share * owned, E), 'mp', 0, 0, tile...]
    convert_element_type x0 -> x2, other arithmetic: none -> 2.76 us  [per_device(): scaled = (w_query[0].astype(F32) * gain.astype(F32)[:, None]).astype(BF16)]
    unnamed x50 -> x44, local copies, waits for them, and re-layouts: 8.94 us -> 6.26 us
  transfers between devices with their start and end apart: 30 -> 30, of which waited for: 9 -> 8; matrix products, arithmetic and copies ran while one was open for 7% -> 14% of each run, Pallas kernels for 11% -> 8%
where the time goes in v4:
time: 235 us; the launch traced here: 234 us
  starting transfers between devices  58.5 us (25%)
  blocking collectives  51.2 us (22%)
  Pallas kernels  36 us (15%)
  waiting for transfers between devices  31.2 us (13%)
  local copies, waits for them, and re-layouts  19.1 us (8%)
  between operations  15.9 us (7%)
  other arithmetic  12.1 us (5%)
  matrix products  9.57 us (4%)
    all_to_all x1, blocking collectives, per_device(): lax.all_to_all(part.reshape(mp_count, share * owned, E), 'mp', 0, 0, tile...  25.8 us
    ppermute x16, starting transfers between devices, shift(): return lax.ppermute(value, 'mp', pairs)  24.5 us
    pallas_call x1, Pallas kernels, query_matmul(): pl.pallas_call(query_kernel, grid_spec=pltpu.PrefetchScalarGridSpec(num_s...  16.9 us
    pallas_call x1, Pallas kernels, attention(): pl.pallas_call(attend_kernel, grid_spec=pltpu.PrefetchScalarGridSpec(num_...  16.3 us
    all_to_all x1, blocking collectives, per_device(): lax.all_to_all(send, GROUP, 0, 0, tiled=True).reshape(slots, E // cut)  14.5 us
    all_to_all x1, starting transfers between devices, per_device(): lax.all_to_all(piece, GROUP, 0, 0, tiled=True).reshape(slots, share * width)  12.5 us
    all_to_all x1, blocking collectives, per_device(): lax.all_to_all(send.reshape(groups, owned, E // cut), GROUP, 0, 0, tiled=...  10.9 us
    all_to_all x1, waiting for transfers between devices, per_device(): lax.all_to_all(piece, GROUP, 0, 0, tiled=True).reshape(slots, share * width)  7.14 us
  transfers between devices with their start and end apart: 30, of which 8 were waited for; matrix products, arithmetic and copies ran while one was open for 14% of the time, Pallas kernels for 8%

profile of v4, /device:TPU:1, one launch (start us, length us, event | category | flops | bytes accessed | tf_op | source)
XLA Modules:
  0.0 233.5 jit_solution(5541071147858249256)
XLA Ops:
  30.7 2.7 %collective-permute-start.7 = (bf16[2,8,1536]{2,1,0:T(8,128)(2,1)}, bf16[2,8,1536]{2,1,0:T(8,128)(2,1)}, u32[]{:S(2)}, u32[]{:S(2)}) collective-permute-start(bf16[2,8,1536]{2,1,0:T(8,128)(2,1)} %slice.98), channel_id=1, source_target_pairs={{0,48},{4,52},{8,56},{12,60},{16,0},{20,4},{24,8},{28,12},{32,16},... | collective-permute-start | bytes 147464 | tf_op jit(solution)/shard_map/ppermute | solution.py:39
  36.3 2.7 %collective-permute-start.3 = (bf16[2,8,1536]{2,1,0:T(8,128)(2,1)S(1)}, bf16[2,8,1536]{2,1,0:T(8,128)(2,1)S(1)}, u32[]{:S(2)}, u32[]{:S(2)}) collective-permute-start(bf16[2,8,1536]{2,1,0:T(8,128)(2,1)S(1)} %slice.95), channel_id=1, source_target_pairs={{0,12},{4,0},{8,4},{12,8},{16,28},{20,16},{24,20},{28,24},{32,44},... | collective-permute-start | bytes 147464 | tf_op jit(solution)/shard_map/ppermute | solution.py:39
  42.8 2.4 %collective-permute-start.14 = (bf16[4,32,1536]{2,1,0:T(8,128)(2,1)S(1)}, bf16[4,32,1536]{2,1,0:T(8,128)(2,1)S(1)}, u32[]{:S(2)}, u32[]{:S(2)}) collective-permute-start(bf16[4,32,1536]{2,1,0:T(8,128)(2,1)S(1)} %maximum_maximum_fusion.2), channel_id=1, source_target_pairs={{0,12},{4,0},{8,4},{12,8},{16,28},{20,16},{24,20},{28,24},{32,44},... | collective-permute-start | bytes 1179656 | tf_op jit(solution)/shard_map/ppermute | solution.py:39
  45.2 2.7 %collective-permute-start.10 = (bf16[4,32,1536]{2,1,0:T(8,128)(2,1)S(1)}, bf16[4,32,1536]{2,1,0:T(8,128)(2,1)S(1)}, u32[]{:S(2)}, u32[]{:S(2)}) collective-permute-start(bf16[4,32,1536]{2,1,0:T(8,128)(2,1)S(1)} %maximum_maximum_fusion.1), channel_id=1, source_target_pairs={{0,48},{4,52},{8,56},{12,60},{16,0},{20,4},{24,8},{28,12},{32,16},... | collective-permute-start | bytes 1179656 | tf_op jit(solution)/shard_map/ppermute | solution.py:39
  48.6 4.3 %collective-permute-done.13 = bf16[4,32,1536]{2,1,0:T(8,128)(2,1)S(1)} collective-permute-done((bf16[4,32,1536]{2,1,0:T(8,128)(2,1)S(1)}, bf16[4,32,1536]{2,1,0:T(8,128)(2,1)S(1)}, u32[]{:S(2)}, u32[]{:S(2)}) %collective-permute-start.13) | collective-permute-done | bytes 393248 | tf_op jit(solution)/shard_map/ppermute | solution.py:39
  55.8 2.3 collective-permute-start.11
  61.1 4.1 %collective-permute-start.19 = (bf16[1024,512]{1,0:T(8,128)(2,1)S(1)}, bf16[1024,512]{1,0:T(8,128)(2,1)}, u32[]{:S(2)}, u32[]{:S(2)}) collective-permute-start(bf16[1024,512]{1,0:T(8,128)(2,1)S(1)} %get-tuple-element.27.rest_0_), channel_id=1, source_target_pairs={{0,1},{1,0},{2,3},{3,2},{4,5},{5,4},{6,7},{7,6},{8,9},{9,8},{10,11... | collective-permute-start | bytes 3145736 | tf_op jit(solution)/shard_map/ppermute | solution.py:64
  67.4 2.6 %fusion.47 = (f32[8,64]{1,0:T(8,128)S(1)}, f32[8,64,192]{2,1,0:T(8,128)}) fusion(bf16[1536,96]{0,1:T(8,128)(2,1)S(1)} %copy-done, bf16[64,1536]{1,0:T(8,128)(2,1)} %param.15, f32[1536]{0:T(1024)S(1)} %convert_reduce_fusion.1, f32[64]{0:T(128)S(1)} %copy-done.20, f32[64]{0:T(128)S(1)} %copy-done.17, bf16[8,192,192]{2,1,0:T(8,128)(2,1)} %maximum_maximum_fusion), kind=kOutput, calls=%fused_computation.89 | convolution fusion | flops 38442496 | bytes 1286656 | tf_op jit(solution)/shard_map/ld,fpd->flp/dot_general | solution.py:330
  71.3 2.4 %fusion.2 = bf16[8,64,96]{2,1,0:T(8,128)(2,1)} fusion(bf16[8,192,192]{2,1,0:T(8,128)(2,1)} %maximum_maximum_fusion, f32[8,64,192]{2,1,0:T(8,128)} %get-tuple-element.37, f32[8,64]{1,0:T(8,128)S(1)} %get-tuple-element.36, f32[8,64]{1,0:T(8,128)S(1)} %fusion.16), kind=kOutput, calls=%fused_computation.5 | convolution fusion | flops 19169280 | bytes 1019904 | tf_op jit(solution)/shard_map/flp,fpd->fld/dot_general | solution.py:334
  75.4 12.5 %all-to-all-start = ((bf16[16,8,384]{2,1,0:T(8,128)(2,1)}), bf16[16,8,384]{2,1,0:T(8,128)(2,1)S(1)}, u32[]{:S(2)}, u32[]{:S(2)}) async-start(bf16[16,8,384]{2,1,0:T(8,128)(2,1)} %bitcast.90), calls=%async_computation | async-start | bytes 196608 | tf_op jit(solution)/shard_map/all_to_all | solution.py:340
  89.3 7.1 %all-to-all-done = bf16[16,8,384]{2,1,0:T(8,128)(2,1)S(1)} async-done(((bf16[16,8,384]{2,1,0:T(8,128)(2,1)}), bf16[16,8,384]{2,1,0:T(8,128)(2,1)S(1)}, u32[]{:S(2)}, u32[]{:S(2)}) %all-to-all-start) | async-done | bytes 98336 | tf_op jit(solution)/shard_map/all_to_all | solution.py:340
  97.3 5.3 %all-to-all-start.1 = ((bf16[16,8,384]{2,1,0:T(8,128)(2,1)}), bf16[16,8,384]{2,1,0:T(8,128)(2,1)S(1)}, u32[]{:S(2)}, u32[]{:S(2)}) async-start(bf16[16,8,384]{2,1,0:T(8,128)(2,1)} %fusion.3), calls=%async_computation.1 | async-start | bytes 196608 | tf_op jit(solution)/shard_map/all_to_all | solution.py:349
  104.1 6.3 %all-to-all-done.1 = bf16[16,8,384]{2,1,0:T(8,128)(2,1)S(1)} async-done(((bf16[16,8,384]{2,1,0:T(8,128)(2,1)}), bf16[16,8,384]{2,1,0:T(8,128)(2,1)S(1)}, u32[]{:S(2)}, u32[]{:S(2)}) %all-to-all-start.1) | async-done | bytes 98336 | tf_op jit(solution)/shard_map/all_to_all | solution.py:349
  110.4 2.5 %copy-done.1 = bf16[1536,1536]{1,0:T(8,128)(2,1)S(1)} copy-done((bf16[1536,1536]{1,0:T(8,128)(2,1)S(1)}, bf16[1536,1536]{1,0:T(8,128)(2,1)}, u32[]{:S(2)}) %copy-start.1) | copy-done | bytes 4718616
  114.9 4.8 %collective-permute-start.18 = (bf16[32,1536]{1,0:T(8,128)(2,1)S(1)}, bf16[32,1536]{1,0:T(8,128)(2,1)S(1)}, u32[]{:S(2)}, u32[]{:S(2)}) collective-permute-start(bf16[32,1536]{1,0:T(8,128)(2,1)S(1)} %shard_map.150), channel_id=1, source_target_pairs={{0,0},{4,5},{8,10},{12,15},{16,80},{20,85},{24,90},{28,95},{32,160... | collective-permute-start | bytes 294920 | tf_op jit(solution)/shard_map/ppermute | solution.py:364
  119.6 5.6 %collective-permute-done.18 = bf16[32,1536]{1,0:T(8,128)(2,1)S(1)} collective-permute-done((bf16[32,1536]{1,0:T(8,128)(2,1)S(1)}, bf16[32,1536]{1,0:T(8,128)(2,1)S(1)}, u32[]{:S(2)}, u32[]{:S(2)}) %collective-permute-start.18) | collective-permute-done | bytes 98336 | tf_op jit(solution)/shard_map/ppermute | solution.py:364
  126.5 4.4 %all-to-all-start.2 = ((bf16[16,32,1536]{2,1,0:T(8,128)(2,1)}), bf16[16,32,1536]{2,1,0:T(8,128)(2,1)}, u32[]{:S(2)}, u32[]{:S(2)}) async-start(bf16[16,32,1536]{2,1,0:T(8,128)(2,1)} %broadcast_in_dim.10), calls=%async_computation.2 | async-start | bytes 3145728 | tf_op jit(solution)/shard_map/all_to_all | solution.py:369
  134.2 2.7 %collective-permute-done.20.rest_3_ = bf16[1024,512]{1,0:T(8,128)(2,1)} collective-permute-done((bf16[1024,512]{1,0:T(8,128)(2,1)S(1)}, bf16[1024,512]{1,0:T(8,128)(2,1)}, u32[]{:S(2)}, u32[]{:S(2)}) %collective-permute-start.20) | collective-permute-done | bytes 1048608 | tf_op jit(solution)/shard_map/ppermute | solution.py:64
  137.0 16.9 %shard_map.151.q_ref = bf16[768,512]{1,0:T(8,128)(2,1)S(1)} custom-call(s32[4]{0:T(128)S(1)} %pad_add_fusion.where, bf16[768,8192]{1,0:T(8,128)(2,1)} %bitcast.86, bf16[1024,512]{1,0:T(8,128)(2,1)S(1)} %get-tuple-element.27.rest_0_, bf16[1024,512]{1,0:T(8,128)(2,1)S(1)} %get-tuple-element.19.rest_1_, bf16[1024,512]{1,0:T(8,128)(2,1)} %collective-permute-done.19.rest_2_, ...), custom_call_target="tpu_custom_call" | custom-call | tf_op jit(solution)/shard_map/pallas_call | solution.py:154
  154.8 3.2 %all-to-all-done.2 = bf16[16,32,1536]{2,1,0:T(8,128)(2,1)} async-done(((bf16[16,32,1536]{2,1,0:T(8,128)(2,1)}), bf16[16,32,1536]{2,1,0:T(8,128)(2,1)}, u32[]{:S(2)}, u32[]{:S(2)}) %all-to-all-start.2) | async-done | bytes 1572896 | tf_op jit(solution)/shard_map/all_to_all | solution.py:369
  158.1 16.3 %shard_map.152 = (bf16[768,512]{1,0:T(8,128)(2,1)}, bf16[512,1536]{1,0:T(8,128)(2,1)}) custom-call(s32[1]{0:T(128)} %bitcast.84.count, s32[16]{0:T(128)} %multiply_xor_fusion.order, s32[4]{0:T(128)} %copy-done.4, f32[1]{0:T(128)S(6)} %tanh.3.gate_ref, bf16[768,512]{1,0:T(8,128)(2,1)} %copy-done.2, bf16[768,512]{1,0:T(8,128)(2,1)} %bitcast.88, ...), custom_call_target="tpu_custom_call" | custom-call | tf_op jit(solution)/shard_map/pallas_call | solution.py:250
  174.3 25.8 %all_to_all.30 = bf16[16,32,1536]{2,1,0:T(8,128)(2,1)S(1)} all-to-all(bf16[16,32,1536]{2,1,0:T(8,128)(2,1)} %bitcast.87), channel_id=1, replica_groups=mesh['segment'=4,'mp'=16,'dp'=4] {'mp'}, dimensions={0} | all-to-all | bytes 3145728 | tf_op jit(solution)/shard_map/all_to_all | solution.py:382
  200.4 14.5 %all_to_all.31 = bf16[16,8,384]{2,1,0:T(8,128)(2,1)S(1)} all-to-all(bf16[16,8,384]{2,1,0:T(8,128)(2,1)S(1)} %bitcast.91), channel_id=1, replica_groups=mesh['segment'=4,'mp'=16,'dp'=4] {'segment','dp'}, dimensions={0} | all-to-all | bytes 196608 | tf_op jit(solution)/shard_map/all_to_all | solution.py:390
  215.1 10.9 %all_to_all.32 = bf16[16,8,384]{2,1,0:T(8,128)(2,1)S(1)} all-to-all(bf16[16,8,384]{2,1,0:T(8,128)(2,1)S(1)} %fusion.4), channel_id=1, replica_groups=mesh['segment'=4,'mp'=16,'dp'=4] {'segment','dp'}, dimensions={0} | all-to-all | bytes 196608 | tf_op jit(solution)/shard_map/all_to_all | solution.py:393
  (140 shorter events, 52.9 us)
Async XLA Ops:
  7.2 129.8 %all-gather.3.cloned.1.call-start = ((), (), s32[]{:S(2)}) async-start(), calls=%async_computation.6 | async-start | bytes 13369344 | tf_op jit(solution)/shard_map/all_gather | solution.py:300
  12.1 15.8 %collective-permute-start.4 = (bf16[4,8,1536]{2,1,0:T(8,128)(2,1)S(1)}, bf16[4,8,1536]{2,1,0:T(8,128)(2,1)}, u32[]{:S(2)}, u32[]{:S(2)}) collective-permute-start(bf16[4,8,1536]{2,1,0:T(8,128)(2,1)S(1)} %get-tuple-element.32), channel_id=1, source_target_pairs={{0,16},{4,20},{8,24},{12,28},{16,32},{20,36},{24,40},{28,44},{32,4... | collective-permute-start | bytes 294920 | tf_op jit(solution)/shard_map/ppermute | solution.py:39
  14.3 15.0 %collective-permute-start.5 = (bf16[4,8,1536]{2,1,0:T(8,128)(2,1)S(1)}, bf16[4,8,1536]{2,1,0:T(8,128)(2,1)}, u32[]{:S(2)}, u32[]{:S(2)}) collective-permute-start(bf16[4,8,1536]{2,1,0:T(8,128)(2,1)S(1)} %get-tuple-element.32), channel_id=1, source_target_pairs={{0,48},{4,52},{8,56},{12,60},{16,0},{20,4},{24,8},{28,12},{32,16},... | collective-permute-start | bytes 294920 | tf_op jit(solution)/shard_map/ppermute | solution.py:39
  15.9 18.1 %collective-permute-start = (bf16[4,8,1536]{2,1,0:T(8,128)(2,1)S(1)}, bf16[4,8,1536]{2,1,0:T(8,128)(2,1)S(1)}, u32[]{:S(2)}, u32[]{:S(2)}) collective-permute-start(bf16[4,8,1536]{2,1,0:T(8,128)(2,1)S(1)} %get-tuple-element.33), channel_id=1, source_target_pairs={{0,4},{4,8},{8,12},{12,0},{16,20},{20,24},{24,28},{28,16},{32,36},... | collective-permute-start | bytes 294920 | tf_op jit(solution)/shard_map/ppermute | solution.py:39
  17.1 18.4 %collective-permute-start.1 = (bf16[4,8,1536]{2,1,0:T(8,128)(2,1)S(1)}, bf16[4,8,1536]{2,1,0:T(8,128)(2,1)}, u32[]{:S(2)}, u32[]{:S(2)}) collective-permute-start(bf16[4,8,1536]{2,1,0:T(8,128)(2,1)S(1)} %get-tuple-element.33), channel_id=1, source_target_pairs={{0,12},{4,0},{8,4},{12,8},{16,28},{20,16},{24,20},{28,24},{32,44},... | collective-permute-start | bytes 294920 | tf_op jit(solution)/shard_map/ppermute | solution.py:39
  20.9 21.0 %collective-permute-start.8 = (bf16[384,1024]{1,0:T(8,128)(2,1)}, bf16[384,1024]{1,0:T(8,128)(2,1)}, u32[]{:S(2)}, u32[]{:S(2)}) collective-permute-start(bf16[384,1024]{1,0:T(8,128)(2,1)} %pad_maximum_fusion.kv0), channel_id=1, source_target_pairs={{0,2},{1,3},{2,0},{3,1},{4,6},{5,7},{6,4},{7,5},{8,10},{9,11},{10,... | collective-permute-start | bytes 2359304 | tf_op jit(solution)/shard_map/ppermute | solution.py:59
  30.7 8.2 %collective-permute-start.7 = (bf16[2,8,1536]{2,1,0:T(8,128)(2,1)}, bf16[2,8,1536]{2,1,0:T(8,128)(2,1)}, u32[]{:S(2)}, u32[]{:S(2)}) collective-permute-start(bf16[2,8,1536]{2,1,0:T(8,128)(2,1)} %slice.98), channel_id=1, source_target_pairs={{0,48},{4,52},{8,56},{12,60},{16,0},{20,4},{24,8},{28,12},{32,16},... | collective-permute-start | bytes 147464 | tf_op jit(solution)/shard_map/ppermute | solution.py:39
  34.6 31.5 %collective-permute-start.17 = (bf16[1024,512]{1,0:T(8,128)(2,1)S(1)}, bf16[1024,512]{1,0:T(8,128)(2,1)S(1)}, u32[]{:S(2)}, u32[]{:S(2)}) collective-permute-start(bf16[1024,512]{1,0:T(8,128)(2,1)S(1)} %get-tuple-element.27.rest_0_), channel_id=1, source_target_pairs={{0,2},{1,3},{2,0},{3,1},{4,6},{5,7},{6,4},{7,5},{8,10},{9,11},{10,... | collective-permute-start | bytes 3145736 | tf_op jit(solution)/shard_map/ppermute | solution.py:59
  41.9 10.9 %collective-permute-start.13 = (bf16[4,32,1536]{2,1,0:T(8,128)(2,1)S(1)}, bf16[4,32,1536]{2,1,0:T(8,128)(2,1)S(1)}, u32[]{:S(2)}, u32[]{:S(2)}) collective-permute-start(bf16[4,32,1536]{2,1,0:T(8,128)(2,1)S(1)} %maximum_maximum_fusion.2), channel_id=1, source_target_pairs={{0,4},{4,8},{8,12},{12,0},{16,20},{20,24},{24,28},{28,16},{32,36},... | collective-permute-start | bytes 1179656 | tf_op jit(solution)/shard_map/ppermute | solution.py:39
  42.8 12.3 %collective-permute-start.14 = (bf16[4,32,1536]{2,1,0:T(8,128)(2,1)S(1)}, bf16[4,32,1536]{2,1,0:T(8,128)(2,1)S(1)}, u32[]{:S(2)}, u32[]{:S(2)}) collective-permute-start(bf16[4,32,1536]{2,1,0:T(8,128)(2,1)S(1)} %maximum_maximum_fusion.2), channel_id=1, source_target_pairs={{0,12},{4,0},{8,4},{12,8},{16,28},{20,16},{24,20},{28,24},{32,44},... | collective-permute-start | bytes 1179656 | tf_op jit(solution)/shard_map/ppermute | solution.py:39
  45.2 10.5 %collective-permute-start.9 = (bf16[4,32,1536]{2,1,0:T(8,128)(2,1)S(1)}, bf16[4,32,1536]{2,1,0:T(8,128)(2,1)S(1)}, u32[]{:S(2)}, u32[]{:S(2)}) collective-permute-start(bf16[4,32,1536]{2,1,0:T(8,128)(2,1)S(1)} %maximum_maximum_fusion.1), channel_id=1, source_target_pairs={{0,16},{4,20},{8,24},{12,28},{16,32},{20,36},{24,40},{28,44},{32,4... | collective-permute-start | bytes 1179656 | tf_op jit(solution)/shard_map/ppermute | solution.py:39
  45.2 12.9 %collective-permute-start.10 = (bf16[4,32,1536]{2,1,0:T(8,128)(2,1)S(1)}, bf16[4,32,1536]{2,1,0:T(8,128)(2,1)S(1)}, u32[]{:S(2)}, u32[]{:S(2)}) collective-permute-start(bf16[4,32,1536]{2,1,0:T(8,128)(2,1)S(1)} %maximum_maximum_fusion.1), channel_id=1, source_target_pairs={{0,48},{4,52},{8,56},{12,60},{16,0},{20,4},{24,8},{28,12},{32,16},... | collective-permute-start | bytes 1179656 | tf_op jit(solution)/shard_map/ppermute | solution.py:39
  52.9 8.2 %collective-permute-start.15 = (bf16[2,32,1536]{2,1,0:T(8,128)(2,1)S(1)}, bf16[2,32,1536]{2,1,0:T(8,128)(2,1)S(1)}, u32[]{:S(2)}, u32[]{:S(2)}) collective-permute-start(bf16[2,32,1536]{2,1,0:T(8,128)(2,1)S(1)} %slice.101), channel_id=1, source_target_pairs={{0,4},{4,8},{8,12},{12,0},{16,20},{20,24},{24,28},{28,16},{32,36},... | collective-permute-start | bytes 589832 | tf_op jit(solution)/shard_map/ppermute | solution.py:39
  55.2 10.1 %collective-permute-start.16 = (bf16[2,32,1536]{2,1,0:T(8,128)(2,1)S(1)}, bf16[2,32,1536]{2,1,0:T(8,128)(2,1)S(1)}, u32[]{:S(2)}, u32[]{:S(2)}) collective-permute-start(bf16[2,32,1536]{2,1,0:T(8,128)(2,1)S(1)} %slice.102), channel_id=1, source_target_pairs={{0,12},{4,0},{8,4},{12,8},{16,28},{20,16},{24,20},{28,24},{32,44},... | collective-permute-start | bytes 589832 | tf_op jit(solution)/shard_map/ppermute | solution.py:39
  55.8 9.8 %collective-permute-start.11 = (bf16[2,32,1536]{2,1,0:T(8,128)(2,1)S(1)}, bf16[2,32,1536]{2,1,0:T(8,128)(2,1)S(1)}, u32[]{:S(2)}, u32[]{:S(2)}) collective-permute-start(bf16[2,32,1536]{2,1,0:T(8,128)(2,1)S(1)} %slice.99), channel_id=1, source_target_pairs={{0,16},{4,20},{8,24},{12,28},{16,32},{20,36},{24,40},{28,44},{32,4... | collective-permute-start | bytes 589832 | tf_op jit(solution)/shard_map/ppermute | solution.py:39
  58.1 7.5 %collective-permute-start.12 = (bf16[2,32,1536]{2,1,0:T(8,128)(2,1)S(1)}, bf16[2,32,1536]{2,1,0:T(8,128)(2,1)S(1)}, u32[]{:S(2)}, u32[]{:S(2)}) collective-permute-start(bf16[2,32,1536]{2,1,0:T(8,128)(2,1)S(1)} %slice.100), channel_id=1, source_target_pairs={{0,48},{4,52},{8,56},{12,60},{16,0},{20,4},{24,8},{28,12},{32,16},... | collective-permute-start | bytes 589832 | tf_op jit(solution)/shard_map/ppermute | solution.py:39
  61.1 70.9 %collective-permute-start.19 = (bf16[1024,512]{1,0:T(8,128)(2,1)S(1)}, bf16[1024,512]{1,0:T(8,128)(2,1)}, u32[]{:S(2)}, u32[]{:S(2)}) collective-permute-start(bf16[1024,512]{1,0:T(8,128)(2,1)S(1)} %get-tuple-element.27.rest_0_), channel_id=1, source_target_pairs={{0,1},{1,0},{2,3},{3,2},{4,5},{5,4},{6,7},{7,6},{8,9},{9,8},{10,11... | collective-permute-start | bytes 3145736 | tf_op jit(solution)/shard_map/ppermute | solution.py:64
  75.4 21.0 %all-to-all-start = ((bf16[16,8,384]{2,1,0:T(8,128)(2,1)}), bf16[16,8,384]{2,1,0:T(8,128)(2,1)S(1)}, u32[]{:S(2)}, u32[]{:S(2)}) async-start(bf16[16,8,384]{2,1,0:T(8,128)(2,1)} %bitcast.90), calls=%async_computation | async-start | bytes 196608 | tf_op jit(solution)/shard_map/all_to_all | solution.py:340
  96.4 35.2 %collective-permute-start.21 = (bf16[1024,512]{1,0:T(8,128)(2,1)S(1)}, bf16[1024,512]{1,0:T(8,128)(2,1)}, u32[]{:S(2)}, u32[]{:S(2)}) collective-permute-start(bf16[1024,512]{1,0:T(8,128)(2,1)S(1)} %get-tuple-element.19.rest_1_), channel_id=1, source_target_pairs={{0,2},{1,3},{2,0},{3,1},{4,6},{5,7},{6,4},{7,5},{8,10},{9,11},{10,... | collective-permute-start | bytes 3145736 | tf_op jit(solution)/shard_map/ppermute | solution.py:59
  97.3 13.1 %all-to-all-start.1 = ((bf16[16,8,384]{2,1,0:T(8,128)(2,1)}), bf16[16,8,384]{2,1,0:T(8,128)(2,1)S(1)}, u32[]{:S(2)}, u32[]{:S(2)}) async-start(bf16[16,8,384]{2,1,0:T(8,128)(2,1)} %fusion.3), calls=%async_computation.1 | async-start | bytes 196608 | tf_op jit(solution)/shard_map/all_to_all | solution.py:349
  114.9 10.4 %collective-permute-start.18 = (bf16[32,1536]{1,0:T(8,128)(2,1)S(1)}, bf16[32,1536]{1,0:T(8,128)(2,1)S(1)}, u32[]{:S(2)}, u32[]{:S(2)}) collective-permute-start(bf16[32,1536]{1,0:T(8,128)(2,1)S(1)} %shard_map.150), channel_id=1, source_target_pairs={{0,0},{4,5},{8,10},{12,15},{16,80},{20,85},{24,90},{28,95},{32,160... | collective-permute-start | bytes 294920 | tf_op jit(solution)/shard_map/ppermute | solution.py:364
  126.5 31.5 %all-to-all-start.2 = ((bf16[16,32,1536]{2,1,0:T(8,128)(2,1)}), bf16[16,32,1536]{2,1,0:T(8,128)(2,1)}, u32[]{:S(2)}, u32[]{:S(2)}) async-start(bf16[16,32,1536]{2,1,0:T(8,128)(2,1)} %broadcast_in_dim.10), calls=%async_computation.2 | async-start | bytes 3145728 | tf_op jit(solution)/shard_map/all_to_all | solution.py:369
  131.7 26.4 %collective-permute-start.24 = (bf16[384,1024]{1,0:T(8,128)(2,1)}, bf16[384,1024]{1,0:T(8,128)(2,1)}, u32[]{:S(2)}, u32[]{:S(2)}) collective-permute-start(bf16[384,1024]{1,0:T(8,128)(2,1)} %pad_maximum_fusion.kv0), channel_id=1, source_target_pairs={{0,1},{1,0},{2,3},{3,2},{4,5},{5,4},{6,7},{7,6},{8,9},{9,8},{10,11... | collective-permute-start | bytes 2359304 | tf_op jit(solution)/shard_map/ppermute | solution.py:64
  132.1 26.0 %collective-permute-start.25 = (bf16[384,1024]{1,0:T(8,128)(2,1)}, bf16[384,1024]{1,0:T(8,128)(2,1)}, u32[]{:S(2)}, u32[]{:S(2)}) collective-permute-start(bf16[384,1024]{1,0:T(8,128)(2,1)} %collective-permute-done.8.kv2), channel_id=1, source_target_pairs={{0,1},{1,0},{2,3},{3,2},{4,5},{5,4},{6,7},{7,6},{8,9},{9,8},{10,11... | collective-permute-start | bytes 2359304 | tf_op jit(solution)/shard_map/ppermute | solution.py:64
  (28 other events, 244.7 us)
Sparse Core Ops, SparseCore 0:
  10.4 112.2 all-gather.2

commit v5 on v4

--- a/solution.py
+++ b/solution.py
@@ -11,6 +11,7 @@
 HD = 128
 E = 1536
 RESAMPLE_HEAD_DIM = 96
+PAD = 128
 LAT = 64
 FMAX = 8
 SIDE = 4
@@ -47,6 +48,10 @@
     return [value, left, right, far]
 
 
+def direct(value, axis):
+    return [value, shift(value, axis, 1), shift(value, axis, -1), shift(value, axis, 2)]
+
+
 def twice(k):
     return ((k << 1) ^ ((k >> 3) * 19)) & 15
 
@@ -74,20 +79,52 @@
     )(value, gain)
 
 
+def resample_kernel(q_ref, lat_ref, *rest):
+    pieces, out_ref, held = rest[:-2], rest[-2], rest[-1]
+    frames_each = pieces[0].shape[0]
+    count = len(pieces) // 4 * frames_each
+    q = q_ref[...]
+    scale = 1.0 / math.sqrt(RESAMPLE_HEAD_DIM)
+    groups = out_ref.shape[0] // count
+    share = q.shape[0] // groups
+    for f in range(count):
+        first = f // frames_each * 4
+        blocks = [pieces[first + j][f % frames_each] for j in range(4)]
+        pair = jnp.concatenate([lat_ref[...]] + blocks, axis=0)
+        score = scale * lax.dot_general(
+            q, pair[:, :PAD], (((1,), (1,)), ((), ())), preferred_element_type=F32
+        )
+        weight = jnp.exp(score - jnp.max(score, axis=1, keepdims=True))
+        blend = jnp.dot(weight.astype(BF16), pair[:, PAD:], preferred_element_type=F32)
+        blend = blend / jnp.sum(weight, axis=1, keepdims=True)
+        for j in range(share):
+            to = pl.ds(j * groups * count + f, groups, stride=count)
+            held[to, :] = blend[j * groups : (j + 1) * groups]
+    for j in range(share):
+        rows = slice(j * groups * count, (j + 1) * groups * count)
+        out_ref[:, j * PAD : (j + 1) * PAD] = held[rows, :].astype(BF16)
+
+
+def resample(q, lat_pairs, pieces, slots, share):
+    return pl.pallas_call(
+        resample_kernel,
+        out_shape=jax.ShapeDtypeStruct((slots, share * PAD), BF16),
+        scratch_shapes=[pltpu.VMEM((slots * share, PAD), F32)],
+    )(q, lat_pairs, *pieces)
+
+
 def latent_kernel(piece_ref, weight_ref, base_ref, gain_ref, out_ref):
     width = RESAMPLE_HEAD_DIM
-    share = piece_ref.shape[1] // width
+    share = piece_ref.shape[1] // PAD
     heads = weight_ref.shape[0] // width
     owned = piece_ref.shape[0] // heads
     piece = piece_ref[...].astype(F32)
     total = base_ref[...]
     for h in range(heads):
         rows = piece[h * owned : (h + 1) * owned]
-        left = jnp.concatenate(
-            [rows[:, j * width : (j + 1) * width] for j in range(share)], axis=0
-        )
+        left = jnp.concatenate([rows[:, j * PAD : (j + 1) * PAD] for j in range(share)], axis=0)
         total = total + jnp.dot(
-            left.astype(BF16),
+            left[:, :width].astype(BF16),
             weight_ref[h * width : (h + 1) * width, :],
             preferred_element_type=F32,
         )
@@ -98,7 +135,7 @@
     return pl.pallas_call(
         latent_kernel,
         out_shape=jax.ShapeDtypeStruct(base.shape, BF16),
-        compiler_params=pltpu.CompilerParams(vmem_limit_bytes=VMEM_LIMIT),
+        compiler_params=pltpu.CompilerParams(vmem_limit_bytes=56 * 1024 * 1024),
     )(piece, weight, base, gain)
 
 
@@ -107,9 +144,13 @@
     out_ref, held, centered, scale_ref, sems = rest[8:]
     rows, depth = text_ref.shape
     group, width = 64, 256
-    parts = len(weights)
-    block = weights[0].shape[0]
-    copies = [pltpu.make_async_copy(w, held.at[j], sems.at[j]) for j, w in enumerate(weights)]
+    block = depth // 4
+    copies = []
+    for j, weight in enumerate(weights):
+        size = weight.shape[0]
+        at = where[j // 2] * block + (j % 2) * (block - size)
+        to = held.at[pl.ds(pl.multiple_of(at, 256), size), :]
+        copies.append(pltpu.make_async_copy(weight, to, sems.at[j]))
     first = pl.program_id(0) == 0
 
     @pl.when(first)
@@ -138,12 +179,7 @@
         for copy in copies:
             copy.wait()
 
-    total = None
-    for j in range(parts):
-        at = (where[j // 2] * 2 + j % 2) * block
-        cols = pl.ds(pl.multiple_of(at, block), block)
-        term = jnp.dot(centered[:, cols], held[j], preferred_element_type=F32)
-        total = term if total is None else total + term
+    total = jnp.dot(centered[...], held[...], preferred_element_type=F32)
     out_ref[...] = (total * scale_ref[:, :1]).astype(BF16)
 
 
@@ -160,7 +196,7 @@
             + [pl.BlockSpec(memory_space=pl.ANY) for w in weights],
             out_specs=pl.BlockSpec((rows, cols), lambda i, w: (i, 0)),
             scratch_shapes=[
-                pltpu.VMEM((len(weights),) + weights[0].shape, BF16),
+                pltpu.VMEM((depth, cols), BF16),
                 pltpu.VMEM((rows, depth), BF16),
                 pltpu.VMEM((rows, 128), F32),
                 pltpu.SemaphoreType.DMA((len(weights),)),
@@ -295,63 +331,51 @@
     owned = frames.shape[0]
     groups = slots // owned
     width = res_query.shape[1]
-    res_scale = 1.0 / math.sqrt(RESAMPLE_HEAD_DIM)
 
     whole_text = lax.all_gather(text[0, 0], "mp", axis=1, tiled=True)
     media = norm_rows(frames.reshape(-1, E), norm_gains[:1]).reshape(frames.shape)
     half = owned // 2
-    ring_x = [ring(media[:half], "x"), ring(media[half:], "y")]
+    phase = [direct(media[:half], "x"), direct(media[half:], "y")]
+    joined_halves = [jnp.concatenate(blocks, axis=1) for blocks in phase]
+    joined_halves, w_kv, w_query = lax.optimization_barrier((joined_halves, w_kv, w_query))
     kv_local = jnp.concatenate([w_kv[0, :, 0], w_kv[0, :, 1]], axis=1)
     kv_across = over_z(kv_local)
-    depth = w_query.shape[1] // 2
-    gain = lax.dynamic_slice_in_dim(text_gain[0], dp * 2 * depth, 2 * depth, 0)
+    depth = w_query.shape[1]
+    early = depth * 3 // 8
+    gain = lax.dynamic_slice_in_dim(text_gain[0], dp * depth, depth, 0)
     scaled = (w_query[0].astype(F32) * gain.astype(F32)[:, None]).astype(BF16)
-    low_across = over_z(scaled[:depth])
-
-    lat_norm = layer_norm(latent_init, norm_gains[1]).astype(BF16)
-    res_pair = jnp.concatenate([res_kv[:, 0], res_kv[:, 1]], axis=1)
-    res_q = jnp.dot(lat_norm, res_query, preferred_element_type=F32).astype(BF16)
+    low_across = over_z(scaled[:early])
+
+    lat_rows = latent_init.reshape(groups, share, E).swapaxes(0, 1).reshape(LAT, E)
+    lat_norm = layer_norm(lat_rows, norm_gains[1]).astype(BF16)
+    pad = lambda a: jnp.pad(a, ((0, 0), (0, PAD - width)))
+    res_pair = jnp.concatenate([pad(res_kv[:, 0]), pad(res_kv[:, 1])], axis=1)
+    res_q = jnp.dot(lat_norm, pad(res_query), preferred_element_type=F32).astype(BF16)
     lat_pairs = jnp.dot(lat_norm, res_pair, preferred_element_type=F32).astype(BF16)
-    media_halves = []
-    joined_halves = [jnp.concatenate(blocks, axis=1) for blocks in ring_x]
-    joined_halves, kv_across = lax.optimization_barrier((joined_halves, kv_across))
+    pieces = []
     for joined, axis in zip(joined_halves, ("y", "x")):
-        parts = [
-            jnp.einsum("fpe,ec->fpc", block, res_pair, preferred_element_type=F32).astype(BF16)
-            for block in ring(joined, axis)
-        ]
-        media_halves.append(jnp.concatenate(parts, axis=1))
-    media_halves, low_across = lax.optimization_barrier((media_halves, low_across))
-    media_pairs = jnp.concatenate(media_halves, axis=0)
-    pair_list = jnp.concatenate(
-        [jnp.broadcast_to(lat_pairs, (owned,) + lat_pairs.shape), media_pairs], axis=1
-    )
-    score = (
-        jnp.einsum("ld,fpd->flp", res_q, pair_list[:, :, :width], preferred_element_type=F32)
-        * res_scale
-    )
-    weights = jnp.exp(score - jnp.max(score, axis=-1, keepdims=True))
-    blend = jnp.einsum(
-        "flp,fpd->fld", weights.astype(BF16), pair_list[:, :, width:], preferred_element_type=F32
-    )
-    res_context = (blend / jnp.sum(weights, axis=-1)[:, :, None]).astype(BF16)
-
-    piece = res_context.reshape(owned, groups, share * width).swapaxes(0, 1)
-    piece = lax.all_to_all(piece, GROUP, 0, 0, tiled=True).reshape(slots, share * width)
-    piece, query_rest = lax.optimization_barrier((piece, scaled[depth:]))
-    query_high = dp_blocks(query_rest, over_z(query_rest))
-    query_low = dp_blocks(scaled[:depth], low_across)
-    kv_blocks = dp_blocks(kv_local, kv_across)
+        for block in ring(joined, axis):
+            pieces.append(
+                jnp.einsum("fpe,ec->fpc", block, res_pair, preferred_element_type=F32).astype(BF16)
+            )
+    pieces, low_across, kv_across = lax.optimization_barrier((pieces, low_across, kv_across))
+    piece = resample(res_q, lat_pairs, pieces, slots, share)
+
+    piece = lax.all_to_all(
+        piece.reshape(groups, owned, share * PAD), GROUP, 0, 0, tiled=True
+    ).reshape(slots, share * PAD)
+    piece, query_rest = lax.optimization_barrier((piece, scaled[early:]))
+    high_across = over_z(query_rest)
     slot_ids = jnp.arange(slots, dtype=jnp.int32)
     target = (twice(group) ^ (slot_ids // owned)) * owned + slot_ids % owned
     to_dest = (frame_dest[None, :] == target[:, None]).astype(BF16)
     piece = jnp.dot(to_dest, piece, preferred_element_type=F32).astype(BF16)
     piece = lax.all_to_all(
-        piece.reshape(mp_count, owned, share * width), "mp", 0, 0, tiled=True
+        piece.reshape(mp_count, owned, share * PAD), "mp", 0, 0, tiled=True
     )
     base_rows = lax.dynamic_slice_in_dim(latent_init, group * share, share, 0).astype(F32)
     latents = latent_rows(
-        piece.reshape(slots, share * width),
+        piece.reshape(slots, share * PAD),
         res_out,
         jnp.repeat(base_rows, owned, axis=0),
         norm_gains[2:],
@@ -366,6 +390,11 @@
         ("segment", "mp", "dp"),
         [(place(g, m), place(twice(g) ^ m, m)) for g in range(groups) for m in range(mp_count)],
     )
+    crossed = (high_across, low_across, kv_across)
+    high_across, low_across, kv_across = lax.optimization_barrier((crossed, mine))[0]
+    query_high = dp_blocks(query_rest, high_across)
+    query_low = dp_blocks(scaled[:early], low_across)
+    kv_blocks = dp_blocks(kv_local, kv_across)
     dest = lax.all_to_all(
         jnp.broadcast_to(mine, (mp_count,) + mine.shape), "mp", 0, 0, tiled=True
     ).reshape(LAT * owned, E)

time: 235 us -> 238 us (1.013)
  waiting for transfers between devices: 31.2 us -> 42.4 us
  local copies, waits for them, and re-layouts: 19.1 us -> 10.4 us
  other arithmetic: 12.1 us -> 4.83 us
  Pallas kernels: 36 us -> 43.1 us
  blocking collectives: 51.2 us -> 55.3 us
  starting transfers between devices: 58.5 us -> 54.7 us
    ppermute x16 -> x14, waiting for transfers between devices: 5.3 us -> 10.9 us  [shift(): return lax.ppermute(value, 'mp', pairs)]
    dot_general x8, matrix products: 2.61 us -> 7.52 us  [per_device(): jnp.einsum('fpe,ec->fpc', block, res_pair, preferred_element_type=F32)]
    ppermute x3, starting transfers between devices: 5.04 us -> 0.84 us  [dp_blocks(): lax.ppermute(value, 'dp', mate)]
    dot_general x2 -> x1, matrix products: 4.91 us -> 0.83 us  [per_device(): jnp.dot(lat_norm, pad(res_query), preferred_element_type=F32).astype(BF16)]
    pallas_call x0 -> x1, Pallas kernels: none -> 3.98 us  [resample(): pl.pallas_call(resample_kernel, out_shape=jax.ShapeDtypeStruct((slots, sh...]
    ppermute x3, waiting for transfers between devices: 0.01 us -> 3.87 us  [over_z(): return lax.ppermute(value, 'dp', [(0, 2), (1, 3), (2, 0), (3, 1)])]
    ppermute x1, waiting for transfers between devices: 5.61 us -> 9.17 us  [per_device(): lax.ppermute(latents, ('segment', 'mp', 'dp'), [(place(g, m), place(twice...]
    ppermute x3, waiting for transfers between devices: 0.21 us -> 3.51 us  [dp_blocks(): lax.ppermute(across, 'dp', mate)]
  transfers between devices with their start and end apart: 30 -> 28, of which waited for: 8 -> 10; matrix products, arithmetic and copies ran while one was open for 14% -> 9% of each run, Pallas kernels for 8% -> 11%
where the time goes in v5:
time: 238 us; the launch traced here: 237 us
  blocking collectives  55.3 us (23%)
  starting transfers between devices  54.7 us (23%)
  Pallas kernels  43.1 us (18%)
  waiting for transfers between devices  42.4 us (18%)
  between operations  15.7 us (7%)
  local copies, waits for them, and re-layouts  10.4 us (4%)
  matrix products  10.3 us (4%)
  other arithmetic  4.83 us (2%)
    all_to_all x1, blocking collectives, per_device(): lax.all_to_all(part.reshape(mp_count, share * owned, E), 'mp', 0, 0, tile...  28.8 us
    ppermute x14, starting transfers between devices, shift(): return lax.ppermute(value, 'mp', pairs)  23.8 us
    pallas_call x1, Pallas kernels, query_matmul(): pl.pallas_call(query_kernel, grid_spec=pltpu.PrefetchScalarGridSpec(num_s...  16.8 us
    pallas_call x1, Pallas kernels, attention(): pl.pallas_call(attend_kernel, grid_spec=pltpu.PrefetchScalarGridSpec(num_...  16.3 us
    all_to_all x1, blocking collectives, per_device(): lax.all_to_all(send, GROUP, 0, 0, tiled=True).reshape(slots, E // cut)  15.6 us
    all_to_all x1, starting transfers between devices, per_device(): lax.all_to_all(piece.reshape(groups, owned, share * PAD), GROUP, 0, 0, ti...  14.5 us
    all_to_all x1, blocking collectives, per_device(): lax.all_to_all(send.reshape(groups, owned, E // cut), GROUP, 0, 0, tiled=...  10.9 us
    ppermute x14, waiting for transfers between devices, shift(): return lax.ppermute(value, 'mp', pairs)  10.9 us
  transfers between devices with their start and end apart: 28, of which 10 were waited for; matrix products, arithmetic and copies ran while one was open for 9% of the time, Pallas kernels for 11%

profile of v5, /device:TPU:1, one launch (start us, length us, event | category | flops | bytes accessed | tf_op | source)
XLA Modules:
  0.0 236.7 jit_solution(4207447112310140785)
XLA Ops:
  9.3 1.8 shard_map.149
  12.1 2.1 collective-permute-start
  26.0 3.3 %collective-permute-done.5 = bf16[4,8,1536]{2,1,0:T(8,128)(2,1)S(1)} collective-permute-done((bf16[4,8,1536]{2,1,0:T(8,128)(2,1)S(1)}, bf16[4,8,1536]{2,1,0:T(8,128)(2,1)S(1)}, u32[]{:S(2)}, u32[]{:S(2)}) %collective-permute-start.5) | collective-permute-done | bytes 98336 | tf_op jit(solution)/shard_map/ppermute | solution.py:40
  29.7 2.4 collective-permute-start.11
  32.1 2.7 %collective-permute-start.7 = (bf16[4,32,1536]{2,1,0:T(8,128)(2,1)S(1)}, bf16[4,32,1536]{2,1,0:T(8,128)(2,1)S(1)}, u32[]{:S(2)}, u32[]{:S(2)}) collective-permute-start(bf16[4,32,1536]{2,1,0:T(8,128)(2,1)S(1)} %pad_maximum_fusion.1), channel_id=1, source_target_pairs={{0,48},{4,52},{8,56},{12,60},{16,0},{20,4},{24,8},{28,12},{32,16},... | collective-permute-start | bytes 1179656 | tf_op jit(solution)/shard_map/ppermute | solution.py:40
  39.4 5.4 %collective-permute-done.10 = bf16[4,32,1536]{2,1,0:T(8,128)(2,1)S(1)} collective-permute-done((bf16[4,32,1536]{2,1,0:T(8,128)(2,1)S(1)}, bf16[4,32,1536]{2,1,0:T(8,128)(2,1)S(1)}, u32[]{:S(2)}, u32[]{:S(2)}) %collective-permute-start.10) | collective-permute-done | bytes 393248 | tf_op jit(solution)/shard_map/ppermute | solution.py:40
  47.3 3.4 %collective-permute-start.13 = (bf16[2,32,1536]{2,1,0:T(8,128)(2,1)S(1)}, bf16[2,32,1536]{2,1,0:T(8,128)(2,1)S(1)}, u32[]{:S(2)}, u32[]{:S(2)}) collective-permute-start(bf16[2,32,1536]{2,1,0:T(8,128)(2,1)S(1)} %slice.74), channel_id=1, source_target_pairs={{0,12},{4,0},{8,4},{12,8},{16,28},{20,16},{24,20},{28,24},{32,44},... | collective-permute-start | bytes 589832 | tf_op jit(solution)/shard_map/ppermute | solution.py:40
  54.4 3.4 %collective-permute-start.9 = (bf16[2,32,1536]{2,1,0:T(8,128)(2,1)S(1)}, bf16[2,32,1536]{2,1,0:T(8,128)(2,1)S(1)}, u32[]{:S(2)}, u32[]{:S(2)}) collective-permute-start(bf16[2,32,1536]{2,1,0:T(8,128)(2,1)S(1)} %slice.72), channel_id=1, source_target_pairs={{0,48},{4,52},{8,56},{12,60},{16,0},{20,4},{24,8},{28,12},{32,16},... | collective-permute-start | bytes 589832 | tf_op jit(solution)/shard_map/ppermute | solution.py:40
  62.2 3.9 %collective-permute-done.14.rest_4_ = bf16[768,512]{1,0:T(8,128)(2,1)} collective-permute-done((bf16[768,512]{1,0:T(8,128)(2,1)S(1)}, bf16[768,512]{1,0:T(8,128)(2,1)}, u32[]{:S(2)}, u32[]{:S(2)}) %collective-permute-start.14) | collective-permute-done | bytes 786464 | tf_op jit(solution)/shard_map/ppermute | solution.py:64
  66.0 4.0 %shard_map.150 = bf16[128,512]{1,0:T(8,128)(2,1)} custom-call(bf16[64,128]{1,0:T(8,128)(2,1)} %convolution_convert_fusion.11.q_ref, bf16[64,256]{1,0:T(8,128)(2,1)} %convolution_convert_fusion.10.lat_ref, bf16[4,32,256]{2,1,0:T(8,128)(2,1)} %convolution_convert_fusion.9.rest_0_, bf16[4,32,256]{2,1,0:T(8,128)(2,1)} %convolution_convert_fusion.8.rest_1_, ...), custom_call_target="tpu_custom_call" | custom-call | tf_op jit(solution)/shard_map/pallas_call | solution.py:109
  70.0 14.5 %all-to-all-start = ((bf16[16,8,512]{2,1,0:T(8,128)(2,1)}), bf16[16,8,512]{2,1,0:T(8,128)(2,1)S(1)}, u32[]{:S(2)}, u32[]{:S(2)}) async-start(bf16[16,8,512]{2,1,0:T(8,128)(2,1)} %bitcast.91), calls=%async_computation | async-start | bytes 262144 | tf_op jit(solution)/shard_map/all_to_all | solution.py:364
  86.0 7.8 %all-to-all-done = bf16[16,8,512]{2,1,0:T(8,128)(2,1)S(1)} async-done(((bf16[16,8,512]{2,1,0:T(8,128)(2,1)}), bf16[16,8,512]{2,1,0:T(8,128)(2,1)S(1)}, u32[]{:S(2)}, u32[]{:S(2)}) %all-to-all-start) | async-done | bytes 131104 | tf_op jit(solution)/shard_map/all_to_all | solution.py:364
  96.0 3.7 %all-to-all-start.1 = ((bf16[16,8,512]{2,1,0:T(8,128)(2,1)}), bf16[16,8,512]{2,1,0:T(8,128)(2,1)S(1)}, u32[]{:S(2)}, u32[]{:S(2)}) async-start(bf16[16,8,512]{2,1,0:T(8,128)(2,1)} %fusion.3), calls=%async_computation.1 | async-start | bytes 262144 | tf_op jit(solution)/shard_map/all_to_all | solution.py:373
  101.2 6.5 %all-to-all-done.1 = bf16[16,8,512]{2,1,0:T(8,128)(2,1)S(1)} async-done(((bf16[16,8,512]{2,1,0:T(8,128)(2,1)}), bf16[16,8,512]{2,1,0:T(8,128)(2,1)S(1)}, u32[]{:S(2)}, u32[]{:S(2)}) %all-to-all-start.1) | async-done | bytes 131104 | tf_op jit(solution)/shard_map/all_to_all | solution.py:373
  108.3 4.2 %shard_map.151 = bf16[32,1536]{1,0:T(8,128)(2,1)} custom-call(bf16[128,512]{1,0:T(8,128)(2,1)} %bitcast.89, bf16[1536,1536]{1,0:T(8,128)(2,1)} %weight_ref.1, f32[32,1536]{1,0:T(8,128)} %broadcast_bitcast_fusion.base_ref, bf16[1,1536]{1,0:T(2,128)(2,1)} %get-tuple-element.54.gain_ref), custom_call_target="tpu_custom_call" | custom-call | tf_op jit(solution)/shard_map/pallas_call | solution.py:135
  112.5 4.0 %collective-permute-start.16 = (bf16[32,1536]{1,0:T(8,128)(2,1)}, bf16[32,1536]{1,0:T(8,128)(2,1)S(1)}, u32[]{:S(2)}, u32[]{:S(2)}) collective-permute-start(bf16[32,1536]{1,0:T(8,128)(2,1)} %shard_map.151), channel_id=1, source_target_pairs={{0,0},{4,5},{8,10},{12,15},{16,80},{20,85},{24,90},{28,95},{32,160... | collective-permute-start | bytes 294920 | tf_op jit(solution)/shard_map/ppermute | solution.py:388
  116.6 9.2 %collective-permute-done.16 = bf16[32,1536]{1,0:T(8,128)(2,1)S(1)} collective-permute-done((bf16[32,1536]{1,0:T(8,128)(2,1)}, bf16[32,1536]{1,0:T(8,128)(2,1)S(1)}, u32[]{:S(2)}, u32[]{:S(2)}) %collective-permute-start.16) | collective-permute-done | bytes 98336 | tf_op jit(solution)/shard_map/ppermute | solution.py:388
  127.0 5.1 %all-to-all-start.2 = ((bf16[16,32,1536]{2,1,0:T(8,128)(2,1)}), bf16[16,32,1536]{2,1,0:T(8,128)(2,1)}, u32[]{:S(2)}, u32[]{:S(2)}) async-start(bf16[16,32,1536]{2,1,0:T(8,128)(2,1)} %broadcast_in_dim.7), calls=%async_computation.2 | async-start | bytes 3145728 | tf_op jit(solution)/shard_map/all_to_all | solution.py:398
  135.8 2.2 collective-permute-done.20.rest_6_
  139.3 16.8 %shard_map.152.q_ref = bf16[768,512]{1,0:T(8,128)(2,1)S(1)} custom-call(s32[4]{0:T(128)S(1)} %pad_add_fusion.where, bf16[768,8192]{1,0:T(8,128)(2,1)} %bitcast.85, bf16[768,512]{1,0:T(8,128)(2,1)S(1)} %slice.75.rest_0_, bf16[1280,512]{1,0:T(8,128)(2,1)S(1)} %slice.78.rest_1_, bf16[768,512]{1,0:T(8,128)(2,1)} %collective-permute-done.17.rest_2_, ...), custom_call_target="tpu_custom_call" | custom-call | tf_op jit(solution)/shard_map/pallas_call | solution.py:190
  157.1 16.3 %shard_map.153 = (bf16[768,512]{1,0:T(8,128)(2,1)}, bf16[512,1536]{1,0:T(8,128)(2,1)}) custom-call(s32[1]{0:T(128)} %bitcast.84.count, s32[16]{0:T(128)} %multiply_xor_fusion.order, s32[4]{0:T(128)} %copy-done.1, f32[1]{0:T(128)S(6)} %tanh.3.gate_ref, bf16[768,512]{1,0:T(8,128)(2,1)} %copy-done, bf16[768,512]{1,0:T(8,128)(2,1)} %bitcast.88, ...), custom_call_target="tpu_custom_call" | custom-call | tf_op jit(solution)/shard_map/pallas_call | solution.py:286
  173.4 28.8 %all_to_all.30 = bf16[16,32,1536]{2,1,0:T(8,128)(2,1)S(1)} all-to-all(bf16[16,32,1536]{2,1,0:T(8,128)(2,1)} %bitcast.87), channel_id=1, replica_groups=mesh['segment'=4,'mp'=16,'dp'=4] {'mp'}, dimensions={0} | all-to-all | bytes 3145728 | tf_op jit(solution)/shard_map/all_to_all | solution.py:411
  202.4 15.6 %all_to_all.31 = bf16[16,8,384]{2,1,0:T(8,128)(2,1)S(1)} all-to-all(bf16[16,8,384]{2,1,0:T(8,128)(2,1)S(1)} %bitcast.92), channel_id=1, replica_groups=mesh['segment'=4,'mp'=16,'dp'=4] {'segment','dp'}, dimensions={0} | all-to-all | bytes 196608 | tf_op jit(solution)/shard_map/all_to_all | solution.py:419
  218.2 10.9 %all_to_all.32 = bf16[16,8,384]{2,1,0:T(8,128)(2,1)S(1)} all-to-all(bf16[16,8,384]{2,1,0:T(8,128)(2,1)S(1)} %fusion.4), channel_id=1, replica_groups=mesh['segment'=4,'mp'=16,'dp'=4] {'segment','dp'}, dimensions={0} | all-to-all | bytes 196608 | tf_op jit(solution)/shard_map/all_to_all | solution.py:422
  (117 shorter events, 43.1 us)
Async XLA Ops:
  7.2 132.2 %all-gather.3.cloned.1.call-start = ((), (), s32[]{:S(2)}) async-start(), calls=%async_computation.6 | async-start | bytes 13369344 | tf_op jit(solution)/shard_map/all_gather | solution.py:335
  12.1 12.1 %collective-permute-start = (bf16[4,8,1536]{2,1,0:T(8,128)(2,1)S(1)}, bf16[4,8,1536]{2,1,0:T(8,128)(2,1)S(1)}, u32[]{:S(2)}, u32[]{:S(2)}) collective-permute-start(bf16[4,8,1536]{2,1,0:T(8,128)(2,1)S(1)} %get-tuple-element.53), channel_id=1, source_target_pairs={{0,4},{4,8},{8,12},{12,0},{16,20},{20,24},{24,28},{28,16},{32,36},... | collective-permute-start | bytes 294920 | tf_op jit(solution)/shard_map/ppermute | solution.py:40
  14.3 11.7 %collective-permute-start.1 = (bf16[4,8,1536]{2,1,0:T(8,128)(2,1)S(1)}, bf16[4,8,1536]{2,1,0:T(8,128)(2,1)S(1)}, u32[]{:S(2)}, u32[]{:S(2)}) collective-permute-start(bf16[4,8,1536]{2,1,0:T(8,128)(2,1)S(1)} %get-tuple-element.53), channel_id=1, source_target_pairs={{0,12},{4,0},{8,4},{12,8},{16,28},{20,16},{24,20},{28,24},{32,44},... | collective-permute-start | bytes 294920 | tf_op jit(solution)/shard_map/ppermute | solution.py:40
  15.6 10.3 %collective-permute-start.2 = (bf16[4,8,1536]{2,1,0:T(8,128)(2,1)S(1)}, bf16[4,8,1536]{2,1,0:T(8,128)(2,1)S(1)}, u32[]{:S(2)}, u32[]{:S(2)}) collective-permute-start(bf16[4,8,1536]{2,1,0:T(8,128)(2,1)S(1)} %get-tuple-element.53), channel_id=1, source_target_pairs={{0,8},{4,12},{8,0},{12,4},{16,24},{20,28},{24,16},{28,20},{32,40},... | collective-permute-start | bytes 294920 | tf_op jit(solution)/shard_map/ppermute | solution.py:40
  17.3 8.7 %collective-permute-start.3 = (bf16[4,8,1536]{2,1,0:T(8,128)(2,1)S(1)}, bf16[4,8,1536]{2,1,0:T(8,128)(2,1)S(1)}, u32[]{:S(2)}, u32[]{:S(2)}) collective-permute-start(bf16[4,8,1536]{2,1,0:T(8,128)(2,1)S(1)} %get-tuple-element.52), channel_id=1, source_target_pairs={{0,16},{4,20},{8,24},{12,28},{16,32},{20,36},{24,40},{28,44},{32,4... | collective-permute-start | bytes 294920 | tf_op jit(solution)/shard_map/ppermute | solution.py:40
  18.6 7.4 %collective-permute-start.4 = (bf16[4,8,1536]{2,1,0:T(8,128)(2,1)S(1)}, bf16[4,8,1536]{2,1,0:T(8,128)(2,1)S(1)}, u32[]{:S(2)}, u32[]{:S(2)}) collective-permute-start(bf16[4,8,1536]{2,1,0:T(8,128)(2,1)S(1)} %get-tuple-element.52), channel_id=1, source_target_pairs={{0,48},{4,52},{8,56},{12,60},{16,0},{20,4},{24,8},{28,12},{32,16},... | collective-permute-start | bytes 294920 | tf_op jit(solution)/shard_map/ppermute | solution.py:40
  29.3 15.6 %collective-permute-start.10 = (bf16[4,32,1536]{2,1,0:T(8,128)(2,1)S(1)}, bf16[4,32,1536]{2,1,0:T(8,128)(2,1)S(1)}, u32[]{:S(2)}, u32[]{:S(2)}) collective-permute-start(bf16[4,32,1536]{2,1,0:T(8,128)(2,1)S(1)} %pad_maximum_fusion.2), channel_id=1, source_target_pairs={{0,4},{4,8},{8,12},{12,0},{16,20},{20,24},{24,28},{28,16},{32,36},... | collective-permute-start | bytes 1179656 | tf_op jit(solution)/shard_map/ppermute | solution.py:40
  29.7 16.1 %collective-permute-start.11 = (bf16[4,32,1536]{2,1,0:T(8,128)(2,1)S(1)}, bf16[4,32,1536]{2,1,0:T(8,128)(2,1)S(1)}, u32[]{:S(2)}, u32[]{:S(2)}) collective-permute-start(bf16[4,32,1536]{2,1,0:T(8,128)(2,1)S(1)} %pad_maximum_fusion.2), channel_id=1, source_target_pairs={{0,12},{4,0},{8,4},{12,8},{16,28},{20,16},{24,20},{28,24},{32,44},... | collective-permute-start | bytes 1179656 | tf_op jit(solution)/shard_map/ppermute | solution.py:40
  32.0 15.3 %collective-permute-start.6 = (bf16[4,32,1536]{2,1,0:T(8,128)(2,1)S(1)}, bf16[4,32,1536]{2,1,0:T(8,128)(2,1)S(1)}, u32[]{:S(2)}, u32[]{:S(2)}) collective-permute-start(bf16[4,32,1536]{2,1,0:T(8,128)(2,1)S(1)} %pad_maximum_fusion.1), channel_id=1, source_target_pairs={{0,16},{4,20},{8,24},{12,28},{16,32},{20,36},{24,40},{28,44},{32,4... | collective-permute-start | bytes 1179656 | tf_op jit(solution)/shard_map/ppermute | solution.py:40
  32.1 18.7 %collective-permute-start.7 = (bf16[4,32,1536]{2,1,0:T(8,128)(2,1)S(1)}, bf16[4,32,1536]{2,1,0:T(8,128)(2,1)S(1)}, u32[]{:S(2)}, u32[]{:S(2)}) collective-permute-start(bf16[4,32,1536]{2,1,0:T(8,128)(2,1)S(1)} %pad_maximum_fusion.1), channel_id=1, source_target_pairs={{0,48},{4,52},{8,56},{12,60},{16,0},{20,4},{24,8},{28,12},{32,16},... | collective-permute-start | bytes 1179656 | tf_op jit(solution)/shard_map/ppermute | solution.py:40
  35.0 26.3 %collective-permute-start.15 = (bf16[384,1024]{1,0:T(8,128)(2,1)S(1)}, bf16[384,1024]{1,0:T(8,128)(2,1)S(1)}, u32[]{:S(2)}, u32[]{:S(2)}) collective-permute-start(bf16[384,1024]{1,0:T(8,128)(2,1)S(1)} %pad_maximum_fusion.kv0), channel_id=1, source_target_pairs={{0,2},{1,3},{2,0},{3,1},{4,6},{5,7},{6,4},{7,5},{8,10},{9,11},{10,... | collective-permute-start | bytes 2359304 | tf_op jit(solution)/shard_map/ppermute | solution.py:64
  44.9 21.2 %collective-permute-start.14 = (bf16[768,512]{1,0:T(8,128)(2,1)S(1)}, bf16[768,512]{1,0:T(8,128)(2,1)}, u32[]{:S(2)}, u32[]{:S(2)}) collective-permute-start(bf16[768,512]{1,0:T(8,128)(2,1)S(1)} %slice.75.rest_0_), channel_id=1, source_target_pairs={{0,2},{1,3},{2,0},{3,1},{4,6},{5,7},{6,4},{7,5},{8,10},{9,11},{10,... | collective-permute-start | bytes 2359304 | tf_op jit(solution)/shard_map/ppermute | solution.py:64
  45.8 8.6 %collective-permute-start.12 = (bf16[2,32,1536]{2,1,0:T(8,128)(2,1)S(1)}, bf16[2,32,1536]{2,1,0:T(8,128)(2,1)S(1)}, u32[]{:S(2)}, u32[]{:S(2)}) collective-permute-start(bf16[2,32,1536]{2,1,0:T(8,128)(2,1)S(1)} %slice.73), channel_id=1, source_target_pairs={{0,4},{4,8},{8,12},{12,0},{16,20},{20,24},{24,28},{28,16},{32,36},... | collective-permute-start | bytes 589832 | tf_op jit(solution)/shard_map/ppermute | solution.py:40
  47.3 11.3 %collective-permute-start.13 = (bf16[2,32,1536]{2,1,0:T(8,128)(2,1)S(1)}, bf16[2,32,1536]{2,1,0:T(8,128)(2,1)S(1)}, u32[]{:S(2)}, u32[]{:S(2)}) collective-permute-start(bf16[2,32,1536]{2,1,0:T(8,128)(2,1)S(1)} %slice.74), channel_id=1, source_target_pairs={{0,12},{4,0},{8,4},{12,8},{16,28},{20,16},{24,20},{28,24},{32,44},... | collective-permute-start | bytes 589832 | tf_op jit(solution)/shard_map/ppermute | solution.py:40
  50.8 8.8 %collective-permute-start.8 = (bf16[2,32,1536]{2,1,0:T(8,128)(2,1)S(1)}, bf16[2,32,1536]{2,1,0:T(8,128)(2,1)S(1)}, u32[]{:S(2)}, u32[]{:S(2)}) collective-permute-start(bf16[2,32,1536]{2,1,0:T(8,128)(2,1)S(1)} %slice.71), channel_id=1, source_target_pairs={{0,16},{4,20},{8,24},{12,28},{16,32},{20,36},{24,40},{28,44},{32,4... | collective-permute-start | bytes 589832 | tf_op jit(solution)/shard_map/ppermute | solution.py:40
  70.0 23.7 %all-to-all-start = ((bf16[16,8,512]{2,1,0:T(8,128)(2,1)}), bf16[16,8,512]{2,1,0:T(8,128)(2,1)S(1)}, u32[]{:S(2)}, u32[]{:S(2)}) async-start(bf16[16,8,512]{2,1,0:T(8,128)(2,1)} %bitcast.91), calls=%async_computation | async-start | bytes 262144 | tf_op jit(solution)/shard_map/all_to_all | solution.py:364
  93.7 39.1 %collective-permute-start.19 = (bf16[1280,512]{1,0:T(8,128)(2,1)S(1)}, bf16[1280,512]{1,0:T(8,128)(2,1)S(1)}, u32[]{:S(2)}, u32[]{:S(2)}) collective-permute-start(bf16[1280,512]{1,0:T(8,128)(2,1)S(1)} %slice.78.rest_1_), channel_id=1, source_target_pairs={{0,2},{1,3},{2,0},{3,1},{4,6},{5,7},{6,4},{7,5},{8,10},{9,11},{10,... | collective-permute-start | bytes 3932168 | tf_op jit(solution)/shard_map/ppermute | solution.py:64
  96.0 11.6 %all-to-all-start.1 = ((bf16[16,8,512]{2,1,0:T(8,128)(2,1)}), bf16[16,8,512]{2,1,0:T(8,128)(2,1)S(1)}, u32[]{:S(2)}, u32[]{:S(2)}) async-start(bf16[16,8,512]{2,1,0:T(8,128)(2,1)} %fusion.3), calls=%async_computation.1 | async-start | bytes 262144 | tf_op jit(solution)/shard_map/all_to_all | solution.py:373
  112.5 13.3 %collective-permute-start.16 = (bf16[32,1536]{1,0:T(8,128)(2,1)}, bf16[32,1536]{1,0:T(8,128)(2,1)S(1)}, u32[]{:S(2)}, u32[]{:S(2)}) collective-permute-start(bf16[32,1536]{1,0:T(8,128)(2,1)} %shard_map.151), channel_id=1, source_target_pairs={{0,0},{4,5},{8,10},{12,15},{16,80},{20,85},{24,90},{28,95},{32,160... | collective-permute-start | bytes 294920 | tf_op jit(solution)/shard_map/ppermute | solution.py:388
  116.5 17.0 %collective-permute-start.17 = (bf16[768,512]{1,0:T(8,128)(2,1)S(1)}, bf16[768,512]{1,0:T(8,128)(2,1)}, u32[]{:S(2)}, u32[]{:S(2)}) collective-permute-start(bf16[768,512]{1,0:T(8,128)(2,1)S(1)} %slice.75.rest_0_), channel_id=1, source_target_pairs={{0,1},{1,0},{2,3},{3,2},{4,5},{5,4},{6,7},{7,6},{8,9},{9,8},{10,11... | collective-permute-start | bytes 2359304 | tf_op jit(solution)/shard_map/ppermute | solution.py:69
  127.0 30.0 %all-to-all-start.2 = ((bf16[16,32,1536]{2,1,0:T(8,128)(2,1)}), bf16[16,32,1536]{2,1,0:T(8,128)(2,1)}, u32[]{:S(2)}, u32[]{:S(2)}) async-start(bf16[16,32,1536]{2,1,0:T(8,128)(2,1)} %broadcast_in_dim.7), calls=%async_computation.2 | async-start | bytes 3145728 | tf_op jit(solution)/shard_map/all_to_all | solution.py:398
  132.8 6.5 %collective-permute-start.21 = (bf16[1280,512]{1,0:T(8,128)(2,1)S(1)}, bf16[1280,512]{1,0:T(8,128)(2,1)}, u32[]{:S(2)}, u32[]{:S(2)}) collective-permute-start(bf16[1280,512]{1,0:T(8,128)(2,1)S(1)} %collective-permute-done.19.rest_5_), channel_id=1, source_target_pairs={{0,1},{1,0},{2,3},{3,2},{4,5},{5,4},{6,7},{7,6},{8,9},{9,8},{10,11... | collective-permute-start | bytes 3932168 | tf_op jit(solution)/shard_map/ppermute | solution.py:69
  133.3 23.7 %collective-permute-start.22 = (bf16[384,1024]{1,0:T(8,128)(2,1)}, bf16[384,1024]{1,0:T(8,128)(2,1)}, u32[]{:S(2)}, u32[]{:S(2)}) collective-permute-start(bf16[384,1024]{1,0:T(8,128)(2,1)} %copy-done.3), channel_id=1, source_target_pairs={{0,1},{1,0},{2,3},{3,2},{4,5},{5,4},{6,7},{7,6},{8,9},{9,8},{10,11... | collective-permute-start | bytes 2359304 | tf_op jit(solution)/shard_map/ppermute | solution.py:69
  133.4 23.6 %collective-permute-start.23 = (bf16[384,1024]{1,0:T(8,128)(2,1)}, bf16[384,1024]{1,0:T(8,128)(2,1)}, u32[]{:S(2)}, u32[]{:S(2)}) collective-permute-start(bf16[384,1024]{1,0:T(8,128)(2,1)} %copy-done.6), channel_id=1, source_target_pairs={{0,1},{1,0},{2,3},{3,2},{4,5},{5,4},{6,7},{7,6},{8,9},{9,8},{10,11... | collective-permute-start | bytes 2359304 | tf_op jit(solution)/shard_map/ppermute | solution.py:69
  (17 other events, 109.2 us)
Sparse Core Ops, SparseCore 0:
  10.4 114.3 all-gather.2

commit v6 on v5

--- a/solution.py
+++ b/solution.py
@@ -64,9 +64,12 @@
     return lax.ppermute(value, "dp", [(0, 2), (1, 3), (2, 0), (3, 1)])
 
 
+def core_swap(value):
+    return lax.ppermute(value, "dp", [(0, 1), (1, 0), (2, 3), (3, 2)])
+
+
 def dp_blocks(value, across):
-    mate = [(0, 1), (1, 0), (2, 3), (3, 2)]
-    return [value, lax.ppermute(value, "dp", mate), across, lax.ppermute(across, "dp", mate)]
+    return [value, core_swap(value), across, core_swap(across)]
 
 
 def norm_kernel(value_ref, gain_ref, out_ref):
@@ -139,17 +142,19 @@
     )(piece, weight, base, gain)
 
 
-def query_kernel(where, text_ref, *rest):
-    weights = rest[:8]
-    out_ref, held, centered, scale_ref, sems = rest[8:]
+def query_kernel(where, text_ref, gain_ref, *rest):
+    weights = rest[:-5]
+    out_ref, held, centered, scale_ref, sems = rest[-5:]
     rows, depth = text_ref.shape
     group, width = 64, 256
     block = depth // 4
     copies = []
+    filled = 0
     for j, weight in enumerate(weights):
         size = weight.shape[0]
-        at = where[j // 2] * block + (j % 2) * (block - size)
-        to = held.at[pl.ds(pl.multiple_of(at, 256), size), :]
+        at = where[filled // block] * block + filled % block
+        filled += size
+        to = held.at[pl.ds(pl.multiple_of(at, 512), size), :]
         copies.append(pltpu.make_async_copy(weight, to, sems.at[j]))
     first = pl.program_id(0) == 0
 
@@ -169,7 +174,7 @@
         for c in range(depth // width):
             cols = slice(c * width, (c + 1) * width)
             off = text_ref[at, cols].astype(F32) - mean
-            centered[at, cols] = off.astype(BF16)
+            centered[at, cols] = (off * gain_ref[:, cols].astype(F32)).astype(BF16)
             square += off * off
         spread = jnp.sum(square, axis=1, keepdims=True) * (1.0 / depth)
         scale_ref[at, :] = jnp.broadcast_to(lax.rsqrt(spread + 1e-05), (group, 128))
@@ -183,7 +188,7 @@
     out_ref[...] = (total * scale_ref[:, :1]).astype(BF16)
 
 
-def query_matmul(text, weights, where):
+def query_matmul(text, gain, weights, where):
     tokens, depth = text.shape
     cols = weights[0].shape[1]
     rows = 256
@@ -192,7 +197,10 @@
         grid_spec=pltpu.PrefetchScalarGridSpec(
             num_scalar_prefetch=1,
             grid=(tokens // rows,),
-            in_specs=[pl.BlockSpec((rows, depth), lambda i, w: (i, 0))]
+            in_specs=[
+                pl.BlockSpec((rows, depth), lambda i, w: (i, 0)),
+                pl.BlockSpec((1, depth), lambda i, w: (0, 0)),
+            ]
             + [pl.BlockSpec(memory_space=pl.ANY) for w in weights],
             out_specs=pl.BlockSpec((rows, cols), lambda i, w: (i, 0)),
             scratch_shapes=[
@@ -204,7 +212,7 @@
         ),
         out_shape=jax.ShapeDtypeStruct((tokens, cols), BF16),
         compiler_params=pltpu.CompilerParams(vmem_limit_bytes=VMEM_LIMIT),
-    )(where, text, *weights)
+    )(where, text, gain, *weights)
 
 
 def attend_kernel(
@@ -337,14 +345,12 @@
     half = owned // 2
     phase = [direct(media[:half], "x"), direct(media[half:], "y")]
     joined_halves = [jnp.concatenate(blocks, axis=1) for blocks in phase]
-    joined_halves, w_kv, w_query = lax.optimization_barrier((joined_halves, w_kv, w_query))
+    early = w_query.shape[1] // 4
+    low_across = over_z(w_query[0, :early])
+    high_across = over_z(w_query[0, early:])
+    joined_halves, low_across = lax.optimization_barrier((joined_halves, low_across))
+    joined_halves, w_kv = lax.optimization_barrier((joined_halves, w_kv))
     kv_local = jnp.concatenate([w_kv[0, :, 0], w_kv[0, :, 1]], axis=1)
-    kv_across = over_z(kv_local)
-    depth = w_query.shape[1]
-    early = depth * 3 // 8
-    gain = lax.dynamic_slice_in_dim(text_gain[0], dp * depth, depth, 0)
-    scaled = (w_query[0].astype(F32) * gain.astype(F32)[:, None]).astype(BF16)
-    low_across = over_z(scaled[:early])
 
     lat_rows = latent_init.reshape(groups, share, E).swapaxes(0, 1).reshape(LAT, E)
     lat_norm = layer_norm(lat_rows, norm_gains[1]).astype(BF16)
@@ -358,14 +364,17 @@
             pieces.append(
                 jnp.einsum("fpe,ec->fpc", block, res_pair, preferred_element_type=F32).astype(BF16)
             )
-    pieces, low_across, kv_across = lax.optimization_barrier((pieces, low_across, kv_across))
+    pieces, high_across, kv_local = lax.optimization_barrier((pieces, high_across, kv_local))
     piece = resample(res_q, lat_pairs, pieces, slots, share)
 
     piece = lax.all_to_all(
         piece.reshape(groups, owned, share * PAD), GROUP, 0, 0, tiled=True
     ).reshape(slots, share * PAD)
-    piece, query_rest = lax.optimization_barrier((piece, scaled[early:]))
-    high_across = over_z(query_rest)
+    crossed = (low_across, high_across)
+    piece, crossed, kv_local = lax.optimization_barrier((piece, crossed, kv_local))
+    query_blocks = [w_query[0], core_swap(w_query[0]), *crossed]
+    query_blocks += [core_swap(w) for w in crossed]
+    kv_across = over_z(kv_local)
     slot_ids = jnp.arange(slots, dtype=jnp.int32)
     target = (twice(group) ^ (slot_ids // owned)) * owned + slot_ids % owned
     to_dest = (frame_dest[None, :] == target[:, None]).astype(BF16)
@@ -380,6 +389,7 @@
         jnp.repeat(base_rows, owned, axis=0),
         norm_gains[2:],
     )
+    latents, kv_across = lax.optimization_barrier((latents, kv_across))
     dp_count = lax.axis_size("dp")
 
     def place(g, m):
@@ -390,10 +400,7 @@
         ("segment", "mp", "dp"),
         [(place(g, m), place(twice(g) ^ m, m)) for g in range(groups) for m in range(mp_count)],
     )
-    crossed = (high_across, low_across, kv_across)
-    high_across, low_across, kv_across = lax.optimization_barrier((crossed, mine))[0]
-    query_high = dp_blocks(query_rest, high_across)
-    query_low = dp_blocks(scaled[:early], low_across)
+    kv_across = lax.optimization_barrier((kv_across, mine))[0]
     kv_blocks = dp_blocks(kv_local, kv_across)
     dest = lax.all_to_all(
         jnp.broadcast_to(mine, (mp_count,) + mine.shape), "mp", 0, 0, tiled=True
@@ -401,8 +408,7 @@
     order = halved(group ^ jnp.arange(mp_count, dtype=jnp.int32))
 
     where = jnp.stack([dp, dp ^ 1, dp ^ 2, dp ^ 3]).astype(jnp.int32)
-    query_blocks = [w for both in zip(query_low, query_high) for w in both]
-    query = query_matmul(whole_text, query_blocks, where)
+    query = query_matmul(whole_text, text_gain, query_blocks, where)
     dest, query = lax.optimization_barrier((dest, query))
     context, part = attention(
         query, dest, kv_blocks, cotangent[0, 0], frame_counts[0], order, where, jnp.tanh(xgate)

time: 238 us -> 233 us (0.979)
  starting transfers between devices: 54.7 us -> 47.7 us
    all_to_all x1, starting transfers between devices: 14.5 us -> 10.4 us  [per_device(): lax.all_to_all(piece.reshape(groups, owned, share * PAD), GROUP, 0, 0, ti...]
    all_to_all x1, blocking collectives: 15.6 us -> 18.7 us  [per_device(): lax.all_to_all(send, GROUP, 0, 0, tiled=True).reshape(slots, E // cut)]
    ppermute x3, waiting for transfers between devices: 3.87 us -> 1.14 us  [over_z(): return lax.ppermute(value, 'dp', [(0, 2), (1, 3), (2, 0), (3, 1)])]
  transfers between devices with their start and end apart: 28 -> 27, of which waited for: 10 -> 10; matrix products, arithmetic and copies ran while one was open for 9% -> 10% of each run, Pallas kernels for 11% -> 12%
where the time goes in v6:
time: 233 us; the launch traced here: 232 us
  blocking collectives  56.3 us (24%)
  starting transfers between devices  47.7 us (20%)
  Pallas kernels  43.3 us (19%)
  waiting for transfers between devices  41.7 us (18%)
  between operations  15.7 us (7%)
  matrix products  11.4 us (5%)
  local copies, waits for them, and re-layouts  10.7 us (5%)
  other arithmetic  5.1 us (2%)
    all_to_all x1, blocking collectives, per_device(): lax.all_to_all(part.reshape(mp_count, share * owned, E), 'mp', 0, 0, tile...  26.7 us
    ppermute x14, starting transfers between devices, shift(): return lax.ppermute(value, 'mp', pairs)  21.8 us
    all_to_all x1, blocking collectives, per_device(): lax.all_to_all(send, GROUP, 0, 0, tiled=True).reshape(slots, E // cut)  18.7 us
    pallas_call x1, Pallas kernels, query_matmul(): pl.pallas_call(query_kernel, grid_spec=pltpu.PrefetchScalarGridSpec(num_s...  17.2 us
    pallas_call x1, Pallas kernels, attention(): pl.pallas_call(attend_kernel, grid_spec=pltpu.PrefetchScalarGridSpec(num_...  16.3 us
    ppermute x14, waiting for transfers between devices, shift(): return lax.ppermute(value, 'mp', pairs)  12.4 us
    all_to_all x1, blocking collectives, per_device(): lax.all_to_all(send.reshape(groups, owned, E // cut), GROUP, 0, 0, tiled=...  10.9 us
    all_to_all x1, starting transfers between devices, per_device(): lax.all_to_all(piece.reshape(groups, owned, share * PAD), GROUP, 0, 0, ti...  10.4 us
  transfers between devices with their start and end apart: 27, of which 10 were waited for; matrix products, arithmetic and copies ran while one was open for 10% of the time, Pallas kernels for 12%

profile of v6, /device:TPU:1, one launch (start us, length us, event | category | flops | bytes accessed | tf_op | source)
XLA Modules:
  0.0 231.9 jit_solution(1056362018117044073)
XLA Ops:
  9.3 1.8 shard_map.149
  12.1 2.1 collective-permute-start
  24.4 2.1 convolution_convert_fusion.10.lat_ref
  34.1 3.0 %collective-permute-done.5 = bf16[4,8,1536]{2,1,0:T(8,128)(2,1)S(1)} collective-permute-done((bf16[4,8,1536]{2,1,0:T(8,128)(2,1)S(1)}, bf16[4,8,1536]{2,1,0:T(8,128)(2,1)S(1)}, u32[]{:S(2)}, u32[]{:S(2)}) %collective-permute-start.5) | collective-permute-done | bytes 98336 | tf_op jit(solution)/shard_map/ppermute | solution.py:40
  38.4 2.5 %collective-permute-start.12 = (bf16[4,32,1536]{2,1,0:T(8,128)(2,1)S(1)}, bf16[4,32,1536]{2,1,0:T(8,128)(2,1)S(1)}, u32[]{:S(2)}, u32[]{:S(2)}) collective-permute-start(bf16[4,32,1536]{2,1,0:T(8,128)(2,1)S(1)} %pad_maximum_fusion.2), channel_id=1, source_target_pairs={{0,12},{4,0},{8,4},{12,8},{16,28},{20,16},{24,20},{28,24},{32,44},... | collective-permute-start | bytes 1179656 | tf_op jit(solution)/shard_map/ppermute | solution.py:40
  40.9 3.2 %collective-permute-start.8 = (bf16[4,32,1536]{2,1,0:T(8,128)(2,1)S(1)}, bf16[4,32,1536]{2,1,0:T(8,128)(2,1)S(1)}, u32[]{:S(2)}, u32[]{:S(2)}) collective-permute-start(bf16[4,32,1536]{2,1,0:T(8,128)(2,1)S(1)} %pad_maximum_fusion.1), channel_id=1, source_target_pairs={{0,48},{4,52},{8,56},{12,60},{16,0},{20,4},{24,8},{28,12},{32,16},... | collective-permute-start | bytes 1179656 | tf_op jit(solution)/shard_map/ppermute | solution.py:40
  47.2 6.5 %collective-permute-done.11 = bf16[4,32,1536]{2,1,0:T(8,128)(2,1)S(1)} collective-permute-done((bf16[4,32,1536]{2,1,0:T(8,128)(2,1)S(1)}, bf16[4,32,1536]{2,1,0:T(8,128)(2,1)S(1)}, u32[]{:S(2)}, u32[]{:S(2)}) %collective-permute-start.11) | collective-permute-done | bytes 393248 | tf_op jit(solution)/shard_map/ppermute | solution.py:40
  53.8 3.0 %collective-permute-start.14 = (bf16[2,32,1536]{2,1,0:T(8,128)(2,1)S(1)}, bf16[2,32,1536]{2,1,0:T(8,128)(2,1)S(1)}, u32[]{:S(2)}, u32[]{:S(2)}) collective-permute-start(bf16[2,32,1536]{2,1,0:T(8,128)(2,1)S(1)} %slice.73), channel_id=1, source_target_pairs={{0,12},{4,0},{8,4},{12,8},{16,28},{20,16},{24,20},{28,24},{32,44},... | collective-permute-start | bytes 589832 | tf_op jit(solution)/shard_map/ppermute | solution.py:40
  56.8 3.1 %collective-permute-start.10 = (bf16[2,32,1536]{2,1,0:T(8,128)(2,1)S(1)}, bf16[2,32,1536]{2,1,0:T(8,128)(2,1)S(1)}, u32[]{:S(2)}, u32[]{:S(2)}) collective-permute-start(bf16[2,32,1536]{2,1,0:T(8,128)(2,1)S(1)} %slice.71), channel_id=1, source_target_pairs={{0,48},{4,52},{8,56},{12,60},{16,0},{20,4},{24,8},{28,12},{32,16},... | collective-permute-start | bytes 589832 | tf_op jit(solution)/shard_map/ppermute | solution.py:40
  66.7 4.0 %shard_map.150 = bf16[128,512]{1,0:T(8,128)(2,1)} custom-call(bf16[64,128]{1,0:T(8,128)(2,1)} %convolution_convert_fusion.11.q_ref, bf16[64,256]{1,0:T(8,128)(2,1)} %convolution_convert_fusion.10.lat_ref, bf16[4,32,256]{2,1,0:T(8,128)(2,1)} %convolution_convert_fusion.9.rest_0_, bf16[4,32,256]{2,1,0:T(8,128)(2,1)} %convolution_convert_fusion.8.rest_1_, ...), custom_call_target="tpu_custom_call" | custom-call | tf_op jit(solution)/shard_map/pallas_call | solution.py:112
  70.7 10.4 %all-to-all-start = ((bf16[16,8,512]{2,1,0:T(8,128)(2,1)}), bf16[16,8,512]{2,1,0:T(8,128)(2,1)S(1)}, u32[]{:S(2)}, u32[]{:S(2)}) async-start(bf16[16,8,512]{2,1,0:T(8,128)(2,1)} %bitcast.94), calls=%async_computation | async-start | bytes 262144 | tf_op jit(solution)/shard_map/all_to_all | solution.py:370
  81.3 9.0 %all-to-all-done = bf16[16,8,512]{2,1,0:T(8,128)(2,1)S(1)} async-done(((bf16[16,8,512]{2,1,0:T(8,128)(2,1)}), bf16[16,8,512]{2,1,0:T(8,128)(2,1)S(1)}, u32[]{:S(2)}, u32[]{:S(2)}) %all-to-all-start) | async-done | bytes 131104 | tf_op jit(solution)/shard_map/all_to_all | solution.py:370
  91.2 4.4 %all-to-all-start.1 = ((bf16[16,8,512]{2,1,0:T(8,128)(2,1)}), bf16[16,8,512]{2,1,0:T(8,128)(2,1)S(1)}, u32[]{:S(2)}, u32[]{:S(2)}) async-start(bf16[16,8,512]{2,1,0:T(8,128)(2,1)} %fusion.2), calls=%async_computation.1 | async-start | bytes 262144 | tf_op jit(solution)/shard_map/all_to_all | solution.py:382
  96.7 7.5 %all-to-all-done.1 = bf16[16,8,512]{2,1,0:T(8,128)(2,1)S(1)} async-done(((bf16[16,8,512]{2,1,0:T(8,128)(2,1)}), bf16[16,8,512]{2,1,0:T(8,128)(2,1)S(1)}, u32[]{:S(2)}, u32[]{:S(2)}) %all-to-all-start.1) | async-done | bytes 131104 | tf_op jit(solution)/shard_map/all_to_all | solution.py:382
  104.9 4.0 %shard_map.151 = bf16[32,1536]{1,0:T(8,128)(2,1)} custom-call(bf16[128,512]{1,0:T(8,128)(2,1)} %bitcast.92, bf16[1536,1536]{1,0:T(8,128)(2,1)} %weight_ref.1, f32[32,1536]{1,0:T(8,128)} %broadcast_bitcast_fusion.base_ref, bf16[1,1536]{1,0:T(2,128)(2,1)} %get-tuple-element.62.gain_ref), custom_call_target="tpu_custom_call" | custom-call | tf_op jit(solution)/shard_map/pallas_call | solution.py:138
  110.0 3.5 %collective-permute-start.17 = (bf16[32,1536]{1,0:T(8,128)(2,1)}, bf16[32,1536]{1,0:T(8,128)(2,1)S(1)}, u32[]{:S(2)}, u32[]{:S(2)}) collective-permute-start(bf16[32,1536]{1,0:T(8,128)(2,1)} %shard_map.151), channel_id=1, source_target_pairs={{0,0},{4,5},{8,10},{12,15},{16,80},{20,85},{24,90},{28,95},{32,160... | collective-permute-start | bytes 294920 | tf_op jit(solution)/shard_map/ppermute | solution.py:398
  113.5 7.9 %collective-permute-done.17 = bf16[32,1536]{1,0:T(8,128)(2,1)S(1)} collective-permute-done((bf16[32,1536]{1,0:T(8,128)(2,1)}, bf16[32,1536]{1,0:T(8,128)(2,1)S(1)}, u32[]{:S(2)}, u32[]{:S(2)}) %collective-permute-start.17) | collective-permute-done | bytes 98336 | tf_op jit(solution)/shard_map/ppermute | solution.py:398
  122.7 4.5 %all-to-all-start.2 = ((bf16[16,32,1536]{2,1,0:T(8,128)(2,1)}), bf16[16,32,1536]{2,1,0:T(8,128)(2,1)}, u32[]{:S(2)}, u32[]{:S(2)}) async-start(bf16[16,32,1536]{2,1,0:T(8,128)(2,1)} %broadcast_in_dim.7), calls=%async_computation.2 | async-start | bytes 3145728 | tf_op jit(solution)/shard_map/all_to_all | solution.py:405
  131.1 17.2 %shard_map.152.q_ref = bf16[768,512]{1,0:T(8,128)(2,1)S(1)} custom-call(s32[4]{0:T(128)S(1)} %pad_add_fusion.where, bf16[768,8192]{1,0:T(8,128)(2,1)} %bitcast.88, bf16[1,8192]{1,0:T(2,128)(2,1)S(1)} %copy-done.2, bf16[2048,512]{1,0:T(8,128)(2,1)S(1)} %bitcast.87, bf16[2048,512]{1,0:T(8,128)(2,1)} %collective-permute-done.18.rest_1_, ...), custom_call_target="tpu_custom_call" | custom-call | tf_op jit(solution)/shard_map/pallas_call | solution.py:195
  149.2 2.0 all-to-all-done.2
  151.2 16.3 %shard_map.153 = (bf16[768,512]{1,0:T(8,128)(2,1)}, bf16[512,1536]{1,0:T(8,128)(2,1)}) custom-call(s32[1]{0:T(128)} %bitcast.85.count, s32[16]{0:T(128)} %multiply_xor_fusion.order, s32[4]{0:T(128)} %copy-done.3, f32[1]{0:T(128)S(6)} %tanh.3.gate_ref, bf16[768,512]{1,0:T(8,128)(2,1)} %copy-done.1, bf16[768,512]{1,0:T(8,128)(2,1)} %bitcast.91, ...), custom_call_target="tpu_custom_call" | custom-call | tf_op jit(solution)/shard_map/pallas_call | solution.py:294
  167.6 26.7 %all_to_all.30 = bf16[16,32,1536]{2,1,0:T(8,128)(2,1)S(1)} all-to-all(bf16[16,32,1536]{2,1,0:T(8,128)(2,1)} %bitcast.90), channel_id=1, replica_groups=mesh['segment'=4,'mp'=16,'dp'=4] {'mp'}, dimensions={0} | all-to-all | bytes 3145728 | tf_op jit(solution)/shard_map/all_to_all | solution.py:417
  194.5 18.7 %all_to_all.31 = bf16[16,8,384]{2,1,0:T(8,128)(2,1)S(1)} all-to-all(bf16[16,8,384]{2,1,0:T(8,128)(2,1)S(1)} %bitcast.95), channel_id=1, replica_groups=mesh['segment'=4,'mp'=16,'dp'=4] {'segment','dp'}, dimensions={0} | all-to-all | bytes 196608 | tf_op jit(solution)/shard_map/all_to_all | solution.py:425
  213.4 10.9 %all_to_all.32 = bf16[16,8,384]{2,1,0:T(8,128)(2,1)S(1)} all-to-all(bf16[16,8,384]{2,1,0:T(8,128)(2,1)S(1)} %fusion.3), channel_id=1, replica_groups=mesh['segment'=4,'mp'=16,'dp'=4] {'segment','dp'}, dimensions={0} | all-to-all | bytes 196608 | tf_op jit(solution)/shard_map/all_to_all | solution.py:428
  (113 shorter events, 41.8 us)
Async XLA Ops:
  7.2 123.9 %all-gather.3.cloned.1.call-start = ((), (), s32[]{:S(2)}) async-start(), calls=%async_computation.6 | async-start | bytes 13369344 | tf_op jit(solution)/shard_map/all_gather | solution.py:343
  12.1 16.3 %collective-permute-start = (bf16[4,8,1536]{2,1,0:T(8,128)(2,1)S(1)}, bf16[4,8,1536]{2,1,0:T(8,128)(2,1)}, u32[]{:S(2)}, u32[]{:S(2)}) collective-permute-start(bf16[4,8,1536]{2,1,0:T(8,128)(2,1)S(1)} %get-tuple-element.61), channel_id=1, source_target_pairs={{0,4},{4,8},{8,12},{12,0},{16,20},{20,24},{24,28},{28,16},{32,36},... | collective-permute-start | bytes 294920 | tf_op jit(solution)/shard_map/ppermute | solution.py:40
  14.2 15.6 %collective-permute-start.1 = (bf16[4,8,1536]{2,1,0:T(8,128)(2,1)S(1)}, bf16[4,8,1536]{2,1,0:T(8,128)(2,1)}, u32[]{:S(2)}, u32[]{:S(2)}) collective-permute-start(bf16[4,8,1536]{2,1,0:T(8,128)(2,1)S(1)} %get-tuple-element.61), channel_id=1, source_target_pairs={{0,12},{4,0},{8,4},{12,8},{16,28},{20,16},{24,20},{28,24},{32,44},... | collective-permute-start | bytes 294920 | tf_op jit(solution)/shard_map/ppermute | solution.py:40
  15.6 15.9 %collective-permute-start.2 = (bf16[4,8,1536]{2,1,0:T(8,128)(2,1)S(1)}, bf16[4,8,1536]{2,1,0:T(8,128)(2,1)}, u32[]{:S(2)}, u32[]{:S(2)}) collective-permute-start(bf16[4,8,1536]{2,1,0:T(8,128)(2,1)S(1)} %get-tuple-element.61), channel_id=1, source_target_pairs={{0,8},{4,12},{8,0},{12,4},{16,24},{20,28},{24,16},{28,20},{32,40},... | collective-permute-start | bytes 294920 | tf_op jit(solution)/shard_map/ppermute | solution.py:40
  17.2 15.3 %collective-permute-start.3 = (bf16[4,8,1536]{2,1,0:T(8,128)(2,1)S(1)}, bf16[4,8,1536]{2,1,0:T(8,128)(2,1)}, u32[]{:S(2)}, u32[]{:S(2)}) collective-permute-start(bf16[4,8,1536]{2,1,0:T(8,128)(2,1)S(1)} %get-tuple-element.60), channel_id=1, source_target_pairs={{0,16},{4,20},{8,24},{12,28},{16,32},{20,36},{24,40},{28,44},{32,4... | collective-permute-start | bytes 294920 | tf_op jit(solution)/shard_map/ppermute | solution.py:40
  19.6 18.5 %collective-permute-start.6 = (bf16[512,512]{1,0:T(8,128)(2,1)S(1)}, bf16[512,512]{1,0:T(8,128)(2,1)S(1)}, u32[]{:S(2)}, u32[]{:S(2)}) collective-permute-start(bf16[512,512]{1,0:T(8,128)(2,1)S(1)} %slice_bitcast_fusion.1), channel_id=1, source_target_pairs={{0,2},{1,3},{2,0},{3,1},{4,6},{5,7},{6,4},{7,5},{8,10},{9,11},{10,... | collective-permute-start | bytes 1572872 | tf_op jit(solution)/shard_map/ppermute | solution.py:64
  29.9 7.3 %collective-permute-start.5 = (bf16[4,8,1536]{2,1,0:T(8,128)(2,1)S(1)}, bf16[4,8,1536]{2,1,0:T(8,128)(2,1)S(1)}, u32[]{:S(2)}, u32[]{:S(2)}) collective-permute-start(bf16[4,8,1536]{2,1,0:T(8,128)(2,1)S(1)} %get-tuple-element.60), channel_id=1, source_target_pairs={{0,32},{4,36},{8,40},{12,44},{16,48},{20,52},{24,56},{28,60},{32,0... | collective-permute-start | bytes 294920 | tf_op jit(solution)/shard_map/ppermute | solution.py:40
  31.5 35.2 %collective-permute-start.15 = (bf16[1536,512]{1,0:T(8,128)(2,1)S(1)}, bf16[1536,512]{1,0:T(8,128)(2,1)}, u32[]{:S(2)}, u32[]{:S(2)}) collective-permute-start(bf16[1536,512]{1,0:T(8,128)(2,1)S(1)} %slice_bitcast_fusion), channel_id=1, source_target_pairs={{0,2},{1,3},{2,0},{3,1},{4,6},{5,7},{6,4},{7,5},{8,10},{9,11},{10,... | collective-permute-start | bytes 4718600 | tf_op jit(solution)/shard_map/ppermute | solution.py:64
  38.1 15.5 %collective-permute-start.11 = (bf16[4,32,1536]{2,1,0:T(8,128)(2,1)S(1)}, bf16[4,32,1536]{2,1,0:T(8,128)(2,1)S(1)}, u32[]{:S(2)}, u32[]{:S(2)}) collective-permute-start(bf16[4,32,1536]{2,1,0:T(8,128)(2,1)S(1)} %pad_maximum_fusion.2), channel_id=1, source_target_pairs={{0,4},{4,8},{8,12},{12,0},{16,20},{20,24},{24,28},{28,16},{32,36},... | collective-permute-start | bytes 1179656 | tf_op jit(solution)/shard_map/ppermute | solution.py:40
  38.4 15.4 %collective-permute-start.12 = (bf16[4,32,1536]{2,1,0:T(8,128)(2,1)S(1)}, bf16[4,32,1536]{2,1,0:T(8,128)(2,1)S(1)}, u32[]{:S(2)}, u32[]{:S(2)}) collective-permute-start(bf16[4,32,1536]{2,1,0:T(8,128)(2,1)S(1)} %pad_maximum_fusion.2), channel_id=1, source_target_pairs={{0,12},{4,0},{8,4},{12,8},{16,28},{20,16},{24,20},{28,24},{32,44},... | collective-permute-start | bytes 1179656 | tf_op jit(solution)/shard_map/ppermute | solution.py:40
  40.9 15.9 %collective-permute-start.8 = (bf16[4,32,1536]{2,1,0:T(8,128)(2,1)S(1)}, bf16[4,32,1536]{2,1,0:T(8,128)(2,1)S(1)}, u32[]{:S(2)}, u32[]{:S(2)}) collective-permute-start(bf16[4,32,1536]{2,1,0:T(8,128)(2,1)S(1)} %pad_maximum_fusion.1), channel_id=1, source_target_pairs={{0,48},{4,52},{8,56},{12,60},{16,0},{20,4},{24,8},{28,12},{32,16},... | collective-permute-start | bytes 1179656 | tf_op jit(solution)/shard_map/ppermute | solution.py:40
  44.1 15.8 %collective-permute-start.7 = (bf16[4,32,1536]{2,1,0:T(8,128)(2,1)S(1)}, bf16[4,32,1536]{2,1,0:T(8,128)(2,1)S(1)}, u32[]{:S(2)}, u32[]{:S(2)}) collective-permute-start(bf16[4,32,1536]{2,1,0:T(8,128)(2,1)S(1)} %pad_maximum_fusion.1), channel_id=1, source_target_pairs={{0,16},{4,20},{8,24},{12,28},{16,32},{20,36},{24,40},{28,44},{32,4... | collective-permute-start | bytes 1179656 | tf_op jit(solution)/shard_map/ppermute | solution.py:40
  53.7 10.0 %collective-permute-start.13 = (bf16[2,32,1536]{2,1,0:T(8,128)(2,1)S(1)}, bf16[2,32,1536]{2,1,0:T(8,128)(2,1)S(1)}, u32[]{:S(2)}, u32[]{:S(2)}) collective-permute-start(bf16[2,32,1536]{2,1,0:T(8,128)(2,1)S(1)} %slice.72), channel_id=1, source_target_pairs={{0,4},{4,8},{8,12},{12,0},{16,20},{20,24},{24,28},{28,16},{32,36},... | collective-permute-start | bytes 589832 | tf_op jit(solution)/shard_map/ppermute | solution.py:40
  53.8 9.9 %collective-permute-start.14 = (bf16[2,32,1536]{2,1,0:T(8,128)(2,1)S(1)}, bf16[2,32,1536]{2,1,0:T(8,128)(2,1)S(1)}, u32[]{:S(2)}, u32[]{:S(2)}) collective-permute-start(bf16[2,32,1536]{2,1,0:T(8,128)(2,1)S(1)} %slice.73), channel_id=1, source_target_pairs={{0,12},{4,0},{8,4},{12,8},{16,28},{20,16},{24,20},{28,24},{32,44},... | collective-permute-start | bytes 589832 | tf_op jit(solution)/shard_map/ppermute | solution.py:40
  56.8 7.8 %collective-permute-start.10 = (bf16[2,32,1536]{2,1,0:T(8,128)(2,1)S(1)}, bf16[2,32,1536]{2,1,0:T(8,128)(2,1)S(1)}, u32[]{:S(2)}, u32[]{:S(2)}) collective-permute-start(bf16[2,32,1536]{2,1,0:T(8,128)(2,1)S(1)} %slice.71), channel_id=1, source_target_pairs={{0,48},{4,52},{8,56},{12,60},{16,0},{20,4},{24,8},{28,12},{32,16},... | collective-permute-start | bytes 589832 | tf_op jit(solution)/shard_map/ppermute | solution.py:40
  70.7 19.6 %all-to-all-start = ((bf16[16,8,512]{2,1,0:T(8,128)(2,1)}), bf16[16,8,512]{2,1,0:T(8,128)(2,1)S(1)}, u32[]{:S(2)}, u32[]{:S(2)}) async-start(bf16[16,8,512]{2,1,0:T(8,128)(2,1)} %bitcast.94), calls=%async_computation | async-start | bytes 262144 | tf_op jit(solution)/shard_map/all_to_all | solution.py:370
  81.1 48.9 %collective-permute-start.18 = (bf16[2048,512]{1,0:T(8,128)(2,1)S(1)}, bf16[2048,512]{1,0:T(8,128)(2,1)}, u32[]{:S(2)}, u32[]{:S(2)}) collective-permute-start(bf16[2048,512]{1,0:T(8,128)(2,1)S(1)} %bitcast.86), channel_id=1, source_target_pairs={{0,1},{1,0},{2,3},{3,2},{4,5},{5,4},{6,7},{7,6},{8,9},{9,8},{10,11... | collective-permute-start | bytes 6291464 | tf_op jit(solution)/shard_map/ppermute | solution.py:68
  90.2 19.7 %collective-permute-start.16 = (bf16[384,1024]{1,0:T(8,128)(2,1)}, bf16[384,1024]{1,0:T(8,128)(2,1)}, u32[]{:S(2)}, u32[]{:S(2)}) collective-permute-start(bf16[384,1024]{1,0:T(8,128)(2,1)} %pad_maximum_fusion.kv0), channel_id=1, source_target_pairs={{0,2},{1,3},{2,0},{3,1},{4,6},{5,7},{6,4},{7,5},{8,10},{9,11},{10,... | collective-permute-start | bytes 2359304 | tf_op jit(solution)/shard_map/ppermute | solution.py:64
  91.2 13.0 %all-to-all-start.1 = ((bf16[16,8,512]{2,1,0:T(8,128)(2,1)}), bf16[16,8,512]{2,1,0:T(8,128)(2,1)S(1)}, u32[]{:S(2)}, u32[]{:S(2)}) async-start(bf16[16,8,512]{2,1,0:T(8,128)(2,1)} %fusion.2), calls=%async_computation.1 | async-start | bytes 262144 | tf_op jit(solution)/shard_map/all_to_all | solution.py:382
  96.3 34.8 %collective-permute-start.20 = (bf16[1536,512]{1,0:T(8,128)(2,1)}, bf16[1536,512]{1,0:T(8,128)(2,1)}, u32[]{:S(2)}, u32[]{:S(2)}) collective-permute-start(bf16[1536,512]{1,0:T(8,128)(2,1)} %collective-permute-done.15.rest_3_), channel_id=1, source_target_pairs={{0,1},{1,0},{2,3},{3,2},{4,5},{5,4},{6,7},{7,6},{8,9},{9,8},{10,11... | collective-permute-start | bytes 4718600 | tf_op jit(solution)/shard_map/ppermute | solution.py:68
  110.0 11.4 %collective-permute-start.17 = (bf16[32,1536]{1,0:T(8,128)(2,1)}, bf16[32,1536]{1,0:T(8,128)(2,1)S(1)}, u32[]{:S(2)}, u32[]{:S(2)}) collective-permute-start(bf16[32,1536]{1,0:T(8,128)(2,1)} %shard_map.151), channel_id=1, source_target_pairs={{0,0},{4,5},{8,10},{12,15},{16,80},{20,85},{24,90},{28,95},{32,160... | collective-permute-start | bytes 294920 | tf_op jit(solution)/shard_map/ppermute | solution.py:398
  122.7 28.5 %all-to-all-start.2 = ((bf16[16,32,1536]{2,1,0:T(8,128)(2,1)}), bf16[16,32,1536]{2,1,0:T(8,128)(2,1)}, u32[]{:S(2)}, u32[]{:S(2)}) async-start(bf16[16,32,1536]{2,1,0:T(8,128)(2,1)} %broadcast_in_dim.7), calls=%async_computation.2 | async-start | bytes 3145728 | tf_op jit(solution)/shard_map/all_to_all | solution.py:405
  127.2 24.0 %collective-permute-start.21 = (bf16[384,1024]{1,0:T(8,128)(2,1)}, bf16[384,1024]{1,0:T(8,128)(2,1)}, u32[]{:S(2)}, u32[]{:S(2)}) collective-permute-start(bf16[384,1024]{1,0:T(8,128)(2,1)} %pad_maximum_fusion.kv0), channel_id=1, source_target_pairs={{0,1},{1,0},{2,3},{3,2},{4,5},{5,4},{6,7},{7,6},{8,9},{9,8},{10,11... | collective-permute-start | bytes 2359304 | tf_op jit(solution)/shard_map/ppermute | solution.py:68
  127.3 23.9 %collective-permute-start.22 = (bf16[384,1024]{1,0:T(8,128)(2,1)}, bf16[384,1024]{1,0:T(8,128)(2,1)}, u32[]{:S(2)}, u32[]{:S(2)}) collective-permute-start(bf16[384,1024]{1,0:T(8,128)(2,1)} %collective-permute-done.16.kv2), channel_id=1, source_target_pairs={{0,1},{1,0},{2,3},{3,2},{4,5},{5,4},{6,7},{7,6},{8,9},{9,8},{10,11... | collective-permute-start | bytes 2359304 | tf_op jit(solution)/shard_map/ppermute | solution.py:68
  (16 other events, 123.1 us)
Sparse Core Ops, SparseCore 0:
  10.4 116.0 all-gather.2

commit v7 on v6

--- a/solution.py
+++ b/solution.py
@@ -72,14 +72,16 @@
     return [value, core_swap(value), across, core_swap(across)]
 
 
-def norm_kernel(value_ref, gain_ref, out_ref):
-    out_ref[...] = layer_norm(value_ref[...], gain_ref[...]).astype(BF16)
-
-
-def norm_rows(value, gain):
-    return pl.pallas_call(
-        norm_kernel, out_shape=jax.ShapeDtypeStruct(value.shape, BF16)
-    )(value, gain)
+def norm_kernel(value_ref, gains_ref, low_ref, high_ref):
+    gain = gains_ref[...].astype(F32)[:1]
+    half = low_ref.shape[0]
+    low_ref[...] = layer_norm(value_ref[:half, :], gain).astype(BF16)
+    high_ref[...] = layer_norm(value_ref[half:, :], gain).astype(BF16)
+
+
+def norm_halves(value, gains):
+    half = jax.ShapeDtypeStruct((value.shape[0] // 2, value.shape[1]), BF16)
+    return pl.pallas_call(norm_kernel, out_shape=[half, half])(value, gains)
 
 
 def resample_kernel(q_ref, lat_ref, *rest):
@@ -341,9 +343,9 @@
     width = res_query.shape[1]
 
     whole_text = lax.all_gather(text[0, 0], "mp", axis=1, tiled=True)
-    media = norm_rows(frames.reshape(-1, E), norm_gains[:1]).reshape(frames.shape)
-    half = owned // 2
-    phase = [direct(media[:half], "x"), direct(media[half:], "y")]
+    low, high = norm_halves(frames.reshape(-1, E), norm_gains)
+    half_shape = (owned // 2,) + frames.shape[1:]
+    phase = [direct(low.reshape(half_shape), "x"), direct(high.reshape(half_shape), "y")]
     joined_halves = [jnp.concatenate(blocks, axis=1) for blocks in phase]
     early = w_query.shape[1] // 4
     low_across = over_z(w_query[0, :early])
@@ -364,7 +366,11 @@
             pieces.append(
                 jnp.einsum("fpe,ec->fpc", block, res_pair, preferred_element_type=F32).astype(BF16)
             )
-    pieces, high_across, kv_local = lax.optimization_barrier((pieces, high_across, kv_local))
+    order = halved(group ^ jnp.arange(mp_count, dtype=jnp.int32))
+    where = jnp.stack([dp, dp ^ 1, dp ^ 2, dp ^ 3]).astype(jnp.int32)
+    pieces, high_across, kv_local, order, where = lax.optimization_barrier(
+        (pieces, high_across, kv_local, order, where)
+    )
     piece = resample(res_q, lat_pairs, pieces, slots, share)
 
     piece = lax.all_to_all(
@@ -405,9 +411,7 @@
     dest = lax.all_to_all(
         jnp.broadcast_to(mine, (mp_count,) + mine.shape), "mp", 0, 0, tiled=True
     ).reshape(LAT * owned, E)
-    order = halved(group ^ jnp.arange(mp_count, dtype=jnp.int32))
-
-    where = jnp.stack([dp, dp ^ 1, dp ^ 2, dp ^ 3]).astype(jnp.int32)
+
     query = query_matmul(whole_text, text_gain, query_blocks, where)
     dest, query = lax.optimization_barrier((dest, query))
     context, part = attention(

time: 233 us -> 240 us (1.030)
  blocking collectives: 56.3 us -> 66.4 us
  starting transfers between devices: 47.7 us -> 44.2 us
  waiting for transfers between devices: 41.7 us -> 44.4 us
  local copies, waits for them, and re-layouts: 10.7 us -> 8.02 us
    all_to_all x1, blocking collectives: 18.7 us -> 31.7 us  [per_device(): lax.all_to_all(send, GROUP, 0, 0, tiled=True).reshape(slots, E // cut)]
    ppermute x14, starting transfers between devices: 21.8 us -> 18.2 us  [shift(): return lax.ppermute(value, 'mp', pairs)]
    ppermute x14, waiting for transfers between devices: 12.4 us -> 15.8 us  [shift(): return lax.ppermute(value, 'mp', pairs)]
    all_to_all x1, blocking collectives: 26.7 us -> 23.8 us  [per_device(): lax.all_to_all(part.reshape(mp_count, share * owned, E), 'mp', 0, 0, tile...]
  transfers between devices with their start and end apart: 27 -> 27, of which waited for: 10 -> 8; matrix products, arithmetic and copies ran while one was open for 10% -> 9% of each run, Pallas kernels for 12% -> 11%
where the time goes in v7:
time: 240 us; the launch traced here: 239 us
  blocking collectives  66.4 us (28%)
  waiting for transfers between devices  44.4 us (18%)
  starting transfers between devices  44.2 us (18%)
  Pallas kernels  43.3 us (18%)
  between operations  15.7 us (7%)
  matrix products  11.4 us (5%)
  local copies, waits for them, and re-layouts  8.02 us (3%)
  other arithmetic  5.86 us (2%)
    all_to_all x1, blocking collectives, per_device(): lax.all_to_all(send, GROUP, 0, 0, tiled=True).reshape(slots, E // cut)  31.7 us
    all_to_all x1, blocking collectives, per_device(): lax.all_to_all(part.reshape(mp_count, share * owned, E), 'mp', 0, 0, tile...  23.8 us
    ppermute x14, starting transfers between devices, shift(): return lax.ppermute(value, 'mp', pairs)  18.2 us
    pallas_call x1, Pallas kernels, query_matmul(): pl.pallas_call(query_kernel, grid_spec=pltpu.PrefetchScalarGridSpec(num_s...  17.2 us
    pallas_call x1, Pallas kernels, attention(): pl.pallas_call(attend_kernel, grid_spec=pltpu.PrefetchScalarGridSpec(num_...  16.3 us
    ppermute x14, waiting for transfers between devices, shift(): return lax.ppermute(value, 'mp', pairs)  15.8 us
    all_to_all x1, starting transfers between devices, per_device(): lax.all_to_all(piece.reshape(groups, owned, share * PAD), GROUP, 0, 0, ti...  11.9 us
    all_to_all x1, blocking collectives, per_device(): lax.all_to_all(send.reshape(groups, owned, E // cut), GROUP, 0, 0, tiled=...  10.9 us
  transfers between devices with their start and end apart: 27, of which 8 were waited for; matrix products, arithmetic and copies ran while one was open for 9% of the time, Pallas kernels for 11%

profile of v7, /device:TPU:1, one launch (start us, length us, event | category | flops | bytes accessed | tf_op | source)
XLA Modules:
  0.0 239.2 jit_solution(8828437037841124784)
XLA Ops:
  7.9 1.8 shard_map.149
  9.7 2.1 collective-permute-start.3
  13.3 1.6 collective-permute-start.5
  17.2 1.7 collective-permute-start.6
  22.8 2.0 convolution_convert_fusion.10.lat_ref
  29.8 4.7 %collective-permute-done.2 = bf16[4,8,1536]{2,1,0:T(8,128)(2,1)S(1)} collective-permute-done((bf16[4,8,1536]{2,1,0:T(8,128)(2,1)S(1)}, bf16[4,8,1536]{2,1,0:T(8,128)(2,1)S(1)}, u32[]{:S(2)}, u32[]{:S(2)}) %collective-permute-start.2) | collective-permute-done | bytes 98336 | tf_op jit(solution)/shard_map/ppermute | solution.py:40
  35.6 2.7 %collective-permute-start.12 = (bf16[4,32,1536]{2,1,0:T(8,128)(2,1)S(1)}, bf16[4,32,1536]{2,1,0:T(8,128)(2,1)S(1)}, u32[]{:S(2)}, u32[]{:S(2)}) collective-permute-start(bf16[4,32,1536]{2,1,0:T(8,128)(2,1)S(1)} %pad_maximum_fusion.2), channel_id=1, source_target_pairs={{0,12},{4,0},{8,4},{12,8},{16,28},{20,16},{24,20},{28,24},{32,44},... | collective-permute-start | bytes 1179656 | tf_op jit(solution)/shard_map/ppermute | solution.py:40
  42.7 11.0 %collective-permute-done.11 = bf16[4,32,1536]{2,1,0:T(8,128)(2,1)S(1)} collective-permute-done((bf16[4,32,1536]{2,1,0:T(8,128)(2,1)S(1)}, bf16[4,32,1536]{2,1,0:T(8,128)(2,1)S(1)}, u32[]{:S(2)}, u32[]{:S(2)}) %collective-permute-start.11) | collective-permute-done | bytes 393248 | tf_op jit(solution)/shard_map/ppermute | solution.py:40
  53.9 2.9 %collective-permute-start.14 = (bf16[2,32,1536]{2,1,0:T(8,128)(2,1)S(1)}, bf16[2,32,1536]{2,1,0:T(8,128)(2,1)S(1)}, u32[]{:S(2)}, u32[]{:S(2)}) collective-permute-start(bf16[2,32,1536]{2,1,0:T(8,128)(2,1)S(1)} %slice.51), channel_id=1, source_target_pairs={{0,12},{4,0},{8,4},{12,8},{16,28},{20,16},{24,20},{28,24},{32,44},... | collective-permute-start | bytes 589832 | tf_op jit(solution)/shard_map/ppermute | solution.py:40
  64.1 3.9 %shard_map.150 = bf16[128,512]{1,0:T(8,128)(2,1)} custom-call(bf16[64,128]{1,0:T(8,128)(2,1)} %convolution_convert_fusion.11.q_ref, bf16[64,256]{1,0:T(8,128)(2,1)} %convolution_convert_fusion.10.lat_ref, bf16[4,32,256]{2,1,0:T(8,128)(2,1)} %convolution_convert_fusion.9.rest_0_, bf16[4,32,256]{2,1,0:T(8,128)(2,1)} %convolution_convert_fusion.8.rest_1_, ...), custom_call_target="tpu_custom_call" | custom-call | tf_op jit(solution)/shard_map/pallas_call | solution.py:114
  68.0 11.9 %all-to-all-start = ((bf16[16,8,512]{2,1,0:T(8,128)(2,1)}), bf16[16,8,512]{2,1,0:T(8,128)(2,1)S(1)}, u32[]{:S(2)}, u32[]{:S(2)}) async-start(bf16[16,8,512]{2,1,0:T(8,128)(2,1)} %bitcast.92), calls=%async_computation | async-start | bytes 262144 | tf_op jit(solution)/shard_map/all_to_all | solution.py:376
  80.1 9.0 %all-to-all-done = bf16[16,8,512]{2,1,0:T(8,128)(2,1)S(1)} async-done(((bf16[16,8,512]{2,1,0:T(8,128)(2,1)}), bf16[16,8,512]{2,1,0:T(8,128)(2,1)S(1)}, u32[]{:S(2)}, u32[]{:S(2)}) %all-to-all-start) | async-done | bytes 131104 | tf_op jit(solution)/shard_map/all_to_all | solution.py:376
  90.8 3.5 %all-to-all-start.1 = ((bf16[16,8,512]{2,1,0:T(8,128)(2,1)}), bf16[16,8,512]{2,1,0:T(8,128)(2,1)S(1)}, u32[]{:S(2)}, u32[]{:S(2)}) async-start(bf16[16,8,512]{2,1,0:T(8,128)(2,1)} %fusion.2), calls=%async_computation.1 | async-start | bytes 262144 | tf_op jit(solution)/shard_map/all_to_all | solution.py:388
  95.8 7.2 %all-to-all-done.1 = bf16[16,8,512]{2,1,0:T(8,128)(2,1)S(1)} async-done(((bf16[16,8,512]{2,1,0:T(8,128)(2,1)}), bf16[16,8,512]{2,1,0:T(8,128)(2,1)S(1)}, u32[]{:S(2)}, u32[]{:S(2)}) %all-to-all-start.1) | async-done | bytes 131104 | tf_op jit(solution)/shard_map/all_to_all | solution.py:388
  103.7 4.0 %shard_map.151 = bf16[32,1536]{1,0:T(8,128)(2,1)} custom-call(bf16[128,512]{1,0:T(8,128)(2,1)} %bitcast.90, bf16[1536,1536]{1,0:T(8,128)(2,1)} %weight_ref.1, f32[32,1536]{1,0:T(8,128)} %broadcast_bitcast_fusion.base_ref, bf16[1,1536]{1,0:T(2,128)(2,1)} %slice.47.gain_ref), custom_call_target="tpu_custom_call" | custom-call | tf_op jit(solution)/shard_map/pallas_call | solution.py:140
  108.8 3.1 %collective-permute-start.17 = (bf16[32,1536]{1,0:T(8,128)(2,1)}, bf16[32,1536]{1,0:T(8,128)(2,1)S(1)}, u32[]{:S(2)}, u32[]{:S(2)}) collective-permute-start(bf16[32,1536]{1,0:T(8,128)(2,1)} %shard_map.151), channel_id=1, source_target_pairs={{0,0},{4,5},{8,10},{12,15},{16,80},{20,85},{24,90},{28,95},{32,160... | collective-permute-start | bytes 294920 | tf_op jit(solution)/shard_map/ppermute | solution.py:404
  112.0 8.4 %collective-permute-done.17 = bf16[32,1536]{1,0:T(8,128)(2,1)S(1)} collective-permute-done((bf16[32,1536]{1,0:T(8,128)(2,1)}, bf16[32,1536]{1,0:T(8,128)(2,1)S(1)}, u32[]{:S(2)}, u32[]{:S(2)}) %collective-permute-start.17) | collective-permute-done | bytes 98336 | tf_op jit(solution)/shard_map/ppermute | solution.py:404
  121.7 4.5 %all-to-all-start.2 = ((bf16[16,32,1536]{2,1,0:T(8,128)(2,1)}), bf16[16,32,1536]{2,1,0:T(8,128)(2,1)}, u32[]{:S(2)}, u32[]{:S(2)}) async-start(bf16[16,32,1536]{2,1,0:T(8,128)(2,1)} %broadcast_in_dim.7), calls=%async_computation.2 | async-start | bytes 3145728 | tf_op jit(solution)/shard_map/all_to_all | solution.py:411
  128.3 1.8 collective-permute-done.19.rest_4_
  130.2 17.2 %shard_map.152.q_ref = bf16[768,512]{1,0:T(8,128)(2,1)S(1)} custom-call(s32[4]{0:T(128)S(1)} %pad_add_fusion.where, bf16[768,8192]{1,0:T(8,128)(2,1)} %bitcast.86, bf16[1,8192]{1,0:T(2,128)(2,1)S(1)} %copy-done.2, bf16[2048,512]{1,0:T(8,128)(2,1)S(1)} %bitcast.85, bf16[2048,512]{1,0:T(8,128)(2,1)} %collective-permute-done.18.rest_1_, ...), custom_call_target="tpu_custom_call" | custom-call | tf_op jit(solution)/shard_map/pallas_call | solution.py:197
  148.5 16.3 %shard_map.153 = (bf16[768,512]{1,0:T(8,128)(2,1)}, bf16[512,1536]{1,0:T(8,128)(2,1)}) custom-call(s32[1]{0:T(128)} %bitcast.83.count, s32[16]{0:T(128)} %multiply_xor_fusion.order, s32[4]{0:T(128)} %copy-done.3, f32[1]{0:T(128)S(6)} %tanh.3.gate_ref, bf16[768,512]{1,0:T(8,128)(2,1)} %copy-done.1, bf16[768,512]{1,0:T(8,128)(2,1)} %bitcast.89, ...), custom_call_target="tpu_custom_call" | custom-call | tf_op jit(solution)/shard_map/pallas_call | solution.py:296
  164.8 23.8 %all_to_all.30 = bf16[16,32,1536]{2,1,0:T(8,128)(2,1)S(1)} all-to-all(bf16[16,32,1536]{2,1,0:T(8,128)(2,1)} %bitcast.88), channel_id=1, replica_groups=mesh['segment'=4,'mp'=16,'dp'=4] {'mp'}, dimensions={0} | all-to-all | bytes 3145728 | tf_op jit(solution)/shard_map/all_to_all | solution.py:421
  188.9 31.7 %all_to_all.31 = bf16[16,8,384]{2,1,0:T(8,128)(2,1)S(1)} all-to-all(bf16[16,8,384]{2,1,0:T(8,128)(2,1)S(1)} %bitcast.93), channel_id=1, replica_groups=mesh['segment'=4,'mp'=16,'dp'=4] {'segment','dp'}, dimensions={0} | all-to-all | bytes 196608 | tf_op jit(solution)/shard_map/all_to_all | solution.py:429
  220.8 10.9 %all_to_all.32 = bf16[16,8,384]{2,1,0:T(8,128)(2,1)S(1)} all-to-all(bf16[16,8,384]{2,1,0:T(8,128)(2,1)S(1)} %fusion.3), channel_id=1, replica_groups=mesh['segment'=4,'mp'=16,'dp'=4] {'segment','dp'}, dimensions={0} | all-to-all | bytes 196608 | tf_op jit(solution)/shard_map/all_to_all | solution.py:432
  (114 shorter events, 35.5 us)
Async XLA Ops:
  7.2 123.0 %all-gather.3.cloned.1.call-start = ((), (), s32[]{:S(2)}) async-start(), calls=%async_computation.6 | async-start | bytes 13369344 | tf_op jit(solution)/shard_map/all_gather | solution.py:345
  9.7 15.3 %collective-permute-start.3 = (bf16[4,8,1536]{2,1,0:T(8,128)(2,1)}, bf16[4,8,1536]{2,1,0:T(8,128)(2,1)}, u32[]{:S(2)}, u32[]{:S(2)}) collective-permute-start(bf16[4,8,1536]{2,1,0:T(8,128)(2,1)} %bitcast.119), channel_id=1, source_target_pairs={{0,16},{4,20},{8,24},{12,28},{16,32},{20,36},{24,40},{28,44},{32,4... | collective-permute-start | bytes 294920 | tf_op jit(solution)/shard_map/ppermute | solution.py:40
  11.8 15.3 %collective-permute-start.4 = (bf16[4,8,1536]{2,1,0:T(8,128)(2,1)}, bf16[4,8,1536]{2,1,0:T(8,128)(2,1)}, u32[]{:S(2)}, u32[]{:S(2)}) collective-permute-start(bf16[4,8,1536]{2,1,0:T(8,128)(2,1)} %bitcast.120), channel_id=1, source_target_pairs={{0,48},{4,52},{8,56},{12,60},{16,0},{20,4},{24,8},{28,12},{32,16},... | collective-permute-start | bytes 294920 | tf_op jit(solution)/shard_map/ppermute | solution.py:40
  13.3 15.4 %collective-permute-start.5 = (bf16[4,8,1536]{2,1,0:T(8,128)(2,1)}, bf16[4,8,1536]{2,1,0:T(8,128)(2,1)}, u32[]{:S(2)}, u32[]{:S(2)}) collective-permute-start(bf16[4,8,1536]{2,1,0:T(8,128)(2,1)} %bitcast.121), channel_id=1, source_target_pairs={{0,32},{4,36},{8,40},{12,44},{16,48},{20,52},{24,56},{28,60},{32,0... | collective-permute-start | bytes 294920 | tf_op jit(solution)/shard_map/ppermute | solution.py:40
  14.9 14.8 %collective-permute-start = (bf16[4,8,1536]{2,1,0:T(8,128)(2,1)}, bf16[4,8,1536]{2,1,0:T(8,128)(2,1)}, u32[]{:S(2)}, u32[]{:S(2)}) collective-permute-start(bf16[4,8,1536]{2,1,0:T(8,128)(2,1)} %bitcast.115), channel_id=1, source_target_pairs={{0,4},{4,8},{8,12},{12,0},{16,20},{20,24},{24,28},{28,16},{32,36},... | collective-permute-start | bytes 294920 | tf_op jit(solution)/shard_map/ppermute | solution.py:40
  17.2 18.2 %collective-permute-start.6 = (bf16[512,512]{1,0:T(8,128)(2,1)S(1)}, bf16[512,512]{1,0:T(8,128)(2,1)S(1)}, u32[]{:S(2)}, u32[]{:S(2)}) collective-permute-start(bf16[512,512]{1,0:T(8,128)(2,1)S(1)} %slice_bitcast_fusion.1), channel_id=1, source_target_pairs={{0,2},{1,3},{2,0},{3,1},{4,6},{5,7},{6,4},{7,5},{8,10},{9,11},{10,... | collective-permute-start | bytes 1572872 | tf_op jit(solution)/shard_map/ppermute | solution.py:64
  27.2 7.4 %collective-permute-start.2 = (bf16[4,8,1536]{2,1,0:T(8,128)(2,1)S(1)}, bf16[4,8,1536]{2,1,0:T(8,128)(2,1)S(1)}, u32[]{:S(2)}, u32[]{:S(2)}) collective-permute-start(bf16[4,8,1536]{2,1,0:T(8,128)(2,1)S(1)} %bitcast.117), channel_id=1, source_target_pairs={{0,8},{4,12},{8,0},{12,4},{16,24},{20,28},{24,16},{28,20},{32,40},... | collective-permute-start | bytes 294920 | tf_op jit(solution)/shard_map/ppermute | solution.py:40
  28.7 35.4 %collective-permute-start.15 = (bf16[1536,512]{1,0:T(8,128)(2,1)S(1)}, bf16[1536,512]{1,0:T(8,128)(2,1)}, u32[]{:S(2)}, u32[]{:S(2)}) collective-permute-start(bf16[1536,512]{1,0:T(8,128)(2,1)S(1)} %slice_bitcast_fusion), channel_id=1, source_target_pairs={{0,2},{1,3},{2,0},{3,1},{4,6},{5,7},{6,4},{7,5},{8,10},{9,11},{10,... | collective-permute-start | bytes 4718600 | tf_op jit(solution)/shard_map/ppermute | solution.py:64
  35.5 18.3 %collective-permute-start.11 = (bf16[4,32,1536]{2,1,0:T(8,128)(2,1)S(1)}, bf16[4,32,1536]{2,1,0:T(8,128)(2,1)S(1)}, u32[]{:S(2)}, u32[]{:S(2)}) collective-permute-start(bf16[4,32,1536]{2,1,0:T(8,128)(2,1)S(1)} %pad_maximum_fusion.2), channel_id=1, source_target_pairs={{0,4},{4,8},{8,12},{12,0},{16,20},{20,24},{24,28},{28,16},{32,36},... | collective-permute-start | bytes 1179656 | tf_op jit(solution)/shard_map/ppermute | solution.py:40
  35.6 18.3 %collective-permute-start.12 = (bf16[4,32,1536]{2,1,0:T(8,128)(2,1)S(1)}, bf16[4,32,1536]{2,1,0:T(8,128)(2,1)S(1)}, u32[]{:S(2)}, u32[]{:S(2)}) collective-permute-start(bf16[4,32,1536]{2,1,0:T(8,128)(2,1)S(1)} %pad_maximum_fusion.2), channel_id=1, source_target_pairs={{0,12},{4,0},{8,4},{12,8},{16,28},{20,16},{24,20},{28,24},{32,44},... | collective-permute-start | bytes 1179656 | tf_op jit(solution)/shard_map/ppermute | solution.py:40
  38.2 18.6 %collective-permute-start.8 = (bf16[4,32,1536]{2,1,0:T(8,128)(2,1)S(1)}, bf16[4,32,1536]{2,1,0:T(8,128)(2,1)S(1)}, u32[]{:S(2)}, u32[]{:S(2)}) collective-permute-start(bf16[4,32,1536]{2,1,0:T(8,128)(2,1)S(1)} %pad_maximum_fusion.1), channel_id=1, source_target_pairs={{0,48},{4,52},{8,56},{12,60},{16,0},{20,4},{24,8},{28,12},{32,16},... | collective-permute-start | bytes 1179656 | tf_op jit(solution)/shard_map/ppermute | solution.py:40
  38.2 18.7 %collective-permute-start.7 = (bf16[4,32,1536]{2,1,0:T(8,128)(2,1)S(1)}, bf16[4,32,1536]{2,1,0:T(8,128)(2,1)S(1)}, u32[]{:S(2)}, u32[]{:S(2)}) collective-permute-start(bf16[4,32,1536]{2,1,0:T(8,128)(2,1)S(1)} %pad_maximum_fusion.1), channel_id=1, source_target_pairs={{0,16},{4,20},{8,24},{12,28},{16,32},{20,36},{24,40},{28,44},{32,4... | collective-permute-start | bytes 1179656 | tf_op jit(solution)/shard_map/ppermute | solution.py:40
  53.8 8.4 %collective-permute-start.13 = (bf16[2,32,1536]{2,1,0:T(8,128)(2,1)S(1)}, bf16[2,32,1536]{2,1,0:T(8,128)(2,1)S(1)}, u32[]{:S(2)}, u32[]{:S(2)}) collective-permute-start(bf16[2,32,1536]{2,1,0:T(8,128)(2,1)S(1)} %slice.50), channel_id=1, source_target_pairs={{0,4},{4,8},{8,12},{12,0},{16,20},{20,24},{24,28},{28,16},{32,36},... | collective-permute-start | bytes 589832 | tf_op jit(solution)/shard_map/ppermute | solution.py:40
  53.9 8.3 %collective-permute-start.14 = (bf16[2,32,1536]{2,1,0:T(8,128)(2,1)S(1)}, bf16[2,32,1536]{2,1,0:T(8,128)(2,1)S(1)}, u32[]{:S(2)}, u32[]{:S(2)}) collective-permute-start(bf16[2,32,1536]{2,1,0:T(8,128)(2,1)S(1)} %slice.51), channel_id=1, source_target_pairs={{0,12},{4,0},{8,4},{12,8},{16,28},{20,16},{24,20},{28,24},{32,44},... | collective-permute-start | bytes 589832 | tf_op jit(solution)/shard_map/ppermute | solution.py:40
  56.8 6.3 %collective-permute-start.10 = (bf16[2,32,1536]{2,1,0:T(8,128)(2,1)S(1)}, bf16[2,32,1536]{2,1,0:T(8,128)(2,1)S(1)}, u32[]{:S(2)}, u32[]{:S(2)}) collective-permute-start(bf16[2,32,1536]{2,1,0:T(8,128)(2,1)S(1)} %slice.49), channel_id=1, source_target_pairs={{0,48},{4,52},{8,56},{12,60},{16,0},{20,4},{24,8},{28,12},{32,16},... | collective-permute-start | bytes 589832 | tf_op jit(solution)/shard_map/ppermute | solution.py:40
  68.0 21.1 %all-to-all-start = ((bf16[16,8,512]{2,1,0:T(8,128)(2,1)}), bf16[16,8,512]{2,1,0:T(8,128)(2,1)S(1)}, u32[]{:S(2)}, u32[]{:S(2)}) async-start(bf16[16,8,512]{2,1,0:T(8,128)(2,1)} %bitcast.92), calls=%async_computation | async-start | bytes 262144 | tf_op jit(solution)/shard_map/all_to_all | solution.py:376
  79.9 48.4 %collective-permute-start.18 = (bf16[2048,512]{1,0:T(8,128)(2,1)S(1)}, bf16[2048,512]{1,0:T(8,128)(2,1)}, u32[]{:S(2)}, u32[]{:S(2)}) collective-permute-start(bf16[2048,512]{1,0:T(8,128)(2,1)S(1)} %bitcast.84), channel_id=1, source_target_pairs={{0,1},{1,0},{2,3},{3,2},{4,5},{5,4},{6,7},{7,6},{8,9},{9,8},{10,11... | collective-permute-start | bytes 6291464 | tf_op jit(solution)/shard_map/ppermute | solution.py:68
  89.1 19.7 %collective-permute-start.16 = (bf16[384,1024]{1,0:T(8,128)(2,1)}, bf16[384,1024]{1,0:T(8,128)(2,1)}, u32[]{:S(2)}, u32[]{:S(2)}) collective-permute-start(bf16[384,1024]{1,0:T(8,128)(2,1)} %pad_maximum_fusion.kv0), channel_id=1, source_target_pairs={{0,2},{1,3},{2,0},{3,1},{4,6},{5,7},{6,4},{7,5},{8,10},{9,11},{10,... | collective-permute-start | bytes 2359304 | tf_op jit(solution)/shard_map/ppermute | solution.py:64
  90.8 12.2 %all-to-all-start.1 = ((bf16[16,8,512]{2,1,0:T(8,128)(2,1)}), bf16[16,8,512]{2,1,0:T(8,128)(2,1)S(1)}, u32[]{:S(2)}, u32[]{:S(2)}) async-start(bf16[16,8,512]{2,1,0:T(8,128)(2,1)} %fusion.2), calls=%async_computation.1 | async-start | bytes 262144 | tf_op jit(solution)/shard_map/all_to_all | solution.py:388
  95.6 34.5 %collective-permute-start.20 = (bf16[1536,512]{1,0:T(8,128)(2,1)}, bf16[1536,512]{1,0:T(8,128)(2,1)}, u32[]{:S(2)}, u32[]{:S(2)}) collective-permute-start(bf16[1536,512]{1,0:T(8,128)(2,1)} %collective-permute-done.15.rest_3_), channel_id=1, source_target_pairs={{0,1},{1,0},{2,3},{3,2},{4,5},{5,4},{6,7},{7,6},{8,9},{9,8},{10,11... | collective-permute-start | bytes 4718600 | tf_op jit(solution)/shard_map/ppermute | solution.py:68
  108.8 11.6 %collective-permute-start.17 = (bf16[32,1536]{1,0:T(8,128)(2,1)}, bf16[32,1536]{1,0:T(8,128)(2,1)S(1)}, u32[]{:S(2)}, u32[]{:S(2)}) collective-permute-start(bf16[32,1536]{1,0:T(8,128)(2,1)} %shard_map.151), channel_id=1, source_target_pairs={{0,0},{4,5},{8,10},{12,15},{16,80},{20,85},{24,90},{28,95},{32,160... | collective-permute-start | bytes 294920 | tf_op jit(solution)/shard_map/ppermute | solution.py:404
  121.7 26.8 %all-to-all-start.2 = ((bf16[16,32,1536]{2,1,0:T(8,128)(2,1)}), bf16[16,32,1536]{2,1,0:T(8,128)(2,1)}, u32[]{:S(2)}, u32[]{:S(2)}) async-start(bf16[16,32,1536]{2,1,0:T(8,128)(2,1)} %broadcast_in_dim.7), calls=%async_computation.2 | async-start | bytes 3145728 | tf_op jit(solution)/shard_map/all_to_all | solution.py:411
  126.3 22.3 %collective-permute-start.21 = (bf16[384,1024]{1,0:T(8,128)(2,1)}, bf16[384,1024]{1,0:T(8,128)(2,1)}, u32[]{:S(2)}, u32[]{:S(2)}) collective-permute-start(bf16[384,1024]{1,0:T(8,128)(2,1)} %pad_maximum_fusion.kv0), channel_id=1, source_target_pairs={{0,1},{1,0},{2,3},{3,2},{4,5},{5,4},{6,7},{7,6},{8,9},{9,8},{10,11... | collective-permute-start | bytes 2359304 | tf_op jit(solution)/shard_map/ppermute | solution.py:68
  126.4 22.2 %collective-permute-start.22 = (bf16[384,1024]{1,0:T(8,128)(2,1)}, bf16[384,1024]{1,0:T(8,128)(2,1)}, u32[]{:S(2)}, u32[]{:S(2)}) collective-permute-start(bf16[384,1024]{1,0:T(8,128)(2,1)} %collective-permute-done.16.kv2), channel_id=1, source_target_pairs={{0,1},{1,0},{2,3},{3,2},{4,5},{5,4},{6,7},{7,6},{8,9},{9,8},{10,11... | collective-permute-start | bytes 2359304 | tf_op jit(solution)/shard_map/ppermute | solution.py:68
  (17 other events, 202.8 us)
Sparse Core Ops, SparseCore 0:
  10.4 117.1 all-gather.2

commit v8 on v7

--- a/solution.py
+++ b/solution.py
@@ -147,7 +147,8 @@
 def query_kernel(where, text_ref, gain_ref, *rest):
     weights = rest[:-5]
     out_ref, held, centered, scale_ref, sems = rest[-5:]
-    rows, depth = text_ref.shape
+    senders, rows, sent = text_ref.shape
+    depth = senders * sent
     group, width = 64, 256
     block = depth // 4
     copies = []
@@ -159,6 +160,10 @@
         to = held.at[pl.ds(pl.multiple_of(at, 512), size), :]
         copies.append(pltpu.make_async_copy(weight, to, sems.at[j]))
     first = pl.program_id(0) == 0
+    each = sent // width
+
+    def chunk(c):
+        return c // each, slice(c % each * width, (c % each + 1) * width)
 
     @pl.when(first)
     def _():
@@ -170,12 +175,12 @@
         at = pl.ds(pl.multiple_of(step * group, group), group)
         total = jnp.zeros((group, width), F32)
         for c in range(depth // width):
-            total += text_ref[at, c * width : (c + 1) * width].astype(F32)
+            total += text_ref[chunk(c)[0], at, chunk(c)[1]].astype(F32)
         mean = jnp.sum(total, axis=1, keepdims=True) * (1.0 / depth)
         square = jnp.zeros((group, width), F32)
         for c in range(depth // width):
             cols = slice(c * width, (c + 1) * width)
-            off = text_ref[at, cols].astype(F32) - mean
+            off = text_ref[chunk(c)[0], at, chunk(c)[1]].astype(F32) - mean
             centered[at, cols] = (off * gain_ref[:, cols].astype(F32)).astype(BF16)
             square += off * off
         spread = jnp.sum(square, axis=1, keepdims=True) * (1.0 / depth)
@@ -191,7 +196,8 @@
 
 
 def query_matmul(text, gain, weights, where):
-    tokens, depth = text.shape
+    senders, tokens, sent = text.shape
+    depth = senders * sent
     cols = weights[0].shape[1]
     rows = 256
     return pl.pallas_call(
@@ -200,7 +206,7 @@
             num_scalar_prefetch=1,
             grid=(tokens // rows,),
             in_specs=[
-                pl.BlockSpec((rows, depth), lambda i, w: (i, 0)),
+                pl.BlockSpec((senders, rows, sent), lambda i, w: (0, i, 0)),
                 pl.BlockSpec((1, depth), lambda i, w: (0, 0)),
             ]
             + [pl.BlockSpec(memory_space=pl.ANY) for w in weights],
@@ -342,7 +348,7 @@
     groups = slots // owned
     width = res_query.shape[1]
 
-    whole_text = lax.all_gather(text[0, 0], "mp", axis=1, tiled=True)
+    whole_text = lax.all_gather(text[0, 0], "mp", axis=0)
     low, high = norm_halves(frames.reshape(-1, E), norm_gains)
     half_shape = (owned // 2,) + frames.shape[1:]
     phase = [direct(low.reshape(half_shape), "x"), direct(high.reshape(half_shape), "y")]

time: 240 us -> 226 us (0.942)
  blocking collectives: 66.4 us -> 52.1 us
    all_to_all x1, blocking collectives: 31.7 us -> 12.5 us  [per_device(): lax.all_to_all(send, GROUP, 0, 0, tiled=True).reshape(slots, E // cut)]
    all_to_all x1, blocking collectives: 23.8 us -> 28.7 us  [per_device(): lax.all_to_all(part.reshape(mp_count, share * owned, E), 'mp', 0, 0, tile...]
  transfers between devices with their start and end apart: 27 -> 27, of which waited for: 8 -> 7; matrix products, arithmetic and copies ran while one was open for 9% -> 10% of each run, Pallas kernels for 11% -> 12%
where the time goes in v8:
time: 226 us; the launch traced here: 225 us
  blocking collectives  52.1 us (23%)
  starting transfers between devices  44.9 us (20%)
  Pallas kernels  43.6 us (19%)
  waiting for transfers between devices  43.5 us (19%)
  between operations  15.7 us (7%)
  matrix products  11.4 us (5%)
  local copies, waits for them, and re-layouts  8.02 us (4%)
  other arithmetic  5.84 us (3%)
    all_to_all x1, blocking collectives, per_device(): lax.all_to_all(part.reshape(mp_count, share * owned, E), 'mp', 0, 0, tile...  28.7 us
    ppermute x14, starting transfers between devices, shift(): return lax.ppermute(value, 'mp', pairs)  18.2 us
    pallas_call x1, Pallas kernels, query_matmul(): pl.pallas_call(query_kernel, grid_spec=pltpu.PrefetchScalarGridSpec(num_s...  17.3 us
    pallas_call x1, Pallas kernels, attention(): pl.pallas_call(attend_kernel, grid_spec=pltpu.PrefetchScalarGridSpec(num_...  16.3 us
    ppermute x14, waiting for transfers between devices, shift(): return lax.ppermute(value, 'mp', pairs)  15.1 us
    all_to_all x1, starting transfers between devices, per_device(): lax.all_to_all(piece.reshape(groups, owned, share * PAD), GROUP, 0, 0, ti...  12.5 us
    all_to_all x1, blocking collectives, per_device(): lax.all_to_all(send, GROUP, 0, 0, tiled=True).reshape(slots, E // cut)  12.5 us
    all_to_all x1, blocking collectives, per_device(): lax.all_to_all(send.reshape(groups, owned, E // cut), GROUP, 0, 0, tiled=...  10.9 us
  transfers between devices with their start and end apart: 27, of which 7 were waited for; matrix products, arithmetic and copies ran while one was open for 10% of the time, Pallas kernels for 12%

profile of v8, /device:TPU:1, one launch (start us, length us, event | category | flops | bytes accessed | tf_op | source)
XLA Modules:
  0.0 224.9 jit_solution(1745647127168591135)
XLA Ops:
  7.9 1.8 shard_map.149
  9.7 2.1 collective-permute-start.3
  13.3 1.6 collective-permute-start.5
  17.2 1.7 collective-permute-start.6
  22.8 2.0 convolution_convert_fusion.10.lat_ref
  29.8 4.7 %collective-permute-done.2 = bf16[4,8,1536]{2,1,0:T(8,128)(2,1)S(1)} collective-permute-done((bf16[4,8,1536]{2,1,0:T(8,128)(2,1)S(1)}, bf16[4,8,1536]{2,1,0:T(8,128)(2,1)S(1)}, u32[]{:S(2)}, u32[]{:S(2)}) %collective-permute-start.2) | collective-permute-done | bytes 98336 | tf_op jit(solution)/shard_map/ppermute | solution.py:40
  35.5 2.7 %collective-permute-start.12 = (bf16[4,32,1536]{2,1,0:T(8,128)(2,1)S(1)}, bf16[4,32,1536]{2,1,0:T(8,128)(2,1)S(1)}, u32[]{:S(2)}, u32[]{:S(2)}) collective-permute-start(bf16[4,32,1536]{2,1,0:T(8,128)(2,1)S(1)} %pad_maximum_fusion.2), channel_id=1, source_target_pairs={{0,12},{4,0},{8,4},{12,8},{16,28},{20,16},{24,20},{28,24},{32,44},... | collective-permute-start | bytes 1179656 | tf_op jit(solution)/shard_map/ppermute | solution.py:40
  42.6 10.4 %collective-permute-done.11 = bf16[4,32,1536]{2,1,0:T(8,128)(2,1)S(1)} collective-permute-done((bf16[4,32,1536]{2,1,0:T(8,128)(2,1)S(1)}, bf16[4,32,1536]{2,1,0:T(8,128)(2,1)S(1)}, u32[]{:S(2)}, u32[]{:S(2)}) %collective-permute-start.11) | collective-permute-done | bytes 393248 | tf_op jit(solution)/shard_map/ppermute | solution.py:40
  53.2 2.9 %collective-permute-start.14 = (bf16[2,32,1536]{2,1,0:T(8,128)(2,1)S(1)}, bf16[2,32,1536]{2,1,0:T(8,128)(2,1)S(1)}, u32[]{:S(2)}, u32[]{:S(2)}) collective-permute-start(bf16[2,32,1536]{2,1,0:T(8,128)(2,1)S(1)} %slice.51), channel_id=1, source_target_pairs={{0,12},{4,0},{8,4},{12,8},{16,28},{20,16},{24,20},{28,24},{32,44},... | collective-permute-start | bytes 589832 | tf_op jit(solution)/shard_map/ppermute | solution.py:40
  63.4 4.2 %shard_map.150 = bf16[128,512]{1,0:T(8,128)(2,1)} custom-call(bf16[64,128]{1,0:T(8,128)(2,1)} %convolution_convert_fusion.11.q_ref, bf16[64,256]{1,0:T(8,128)(2,1)} %convolution_convert_fusion.10.lat_ref, bf16[4,32,256]{2,1,0:T(8,128)(2,1)} %convolution_convert_fusion.9.rest_0_, bf16[4,32,256]{2,1,0:T(8,128)(2,1)} %convolution_convert_fusion.8.rest_1_, ...), custom_call_target="tpu_custom_call" | custom-call | tf_op jit(solution)/shard_map/pallas_call | solution.py:114
  67.6 12.5 %all-to-all-start = ((bf16[16,8,512]{2,1,0:T(8,128)(2,1)}), bf16[16,8,512]{2,1,0:T(8,128)(2,1)S(1)}, u32[]{:S(2)}, u32[]{:S(2)}) async-start(bf16[16,8,512]{2,1,0:T(8,128)(2,1)} %bitcast.92), calls=%async_computation | async-start | bytes 262144 | tf_op jit(solution)/shard_map/all_to_all | solution.py:382
  80.3 9.0 %all-to-all-done = bf16[16,8,512]{2,1,0:T(8,128)(2,1)S(1)} async-done(((bf16[16,8,512]{2,1,0:T(8,128)(2,1)}), bf16[16,8,512]{2,1,0:T(8,128)(2,1)S(1)}, u32[]{:S(2)}, u32[]{:S(2)}) %all-to-all-start) | async-done | bytes 131104 | tf_op jit(solution)/shard_map/all_to_all | solution.py:382
  91.0 3.5 %all-to-all-start.1 = ((bf16[16,8,512]{2,1,0:T(8,128)(2,1)}), bf16[16,8,512]{2,1,0:T(8,128)(2,1)S(1)}, u32[]{:S(2)}, u32[]{:S(2)}) async-start(bf16[16,8,512]{2,1,0:T(8,128)(2,1)} %fusion.2), calls=%async_computation.1 | async-start | bytes 262144 | tf_op jit(solution)/shard_map/all_to_all | solution.py:394
  96.0 7.2 %all-to-all-done.1 = bf16[16,8,512]{2,1,0:T(8,128)(2,1)S(1)} async-done(((bf16[16,8,512]{2,1,0:T(8,128)(2,1)}), bf16[16,8,512]{2,1,0:T(8,128)(2,1)S(1)}, u32[]{:S(2)}, u32[]{:S(2)}) %all-to-all-start.1) | async-done | bytes 131104 | tf_op jit(solution)/shard_map/all_to_all | solution.py:394
  103.9 4.0 %shard_map.151 = bf16[32,1536]{1,0:T(8,128)(2,1)} custom-call(bf16[128,512]{1,0:T(8,128)(2,1)} %bitcast.90, bf16[1536,1536]{1,0:T(8,128)(2,1)} %weight_ref.1, f32[32,1536]{1,0:T(8,128)} %broadcast_bitcast_fusion.base_ref, bf16[1,1536]{1,0:T(2,128)(2,1)} %slice.47.gain_ref), custom_call_target="tpu_custom_call" | custom-call | tf_op jit(solution)/shard_map/pallas_call | solution.py:140
  109.0 3.1 %collective-permute-start.17 = (bf16[32,1536]{1,0:T(8,128)(2,1)}, bf16[32,1536]{1,0:T(8,128)(2,1)S(1)}, u32[]{:S(2)}, u32[]{:S(2)}) collective-permute-start(bf16[32,1536]{1,0:T(8,128)(2,1)} %shard_map.151), channel_id=1, source_target_pairs={{0,0},{4,5},{8,10},{12,15},{16,80},{20,85},{24,90},{28,95},{32,160... | collective-permute-start | bytes 294920 | tf_op jit(solution)/shard_map/ppermute | solution.py:410
  112.2 8.4 %collective-permute-done.17 = bf16[32,1536]{1,0:T(8,128)(2,1)S(1)} collective-permute-done((bf16[32,1536]{1,0:T(8,128)(2,1)}, bf16[32,1536]{1,0:T(8,128)(2,1)S(1)}, u32[]{:S(2)}, u32[]{:S(2)}) %collective-permute-start.17) | collective-permute-done | bytes 98336 | tf_op jit(solution)/shard_map/ppermute | solution.py:410
  121.9 4.5 %all-to-all-start.2 = ((bf16[16,32,1536]{2,1,0:T(8,128)(2,1)}), bf16[16,32,1536]{2,1,0:T(8,128)(2,1)}, u32[]{:S(2)}, u32[]{:S(2)}) async-start(bf16[16,32,1536]{2,1,0:T(8,128)(2,1)} %broadcast_in_dim.7), calls=%async_computation.2 | async-start | bytes 3145728 | tf_op jit(solution)/shard_map/all_to_all | solution.py:417
  128.5 1.8 collective-permute-done.19.rest_4_
  130.3 17.3 %shard_map.152.q_ref = bf16[768,512]{1,0:T(8,128)(2,1)S(1)} custom-call(s32[4]{0:T(128)S(1)} %pad_add_fusion.where, bf16[16,768,512]{2,1,0:T(8,128)(2,1)} %bitcast.86, bf16[1,8192]{1,0:T(2,128)(2,1)S(1)} %copy-done.2, bf16[2048,512]{1,0:T(8,128)(2,1)S(1)} %bitcast.85, bf16[2048,512]{1,0:T(8,128)(2,1)} %collective-permute-done.18.rest_1_, ...), custom_call_target="tpu_custom_call" | custom-call | tf_op jit(solution)/shard_map/pallas_call | solution.py:203
  148.5 16.3 %shard_map.153 = (bf16[768,512]{1,0:T(8,128)(2,1)}, bf16[512,1536]{1,0:T(8,128)(2,1)}) custom-call(s32[1]{0:T(128)} %bitcast.83.count, s32[16]{0:T(128)} %multiply_xor_fusion.order, s32[4]{0:T(128)} %copy-done.3, f32[1]{0:T(128)S(6)} %tanh.3.gate_ref, bf16[768,512]{1,0:T(8,128)(2,1)} %copy-done.1, bf16[768,512]{1,0:T(8,128)(2,1)} %bitcast.89, ...), custom_call_target="tpu_custom_call" | custom-call | tf_op jit(solution)/shard_map/pallas_call | solution.py:302
  164.8 28.7 %all_to_all.30 = bf16[16,32,1536]{2,1,0:T(8,128)(2,1)S(1)} all-to-all(bf16[16,32,1536]{2,1,0:T(8,128)(2,1)} %bitcast.88), channel_id=1, replica_groups=mesh['segment'=4,'mp'=16,'dp'=4] {'mp'}, dimensions={0} | all-to-all | bytes 3145728 | tf_op jit(solution)/shard_map/all_to_all | solution.py:427
  193.8 12.5 %all_to_all.31 = bf16[16,8,384]{2,1,0:T(8,128)(2,1)S(1)} all-to-all(bf16[16,8,384]{2,1,0:T(8,128)(2,1)S(1)} %bitcast.93), channel_id=1, replica_groups=mesh['segment'=4,'mp'=16,'dp'=4] {'segment','dp'}, dimensions={0} | all-to-all | bytes 196608 | tf_op jit(solution)/shard_map/all_to_all | solution.py:435
  206.5 10.9 %all_to_all.32 = bf16[16,8,384]{2,1,0:T(8,128)(2,1)S(1)} all-to-all(bf16[16,8,384]{2,1,0:T(8,128)(2,1)S(1)} %fusion.3), channel_id=1, replica_groups=mesh['segment'=4,'mp'=16,'dp'=4] {'segment','dp'}, dimensions={0} | all-to-all | bytes 196608 | tf_op jit(solution)/shard_map/all_to_all | solution.py:438
  (114 shorter events, 35.2 us)
Async XLA Ops:
  7.2 123.2 %all-gather.3.cloned.1.call-start = ((), (), s32[]{:S(2)}) async-start(), calls=%async_computation.6 | async-start | bytes 13369344 | tf_op jit(solution)/shard_map/all_gather | solution.py:351
  9.7 15.3 %collective-permute-start.3 = (bf16[4,8,1536]{2,1,0:T(8,128)(2,1)}, bf16[4,8,1536]{2,1,0:T(8,128)(2,1)}, u32[]{:S(2)}, u32[]{:S(2)}) collective-permute-start(bf16[4,8,1536]{2,1,0:T(8,128)(2,1)} %bitcast.119), channel_id=1, source_target_pairs={{0,16},{4,20},{8,24},{12,28},{16,32},{20,36},{24,40},{28,44},{32,4... | collective-permute-start | bytes 294920 | tf_op jit(solution)/shard_map/ppermute | solution.py:40
  11.8 15.3 %collective-permute-start.4 = (bf16[4,8,1536]{2,1,0:T(8,128)(2,1)}, bf16[4,8,1536]{2,1,0:T(8,128)(2,1)}, u32[]{:S(2)}, u32[]{:S(2)}) collective-permute-start(bf16[4,8,1536]{2,1,0:T(8,128)(2,1)} %bitcast.120), channel_id=1, source_target_pairs={{0,48},{4,52},{8,56},{12,60},{16,0},{20,4},{24,8},{28,12},{32,16},... | collective-permute-start | bytes 294920 | tf_op jit(solution)/shard_map/ppermute | solution.py:40
  13.3 15.4 %collective-permute-start.5 = (bf16[4,8,1536]{2,1,0:T(8,128)(2,1)}, bf16[4,8,1536]{2,1,0:T(8,128)(2,1)}, u32[]{:S(2)}, u32[]{:S(2)}) collective-permute-start(bf16[4,8,1536]{2,1,0:T(8,128)(2,1)} %bitcast.121), channel_id=1, source_target_pairs={{0,32},{4,36},{8,40},{12,44},{16,48},{20,52},{24,56},{28,60},{32,0... | collective-permute-start | bytes 294920 | tf_op jit(solution)/shard_map/ppermute | solution.py:40
  14.9 14.8 %collective-permute-start = (bf16[4,8,1536]{2,1,0:T(8,128)(2,1)}, bf16[4,8,1536]{2,1,0:T(8,128)(2,1)}, u32[]{:S(2)}, u32[]{:S(2)}) collective-permute-start(bf16[4,8,1536]{2,1,0:T(8,128)(2,1)} %bitcast.115), channel_id=1, source_target_pairs={{0,4},{4,8},{8,12},{12,0},{16,20},{20,24},{24,28},{28,16},{32,36},... | collective-permute-start | bytes 294920 | tf_op jit(solution)/shard_map/ppermute | solution.py:40
  17.2 18.2 %collective-permute-start.6 = (bf16[512,512]{1,0:T(8,128)(2,1)S(1)}, bf16[512,512]{1,0:T(8,128)(2,1)S(1)}, u32[]{:S(2)}, u32[]{:S(2)}) collective-permute-start(bf16[512,512]{1,0:T(8,128)(2,1)S(1)} %slice_bitcast_fusion.1), channel_id=1, source_target_pairs={{0,2},{1,3},{2,0},{3,1},{4,6},{5,7},{6,4},{7,5},{8,10},{9,11},{10,... | collective-permute-start | bytes 1572872 | tf_op jit(solution)/shard_map/ppermute | solution.py:64
  27.2 7.3 %collective-permute-start.2 = (bf16[4,8,1536]{2,1,0:T(8,128)(2,1)S(1)}, bf16[4,8,1536]{2,1,0:T(8,128)(2,1)S(1)}, u32[]{:S(2)}, u32[]{:S(2)}) collective-permute-start(bf16[4,8,1536]{2,1,0:T(8,128)(2,1)S(1)} %bitcast.117), channel_id=1, source_target_pairs={{0,8},{4,12},{8,0},{12,4},{16,24},{20,28},{24,16},{28,20},{32,40},... | collective-permute-start | bytes 294920 | tf_op jit(solution)/shard_map/ppermute | solution.py:40
  28.7 34.7 %collective-permute-start.15 = (bf16[1536,512]{1,0:T(8,128)(2,1)S(1)}, bf16[1536,512]{1,0:T(8,128)(2,1)}, u32[]{:S(2)}, u32[]{:S(2)}) collective-permute-start(bf16[1536,512]{1,0:T(8,128)(2,1)S(1)} %slice_bitcast_fusion), channel_id=1, source_target_pairs={{0,2},{1,3},{2,0},{3,1},{4,6},{5,7},{6,4},{7,5},{8,10},{9,11},{10,... | collective-permute-start | bytes 4718600 | tf_op jit(solution)/shard_map/ppermute | solution.py:64
  35.4 17.7 %collective-permute-start.11 = (bf16[4,32,1536]{2,1,0:T(8,128)(2,1)S(1)}, bf16[4,32,1536]{2,1,0:T(8,128)(2,1)S(1)}, u32[]{:S(2)}, u32[]{:S(2)}) collective-permute-start(bf16[4,32,1536]{2,1,0:T(8,128)(2,1)S(1)} %pad_maximum_fusion.2), channel_id=1, source_target_pairs={{0,4},{4,8},{8,12},{12,0},{16,20},{20,24},{24,28},{28,16},{32,36},... | collective-permute-start | bytes 1179656 | tf_op jit(solution)/shard_map/ppermute | solution.py:40
  35.5 17.7 %collective-permute-start.12 = (bf16[4,32,1536]{2,1,0:T(8,128)(2,1)S(1)}, bf16[4,32,1536]{2,1,0:T(8,128)(2,1)S(1)}, u32[]{:S(2)}, u32[]{:S(2)}) collective-permute-start(bf16[4,32,1536]{2,1,0:T(8,128)(2,1)S(1)} %pad_maximum_fusion.2), channel_id=1, source_target_pairs={{0,12},{4,0},{8,4},{12,8},{16,28},{20,16},{24,20},{28,24},{32,44},... | collective-permute-start | bytes 1179656 | tf_op jit(solution)/shard_map/ppermute | solution.py:40
  38.1 18.0 %collective-permute-start.8 = (bf16[4,32,1536]{2,1,0:T(8,128)(2,1)S(1)}, bf16[4,32,1536]{2,1,0:T(8,128)(2,1)S(1)}, u32[]{:S(2)}, u32[]{:S(2)}) collective-permute-start(bf16[4,32,1536]{2,1,0:T(8,128)(2,1)S(1)} %pad_maximum_fusion.1), channel_id=1, source_target_pairs={{0,48},{4,52},{8,56},{12,60},{16,0},{20,4},{24,8},{28,12},{32,16},... | collective-permute-start | bytes 1179656 | tf_op jit(solution)/shard_map/ppermute | solution.py:40
  38.1 18.1 %collective-permute-start.7 = (bf16[4,32,1536]{2,1,0:T(8,128)(2,1)S(1)}, bf16[4,32,1536]{2,1,0:T(8,128)(2,1)S(1)}, u32[]{:S(2)}, u32[]{:S(2)}) collective-permute-start(bf16[4,32,1536]{2,1,0:T(8,128)(2,1)S(1)} %pad_maximum_fusion.1), channel_id=1, source_target_pairs={{0,16},{4,20},{8,24},{12,28},{16,32},{20,36},{24,40},{28,44},{32,4... | collective-permute-start | bytes 1179656 | tf_op jit(solution)/shard_map/ppermute | solution.py:40
  53.1 8.4 %collective-permute-start.13 = (bf16[2,32,1536]{2,1,0:T(8,128)(2,1)S(1)}, bf16[2,32,1536]{2,1,0:T(8,128)(2,1)S(1)}, u32[]{:S(2)}, u32[]{:S(2)}) collective-permute-start(bf16[2,32,1536]{2,1,0:T(8,128)(2,1)S(1)} %slice.50), channel_id=1, source_target_pairs={{0,4},{4,8},{8,12},{12,0},{16,20},{20,24},{24,28},{28,16},{32,36},... | collective-permute-start | bytes 589832 | tf_op jit(solution)/shard_map/ppermute | solution.py:40
  53.2 8.3 %collective-permute-start.14 = (bf16[2,32,1536]{2,1,0:T(8,128)(2,1)S(1)}, bf16[2,32,1536]{2,1,0:T(8,128)(2,1)S(1)}, u32[]{:S(2)}, u32[]{:S(2)}) collective-permute-start(bf16[2,32,1536]{2,1,0:T(8,128)(2,1)S(1)} %slice.51), channel_id=1, source_target_pairs={{0,12},{4,0},{8,4},{12,8},{16,28},{20,16},{24,20},{28,24},{32,44},... | collective-permute-start | bytes 589832 | tf_op jit(solution)/shard_map/ppermute | solution.py:40
  56.1 6.3 %collective-permute-start.10 = (bf16[2,32,1536]{2,1,0:T(8,128)(2,1)S(1)}, bf16[2,32,1536]{2,1,0:T(8,128)(2,1)S(1)}, u32[]{:S(2)}, u32[]{:S(2)}) collective-permute-start(bf16[2,32,1536]{2,1,0:T(8,128)(2,1)S(1)} %slice.49), channel_id=1, source_target_pairs={{0,48},{4,52},{8,56},{12,60},{16,0},{20,4},{24,8},{28,12},{32,16},... | collective-permute-start | bytes 589832 | tf_op jit(solution)/shard_map/ppermute | solution.py:40
  67.6 21.7 %all-to-all-start = ((bf16[16,8,512]{2,1,0:T(8,128)(2,1)}), bf16[16,8,512]{2,1,0:T(8,128)(2,1)S(1)}, u32[]{:S(2)}, u32[]{:S(2)}) async-start(bf16[16,8,512]{2,1,0:T(8,128)(2,1)} %bitcast.92), calls=%async_computation | async-start | bytes 262144 | tf_op jit(solution)/shard_map/all_to_all | solution.py:382
  80.1 48.4 %collective-permute-start.18 = (bf16[2048,512]{1,0:T(8,128)(2,1)S(1)}, bf16[2048,512]{1,0:T(8,128)(2,1)}, u32[]{:S(2)}, u32[]{:S(2)}) collective-permute-start(bf16[2048,512]{1,0:T(8,128)(2,1)S(1)} %bitcast.84), channel_id=1, source_target_pairs={{0,1},{1,0},{2,3},{3,2},{4,5},{5,4},{6,7},{7,6},{8,9},{9,8},{10,11... | collective-permute-start | bytes 6291464 | tf_op jit(solution)/shard_map/ppermute | solution.py:68
  89.3 19.7 %collective-permute-start.16 = (bf16[384,1024]{1,0:T(8,128)(2,1)}, bf16[384,1024]{1,0:T(8,128)(2,1)}, u32[]{:S(2)}, u32[]{:S(2)}) collective-permute-start(bf16[384,1024]{1,0:T(8,128)(2,1)} %pad_maximum_fusion.kv0), channel_id=1, source_target_pairs={{0,2},{1,3},{2,0},{3,1},{4,6},{5,7},{6,4},{7,5},{8,10},{9,11},{10,... | collective-permute-start | bytes 2359304 | tf_op jit(solution)/shard_map/ppermute | solution.py:64
  91.0 12.2 %all-to-all-start.1 = ((bf16[16,8,512]{2,1,0:T(8,128)(2,1)}), bf16[16,8,512]{2,1,0:T(8,128)(2,1)S(1)}, u32[]{:S(2)}, u32[]{:S(2)}) async-start(bf16[16,8,512]{2,1,0:T(8,128)(2,1)} %fusion.2), calls=%async_computation.1 | async-start | bytes 262144 | tf_op jit(solution)/shard_map/all_to_all | solution.py:394
  95.8 34.5 %collective-permute-start.20 = (bf16[1536,512]{1,0:T(8,128)(2,1)}, bf16[1536,512]{1,0:T(8,128)(2,1)}, u32[]{:S(2)}, u32[]{:S(2)}) collective-permute-start(bf16[1536,512]{1,0:T(8,128)(2,1)} %collective-permute-done.15.rest_3_), channel_id=1, source_target_pairs={{0,1},{1,0},{2,3},{3,2},{4,5},{5,4},{6,7},{7,6},{8,9},{9,8},{10,11... | collective-permute-start | bytes 4718600 | tf_op jit(solution)/shard_map/ppermute | solution.py:68
  109.0 11.6 %collective-permute-start.17 = (bf16[32,1536]{1,0:T(8,128)(2,1)}, bf16[32,1536]{1,0:T(8,128)(2,1)S(1)}, u32[]{:S(2)}, u32[]{:S(2)}) collective-permute-start(bf16[32,1536]{1,0:T(8,128)(2,1)} %shard_map.151), channel_id=1, source_target_pairs={{0,0},{4,5},{8,10},{12,15},{16,80},{20,85},{24,90},{28,95},{32,160... | collective-permute-start | bytes 294920 | tf_op jit(solution)/shard_map/ppermute | solution.py:410
  121.9 26.6 %all-to-all-start.2 = ((bf16[16,32,1536]{2,1,0:T(8,128)(2,1)}), bf16[16,32,1536]{2,1,0:T(8,128)(2,1)}, u32[]{:S(2)}, u32[]{:S(2)}) async-start(bf16[16,32,1536]{2,1,0:T(8,128)(2,1)} %broadcast_in_dim.7), calls=%async_computation.2 | async-start | bytes 3145728 | tf_op jit(solution)/shard_map/all_to_all | solution.py:417
  126.5 22.1 %collective-permute-start.21 = (bf16[384,1024]{1,0:T(8,128)(2,1)}, bf16[384,1024]{1,0:T(8,128)(2,1)}, u32[]{:S(2)}, u32[]{:S(2)}) collective-permute-start(bf16[384,1024]{1,0:T(8,128)(2,1)} %pad_maximum_fusion.kv0), channel_id=1, source_target_pairs={{0,1},{1,0},{2,3},{3,2},{4,5},{5,4},{6,7},{7,6},{8,9},{9,8},{10,11... | collective-permute-start | bytes 2359304 | tf_op jit(solution)/shard_map/ppermute | solution.py:68
  126.6 22.0 %collective-permute-start.22 = (bf16[384,1024]{1,0:T(8,128)(2,1)}, bf16[384,1024]{1,0:T(8,128)(2,1)}, u32[]{:S(2)}, u32[]{:S(2)}) collective-permute-start(bf16[384,1024]{1,0:T(8,128)(2,1)} %collective-permute-done.16.kv2), channel_id=1, source_target_pairs={{0,1},{1,0},{2,3},{3,2},{4,5},{5,4},{6,7},{7,6},{8,9},{9,8},{10,11... | collective-permute-start | bytes 2359304 | tf_op jit(solution)/shard_map/ppermute | solution.py:68
  (17 other events, 203.8 us)
Sparse Core Ops, SparseCore 0:
  10.4 108.4 all-gather.2

commit v9 on v8

--- a/solution.py
+++ b/solution.py
@@ -401,7 +401,7 @@
         jnp.repeat(base_rows, owned, axis=0),
         norm_gains[2:],
     )
-    latents, kv_across = lax.optimization_barrier((latents, kv_across))
+    latents, kv_across, query_blocks = lax.optimization_barrier((latents, kv_across, query_blocks))
     dp_count = lax.axis_size("dp")
 
     def place(g, m):

time: 226 us -> 234 us (1.035)
  blocking collectives: 52.1 us -> 69.9 us
  starting transfers between devices: 44.9 us -> 36.3 us
    all_to_all x0 -> x1, blocking collectives: none -> 17.6 us  [per_device(): lax.all_to_all(piece.reshape(groups, owned, share * PAD), GROUP, 0, 0, ti...]
    all_to_all x1 -> x0, starting transfers between devices: 12.5 us -> none  [per_device(): lax.all_to_all(piece.reshape(groups, owned, share * PAD), GROUP, 0, 0, ti...]
    ppermute x14, waiting for transfers between devices: 15.1 us -> 24.9 us  [shift(): return lax.ppermute(value, 'mp', pairs)]
    all_to_all x1 -> x0, waiting for transfers between devices: 8.97 us -> none  [per_device(): lax.all_to_all(piece.reshape(groups, owned, share * PAD), GROUP, 0, 0, ti...]
    all_to_all x1, waiting for transfers between devices: 0.01 us -> 4.35 us  [per_device(): lax.all_to_all(jnp.broadcast_to(mine, (mp_count,) + mine.shape), 'mp', 0,...]
    all_to_all x1, blocking collectives: 12.5 us -> 16.2 us  [per_device(): lax.all_to_all(send, GROUP, 0, 0, tiled=True).reshape(slots, E // cut)]
    all_to_all x1, blocking collectives: 28.7 us -> 25.2 us  [per_device(): lax.all_to_all(part.reshape(mp_count, share * owned, E), 'mp', 0, 0, tile...]
    ppermute x1, waiting for transfers between devices: 8.43 us -> 5.6 us  [per_device(): lax.ppermute(latents, ('segment', 'mp', 'dp'), [(place(g, m), place(twice...]
  transfers between devices with their start and end apart: 27 -> 26, of which waited for: 7 -> 7; matrix products, arithmetic and copies ran while one was open for 10% -> 9% of each run, Pallas kernels for 12% -> 12%
where the time goes in v9:
time: 234 us; the launch traced here: 233 us
  blocking collectives  69.9 us (30%)
  Pallas kernels  43.3 us (19%)
  waiting for transfers between devices  43 us (18%)
  starting transfers between devices  36.3 us (16%)
  between operations  15.7 us (7%)
  matrix products  11.3 us (5%)
  local copies, waits for them, and re-layouts  8.02 us (3%)
  other arithmetic  5.82 us (2%)
    all_to_all x1, blocking collectives, per_device(): lax.all_to_all(part.reshape(mp_count, share * owned, E), 'mp', 0, 0, tile...  25.2 us
    ppermute x14, waiting for transfers between devices, shift(): return lax.ppermute(value, 'mp', pairs)  24.9 us
    ppermute x14, starting transfers between devices, shift(): return lax.ppermute(value, 'mp', pairs)  18.7 us
    all_to_all x1, blocking collectives, per_device(): lax.all_to_all(piece.reshape(groups, owned, share * PAD), GROUP, 0, 0, ti...  17.6 us
    pallas_call x1, Pallas kernels, query_matmul(): pl.pallas_call(query_kernel, grid_spec=pltpu.PrefetchScalarGridSpec(num_s...  17.3 us
    pallas_call x1, Pallas kernels, attention(): pl.pallas_call(attend_kernel, grid_spec=pltpu.PrefetchScalarGridSpec(num_...  16.3 us
    all_to_all x1, blocking collectives, per_device(): lax.all_to_all(send, GROUP, 0, 0, tiled=True).reshape(slots, E // cut)  16.2 us
    all_to_all x1, blocking collectives, per_device(): lax.all_to_all(send.reshape(groups, owned, E // cut), GROUP, 0, 0, tiled=...  10.9 us
  transfers between devices with their start and end apart: 26, of which 7 were waited for; matrix products, arithmetic and copies ran while one was open for 9% of the time, Pallas kernels for 12%

profile of v9, /device:TPU:1, one launch (start us, length us, event | category | flops | bytes accessed | tf_op | source)
XLA Modules:
  0.0 233.4 jit_solution(7456089321340834103)
XLA Ops:
  7.9 1.8 shard_map.149
  9.7 2.1 collective-permute-start.3
  17.2 1.7 collective-permute-start.6
  22.8 2.0 convolution_convert_fusion.10.lat_ref
  29.7 4.6 %collective-permute-done.2 = bf16[4,8,1536]{2,1,0:T(8,128)(2,1)S(1)} collective-permute-done((bf16[4,8,1536]{2,1,0:T(8,128)(2,1)S(1)}, bf16[4,8,1536]{2,1,0:T(8,128)(2,1)S(1)}, u32[]{:S(2)}, u32[]{:S(2)}) %collective-permute-start.2) | collective-permute-done | bytes 98336 | tf_op jit(solution)/shard_map/ppermute | solution.py:40
  35.4 2.7 %collective-permute-start.12 = (bf16[4,32,1536]{2,1,0:T(8,128)(2,1)S(1)}, bf16[4,32,1536]{2,1,0:T(8,128)(2,1)S(1)}, u32[]{:S(2)}, u32[]{:S(2)}) collective-permute-start(bf16[4,32,1536]{2,1,0:T(8,128)(2,1)S(1)} %pad_maximum_fusion.2), channel_id=1, source_target_pairs={{0,12},{4,0},{8,4},{12,8},{16,28},{20,16},{24,20},{28,24},{32,44},... | collective-permute-start | bytes 1179656 | tf_op jit(solution)/shard_map/ppermute | solution.py:40
  42.6 10.5 %collective-permute-done.11 = bf16[4,32,1536]{2,1,0:T(8,128)(2,1)S(1)} collective-permute-done((bf16[4,32,1536]{2,1,0:T(8,128)(2,1)S(1)}, bf16[4,32,1536]{2,1,0:T(8,128)(2,1)S(1)}, u32[]{:S(2)}, u32[]{:S(2)}) %collective-permute-start.11) | collective-permute-done | bytes 393248 | tf_op jit(solution)/shard_map/ppermute | solution.py:40
  53.0 1.7 collective-permute-start.17
  54.9 2.9 %collective-permute-start.14 = (bf16[2,32,1536]{2,1,0:T(8,128)(2,1)S(1)}, bf16[2,32,1536]{2,1,0:T(8,128)(2,1)S(1)}, u32[]{:S(2)}, u32[]{:S(2)}) collective-permute-start(bf16[2,32,1536]{2,1,0:T(8,128)(2,1)S(1)} %slice.51), channel_id=1, source_target_pairs={{0,12},{4,0},{8,4},{12,8},{16,28},{20,16},{24,20},{28,24},{32,44},... | collective-permute-start | bytes 589832 | tf_op jit(solution)/shard_map/ppermute | solution.py:40
  65.0 9.3 %collective-permute-done.9 = bf16[2,32,1536]{2,1,0:T(8,128)(2,1)S(1)} collective-permute-done((bf16[2,32,1536]{2,1,0:T(8,128)(2,1)S(1)}, bf16[2,32,1536]{2,1,0:T(8,128)(2,1)S(1)}, u32[]{:S(2)}, u32[]{:S(2)}) %collective-permute-start.9) | collective-permute-done | bytes 196640 | tf_op jit(solution)/shard_map/ppermute | solution.py:40
  75.2 4.0 %shard_map.150 = bf16[128,512]{1,0:T(8,128)(2,1)} custom-call(bf16[64,128]{1,0:T(8,128)(2,1)} %convolution_convert_fusion.11.q_ref, bf16[64,256]{1,0:T(8,128)(2,1)} %convolution_convert_fusion.10.lat_ref, bf16[4,32,256]{2,1,0:T(8,128)(2,1)} %convolution_convert_fusion.9.rest_0_, bf16[4,32,256]{2,1,0:T(8,128)(2,1)} %convolution_convert_fusion.8.rest_1_, ...), custom_call_target="tpu_custom_call" | custom-call | tf_op jit(solution)/shard_map/pallas_call | solution.py:114
  79.2 17.6 %all_to_all.30 = bf16[16,8,512]{2,1,0:T(8,128)(2,1)S(1)} all-to-all(bf16[16,8,512]{2,1,0:T(8,128)(2,1)} %bitcast.92), channel_id=1, replica_groups=mesh['segment'=4,'mp'=16,'dp'=4] {'segment','dp'}, dimensions={0} | all-to-all | bytes 262144 | tf_op jit(solution)/shard_map/all_to_all | solution.py:382
  99.3 3.5 %all-to-all-start.1 = ((bf16[16,8,512]{2,1,0:T(8,128)(2,1)}), bf16[16,8,512]{2,1,0:T(8,128)(2,1)S(1)}, u32[]{:S(2)}, u32[]{:S(2)}) async-start(bf16[16,8,512]{2,1,0:T(8,128)(2,1)} %fusion.2), calls=%async_computation.1 | async-start | bytes 262144 | tf_op jit(solution)/shard_map/all_to_all | solution.py:394
  104.2 7.4 %all-to-all-done.1 = bf16[16,8,512]{2,1,0:T(8,128)(2,1)S(1)} async-done(((bf16[16,8,512]{2,1,0:T(8,128)(2,1)}), bf16[16,8,512]{2,1,0:T(8,128)(2,1)S(1)}, u32[]{:S(2)}, u32[]{:S(2)}) %all-to-all-start.1) | async-done | bytes 131104 | tf_op jit(solution)/shard_map/all_to_all | solution.py:394
  112.2 4.0 %shard_map.151 = bf16[32,1536]{1,0:T(8,128)(2,1)} custom-call(bf16[128,512]{1,0:T(8,128)(2,1)} %bitcast.90, bf16[1536,1536]{1,0:T(8,128)(2,1)} %weight_ref.1, f32[32,1536]{1,0:T(8,128)} %broadcast_bitcast_fusion.base_ref, bf16[1,1536]{1,0:T(2,128)(2,1)} %slice.47.gain_ref), custom_call_target="tpu_custom_call" | custom-call | tf_op jit(solution)/shard_map/pallas_call | solution.py:140
  116.2 4.3 %collective-permute-start.20 = (bf16[32,1536]{1,0:T(8,128)(2,1)}, bf16[32,1536]{1,0:T(8,128)(2,1)S(1)}, u32[]{:S(2)}, u32[]{:S(2)}) collective-permute-start(bf16[32,1536]{1,0:T(8,128)(2,1)} %shard_map.151), channel_id=1, source_target_pairs={{0,0},{4,5},{8,10},{12,15},{16,80},{20,85},{24,90},{28,95},{32,160... | collective-permute-start | bytes 294920 | tf_op jit(solution)/shard_map/ppermute | solution.py:410
  120.6 5.6 %collective-permute-done.20 = bf16[32,1536]{1,0:T(8,128)(2,1)S(1)} collective-permute-done((bf16[32,1536]{1,0:T(8,128)(2,1)}, bf16[32,1536]{1,0:T(8,128)(2,1)S(1)}, u32[]{:S(2)}, u32[]{:S(2)}) %collective-permute-start.20) | collective-permute-done | bytes 98336 | tf_op jit(solution)/shard_map/ppermute | solution.py:410
  127.5 4.5 %all-to-all-start.2 = ((bf16[16,32,1536]{2,1,0:T(8,128)(2,1)}), bf16[16,32,1536]{2,1,0:T(8,128)(2,1)}, u32[]{:S(2)}, u32[]{:S(2)}) async-start(bf16[16,32,1536]{2,1,0:T(8,128)(2,1)} %broadcast_in_dim.7), calls=%async_computation.2 | async-start | bytes 3145728 | tf_op jit(solution)/shard_map/all_to_all | solution.py:417
  134.3 17.3 %shard_map.152.q_ref = bf16[768,512]{1,0:T(8,128)(2,1)S(1)} custom-call(s32[4]{0:T(128)S(1)} %pad_add_fusion.where, bf16[16,768,512]{2,1,0:T(8,128)(2,1)} %bitcast.86, bf16[1,8192]{1,0:T(2,128)(2,1)S(1)} %copy-done.2, bf16[2048,512]{1,0:T(8,128)(2,1)S(1)} %bitcast.85, bf16[2048,512]{1,0:T(8,128)(2,1)} %collective-permute-done.17.rest_1_, ...), custom_call_target="tpu_custom_call" | custom-call | tf_op jit(solution)/shard_map/pallas_call | solution.py:203
  152.4 4.3 %all-to-all-done.2 = bf16[16,32,1536]{2,1,0:T(8,128)(2,1)} async-done(((bf16[16,32,1536]{2,1,0:T(8,128)(2,1)}), bf16[16,32,1536]{2,1,0:T(8,128)(2,1)}, u32[]{:S(2)}, u32[]{:S(2)}) %all-to-all-start.2) | async-done | bytes 1572896 | tf_op jit(solution)/shard_map/all_to_all | solution.py:417
  156.8 16.3 %shard_map.153 = (bf16[768,512]{1,0:T(8,128)(2,1)}, bf16[512,1536]{1,0:T(8,128)(2,1)}) custom-call(s32[1]{0:T(128)} %bitcast.83.count, s32[16]{0:T(128)} %multiply_xor_fusion.order, s32[4]{0:T(128)} %copy-done.3, f32[1]{0:T(128)S(6)} %tanh.3.gate_ref, bf16[768,512]{1,0:T(8,128)(2,1)} %copy-done.1, bf16[768,512]{1,0:T(8,128)(2,1)} %bitcast.89, ...), custom_call_target="tpu_custom_call" | custom-call | tf_op jit(solution)/shard_map/pallas_call | solution.py:302
  173.1 25.2 %all_to_all.31 = bf16[16,32,1536]{2,1,0:T(8,128)(2,1)S(1)} all-to-all(bf16[16,32,1536]{2,1,0:T(8,128)(2,1)} %bitcast.88), channel_id=1, replica_groups=mesh['segment'=4,'mp'=16,'dp'=4] {'mp'}, dimensions={0} | all-to-all | bytes 3145728 | tf_op jit(solution)/shard_map/all_to_all | solution.py:427
  198.5 16.2 %all_to_all.32 = bf16[16,8,384]{2,1,0:T(8,128)(2,1)S(1)} all-to-all(bf16[16,8,384]{2,1,0:T(8,128)(2,1)S(1)} %bitcast.93), channel_id=1, replica_groups=mesh['segment'=4,'mp'=16,'dp'=4] {'segment','dp'}, dimensions={0} | all-to-all | bytes 196608 | tf_op jit(solution)/shard_map/all_to_all | solution.py:435
  215.0 10.9 %all_to_all.33 = bf16[16,8,384]{2,1,0:T(8,128)(2,1)S(1)} all-to-all(bf16[16,8,384]{2,1,0:T(8,128)(2,1)S(1)} %fusion.3), channel_id=1, replica_groups=mesh['segment'=4,'mp'=16,'dp'=4] {'segment','dp'}, dimensions={0} | all-to-all | bytes 196608 | tf_op jit(solution)/shard_map/all_to_all | solution.py:438
  (113 shorter events, 37.2 us)
Async XLA Ops:
  7.2 127.1 %all-gather.3.cloned.1.call-start = ((), (), s32[]{:S(2)}) async-start(), calls=%async_computation.6 | async-start | bytes 13369344 | tf_op jit(solution)/shard_map/all_gather | solution.py:351
  9.7 15.3 %collective-permute-start.3 = (bf16[4,8,1536]{2,1,0:T(8,128)(2,1)}, bf16[4,8,1536]{2,1,0:T(8,128)(2,1)}, u32[]{:S(2)}, u32[]{:S(2)}) collective-permute-start(bf16[4,8,1536]{2,1,0:T(8,128)(2,1)} %bitcast.119), channel_id=1, source_target_pairs={{0,16},{4,20},{8,24},{12,28},{16,32},{20,36},{24,40},{28,44},{32,4... | collective-permute-start | bytes 294920 | tf_op jit(solution)/shard_map/ppermute | solution.py:40
  11.8 15.3 %collective-permute-start.4 = (bf16[4,8,1536]{2,1,0:T(8,128)(2,1)}, bf16[4,8,1536]{2,1,0:T(8,128)(2,1)}, u32[]{:S(2)}, u32[]{:S(2)}) collective-permute-start(bf16[4,8,1536]{2,1,0:T(8,128)(2,1)} %bitcast.120), channel_id=1, source_target_pairs={{0,48},{4,52},{8,56},{12,60},{16,0},{20,4},{24,8},{28,12},{32,16},... | collective-permute-start | bytes 294920 | tf_op jit(solution)/shard_map/ppermute | solution.py:40
  13.3 15.4 %collective-permute-start.5 = (bf16[4,8,1536]{2,1,0:T(8,128)(2,1)}, bf16[4,8,1536]{2,1,0:T(8,128)(2,1)}, u32[]{:S(2)}, u32[]{:S(2)}) collective-permute-start(bf16[4,8,1536]{2,1,0:T(8,128)(2,1)} %bitcast.121), channel_id=1, source_target_pairs={{0,32},{4,36},{8,40},{12,44},{16,48},{20,52},{24,56},{28,60},{32,0... | collective-permute-start | bytes 294920 | tf_op jit(solution)/shard_map/ppermute | solution.py:40
  14.9 14.8 %collective-permute-start = (bf16[4,8,1536]{2,1,0:T(8,128)(2,1)}, bf16[4,8,1536]{2,1,0:T(8,128)(2,1)}, u32[]{:S(2)}, u32[]{:S(2)}) collective-permute-start(bf16[4,8,1536]{2,1,0:T(8,128)(2,1)} %bitcast.115), channel_id=1, source_target_pairs={{0,4},{4,8},{8,12},{12,0},{16,20},{20,24},{24,28},{28,16},{32,36},... | collective-permute-start | bytes 294920 | tf_op jit(solution)/shard_map/ppermute | solution.py:40
  17.2 18.1 %collective-permute-start.6 = (bf16[512,512]{1,0:T(8,128)(2,1)S(1)}, bf16[512,512]{1,0:T(8,128)(2,1)S(1)}, u32[]{:S(2)}, u32[]{:S(2)}) collective-permute-start(bf16[512,512]{1,0:T(8,128)(2,1)S(1)} %slice_bitcast_fusion.1), channel_id=1, source_target_pairs={{0,2},{1,3},{2,0},{3,1},{4,6},{5,7},{6,4},{7,5},{8,10},{9,11},{10,... | collective-permute-start | bytes 1572872 | tf_op jit(solution)/shard_map/ppermute | solution.py:64
  27.1 7.2 %collective-permute-start.2 = (bf16[4,8,1536]{2,1,0:T(8,128)(2,1)S(1)}, bf16[4,8,1536]{2,1,0:T(8,128)(2,1)S(1)}, u32[]{:S(2)}, u32[]{:S(2)}) collective-permute-start(bf16[4,8,1536]{2,1,0:T(8,128)(2,1)S(1)} %bitcast.117), channel_id=1, source_target_pairs={{0,8},{4,12},{8,0},{12,4},{16,24},{20,28},{24,16},{28,20},{32,40},... | collective-permute-start | bytes 294920 | tf_op jit(solution)/shard_map/ppermute | solution.py:40
  28.7 46.6 %collective-permute-start.15 = (bf16[1536,512]{1,0:T(8,128)(2,1)S(1)}, bf16[1536,512]{1,0:T(8,128)(2,1)}, u32[]{:S(2)}, u32[]{:S(2)}) collective-permute-start(bf16[1536,512]{1,0:T(8,128)(2,1)S(1)} %slice_bitcast_fusion), channel_id=1, source_target_pairs={{0,2},{1,3},{2,0},{3,1},{4,6},{5,7},{6,4},{7,5},{8,10},{9,11},{10,... | collective-permute-start | bytes 4718600 | tf_op jit(solution)/shard_map/ppermute | solution.py:64
  35.3 17.7 %collective-permute-start.11 = (bf16[4,32,1536]{2,1,0:T(8,128)(2,1)S(1)}, bf16[4,32,1536]{2,1,0:T(8,128)(2,1)S(1)}, u32[]{:S(2)}, u32[]{:S(2)}) collective-permute-start(bf16[4,32,1536]{2,1,0:T(8,128)(2,1)S(1)} %pad_maximum_fusion.2), channel_id=1, source_target_pairs={{0,4},{4,8},{8,12},{12,0},{16,20},{20,24},{24,28},{28,16},{32,36},... | collective-permute-start | bytes 1179656 | tf_op jit(solution)/shard_map/ppermute | solution.py:40
  35.4 19.3 %collective-permute-start.12 = (bf16[4,32,1536]{2,1,0:T(8,128)(2,1)S(1)}, bf16[4,32,1536]{2,1,0:T(8,128)(2,1)S(1)}, u32[]{:S(2)}, u32[]{:S(2)}) collective-permute-start(bf16[4,32,1536]{2,1,0:T(8,128)(2,1)S(1)} %pad_maximum_fusion.2), channel_id=1, source_target_pairs={{0,12},{4,0},{8,4},{12,8},{16,28},{20,16},{24,20},{28,24},{32,44},... | collective-permute-start | bytes 1179656 | tf_op jit(solution)/shard_map/ppermute | solution.py:40
  38.1 16.8 %collective-permute-start.8 = (bf16[4,32,1536]{2,1,0:T(8,128)(2,1)S(1)}, bf16[4,32,1536]{2,1,0:T(8,128)(2,1)S(1)}, u32[]{:S(2)}, u32[]{:S(2)}) collective-permute-start(bf16[4,32,1536]{2,1,0:T(8,128)(2,1)S(1)} %pad_maximum_fusion.1), channel_id=1, source_target_pairs={{0,48},{4,52},{8,56},{12,60},{16,0},{20,4},{24,8},{28,12},{32,16},... | collective-permute-start | bytes 1179656 | tf_op jit(solution)/shard_map/ppermute | solution.py:40
  38.1 19.7 %collective-permute-start.7 = (bf16[4,32,1536]{2,1,0:T(8,128)(2,1)S(1)}, bf16[4,32,1536]{2,1,0:T(8,128)(2,1)S(1)}, u32[]{:S(2)}, u32[]{:S(2)}) collective-permute-start(bf16[4,32,1536]{2,1,0:T(8,128)(2,1)S(1)} %pad_maximum_fusion.1), channel_id=1, source_target_pairs={{0,16},{4,20},{8,24},{12,28},{16,32},{20,36},{24,40},{28,44},{32,4... | collective-permute-start | bytes 1179656 | tf_op jit(solution)/shard_map/ppermute | solution.py:40
  53.0 63.2 %collective-permute-start.17 = (bf16[2048,512]{1,0:T(8,128)(2,1)S(1)}, bf16[2048,512]{1,0:T(8,128)(2,1)}, u32[]{:S(2)}, u32[]{:S(2)}) collective-permute-start(bf16[2048,512]{1,0:T(8,128)(2,1)S(1)} %bitcast.84), channel_id=1, source_target_pairs={{0,1},{1,0},{2,3},{3,2},{4,5},{5,4},{6,7},{7,6},{8,9},{9,8},{10,11... | collective-permute-start | bytes 6291464 | tf_op jit(solution)/shard_map/ppermute | solution.py:68
  54.7 7.8 %collective-permute-start.13 = (bf16[2,32,1536]{2,1,0:T(8,128)(2,1)S(1)}, bf16[2,32,1536]{2,1,0:T(8,128)(2,1)S(1)}, u32[]{:S(2)}, u32[]{:S(2)}) collective-permute-start(bf16[2,32,1536]{2,1,0:T(8,128)(2,1)S(1)} %slice.50), channel_id=1, source_target_pairs={{0,4},{4,8},{8,12},{12,0},{16,20},{20,24},{24,28},{28,16},{32,36},... | collective-permute-start | bytes 589832 | tf_op jit(solution)/shard_map/ppermute | solution.py:40
  54.9 9.2 %collective-permute-start.14 = (bf16[2,32,1536]{2,1,0:T(8,128)(2,1)S(1)}, bf16[2,32,1536]{2,1,0:T(8,128)(2,1)S(1)}, u32[]{:S(2)}, u32[]{:S(2)}) collective-permute-start(bf16[2,32,1536]{2,1,0:T(8,128)(2,1)S(1)} %slice.51), channel_id=1, source_target_pairs={{0,12},{4,0},{8,4},{12,8},{16,28},{20,16},{24,20},{28,24},{32,44},... | collective-permute-start | bytes 589832 | tf_op jit(solution)/shard_map/ppermute | solution.py:40
  62.6 11.7 %collective-permute-start.9 = (bf16[2,32,1536]{2,1,0:T(8,128)(2,1)S(1)}, bf16[2,32,1536]{2,1,0:T(8,128)(2,1)S(1)}, u32[]{:S(2)}, u32[]{:S(2)}) collective-permute-start(bf16[2,32,1536]{2,1,0:T(8,128)(2,1)S(1)} %slice.48), channel_id=1, source_target_pairs={{0,16},{4,20},{8,24},{12,28},{16,32},{20,36},{24,40},{28,44},{32,4... | collective-permute-start | bytes 589832 | tf_op jit(solution)/shard_map/ppermute | solution.py:40
  96.8 19.4 %collective-permute-start.19 = (bf16[1536,512]{1,0:T(8,128)(2,1)}, bf16[1536,512]{1,0:T(8,128)(2,1)}, u32[]{:S(2)}, u32[]{:S(2)}) collective-permute-start(bf16[1536,512]{1,0:T(8,128)(2,1)} %collective-permute-done.15.rest_3_), channel_id=1, source_target_pairs={{0,1},{1,0},{2,3},{3,2},{4,5},{5,4},{6,7},{7,6},{8,9},{9,8},{10,11... | collective-permute-start | bytes 4718600 | tf_op jit(solution)/shard_map/ppermute | solution.py:68
  96.8 19.4 %collective-permute-start.16 = (bf16[384,1024]{1,0:T(8,128)(2,1)}, bf16[384,1024]{1,0:T(8,128)(2,1)}, u32[]{:S(2)}, u32[]{:S(2)}) collective-permute-start(bf16[384,1024]{1,0:T(8,128)(2,1)} %pad_maximum_fusion.kv0), channel_id=1, source_target_pairs={{0,2},{1,3},{2,0},{3,1},{4,6},{5,7},{6,4},{7,5},{8,10},{9,11},{10,... | collective-permute-start | bytes 2359304 | tf_op jit(solution)/shard_map/ppermute | solution.py:64
  97.7 18.5 %collective-permute-start.18 = (bf16[512,512]{1,0:T(8,128)(2,1)S(1)}, bf16[512,512]{1,0:T(8,128)(2,1)S(1)}, u32[]{:S(2)}, u32[]{:S(2)}) collective-permute-start(bf16[512,512]{1,0:T(8,128)(2,1)S(1)} %collective-permute-done.6.rest_2_), channel_id=1, source_target_pairs={{0,1},{1,0},{2,3},{3,2},{4,5},{5,4},{6,7},{7,6},{8,9},{9,8},{10,11... | collective-permute-start | bytes 1572872 | tf_op jit(solution)/shard_map/ppermute | solution.py:68
  99.3 12.2 %all-to-all-start.1 = ((bf16[16,8,512]{2,1,0:T(8,128)(2,1)}), bf16[16,8,512]{2,1,0:T(8,128)(2,1)S(1)}, u32[]{:S(2)}, u32[]{:S(2)}) async-start(bf16[16,8,512]{2,1,0:T(8,128)(2,1)} %fusion.2), calls=%async_computation.1 | async-start | bytes 262144 | tf_op jit(solution)/shard_map/all_to_all | solution.py:394
  116.2 9.9 %collective-permute-start.20 = (bf16[32,1536]{1,0:T(8,128)(2,1)}, bf16[32,1536]{1,0:T(8,128)(2,1)S(1)}, u32[]{:S(2)}, u32[]{:S(2)}) collective-permute-start(bf16[32,1536]{1,0:T(8,128)(2,1)} %shard_map.151), channel_id=1, source_target_pairs={{0,0},{4,5},{8,10},{12,15},{16,80},{20,85},{24,90},{28,95},{32,160... | collective-permute-start | bytes 294920 | tf_op jit(solution)/shard_map/ppermute | solution.py:410
  127.5 29.3 %all-to-all-start.2 = ((bf16[16,32,1536]{2,1,0:T(8,128)(2,1)}), bf16[16,32,1536]{2,1,0:T(8,128)(2,1)}, u32[]{:S(2)}, u32[]{:S(2)}) async-start(bf16[16,32,1536]{2,1,0:T(8,128)(2,1)} %broadcast_in_dim.7), calls=%async_computation.2 | async-start | bytes 3145728 | tf_op jit(solution)/shard_map/all_to_all | solution.py:417
  132.0 24.7 %collective-permute-start.21 = (bf16[384,1024]{1,0:T(8,128)(2,1)}, bf16[384,1024]{1,0:T(8,128)(2,1)}, u32[]{:S(2)}, u32[]{:S(2)}) collective-permute-start(bf16[384,1024]{1,0:T(8,128)(2,1)} %pad_maximum_fusion.kv0), channel_id=1, source_target_pairs={{0,1},{1,0},{2,3},{3,2},{4,5},{5,4},{6,7},{7,6},{8,9},{9,8},{10,11... | collective-permute-start | bytes 2359304 | tf_op jit(solution)/shard_map/ppermute | solution.py:68
  132.6 24.2 %collective-permute-start.22 = (bf16[384,1024]{1,0:T(8,128)(2,1)}, bf16[384,1024]{1,0:T(8,128)(2,1)}, u32[]{:S(2)}, u32[]{:S(2)}) collective-permute-start(bf16[384,1024]{1,0:T(8,128)(2,1)} %collective-permute-done.16.kv2), channel_id=1, source_target_pairs={{0,1},{1,0},{2,3},{3,2},{4,5},{5,4},{6,7},{7,6},{8,9},{9,8},{10,11... | collective-permute-start | bytes 2359304 | tf_op jit(solution)/shard_map/ppermute | solution.py:68
  (16 other events, 209.5 us)
Sparse Core Ops, SparseCore 0:
  10.4 112.5 all-gather.2
